TPU v7x, 256 devices: a whole 4x4x8 slice. The times are simulated.
256 devices in a mesh: blk: 16 (over y, z_lo, core), rep: 16 (over x, z_hi).
Axes of the slice: x: 4, y: 4, z: 8 (z_hi: 4, z_lo: 2; z = z_hi * 2 + z_lo), core: 2. Of those that a mesh axis runs over, the one named last changes fastest.
Arguments:
- root_rows: float32 [256, 16384], P(None, 'blk'), may hold values from -520 to 520
- gradient: bfloat16 [2048, 16384], P('rep', 'blk'), may hold values from -6 to 6
Outputs:
- eigen_values: float32 [16384], P('blk')
- projected_energy: float32 [2048, 16384], P('rep', 'blk')
All inputs are finite; a program needn't handle non-finite values.
Results may differ from a plain program's by a relative error of at most 0.0003.
Values sent between devices are 32-bit elements; how exact they have to be, the bound alone decides.
No kernel may reach another device: no remote copies, remote signals or barrier semaphores. Data moves between devices by JAX's collectives and lax.ppermute only.
A program may use at most 64 MiB of HBM per device.

v0:
```python
import jax
import jax.numpy as jnp
from jax import lax
from jax.sharding import PartitionSpec as P

ROOT_ROWS = 256
SWEEPS = 4


def shifted(shard, axis, by):
    length = lax.axis_size(axis)
    return lax.ppermute(shard, axis, [(i, (i + by) % length) for i in range(length)])


def rotate_pair(top_part, bottom_part, cosine, sine_part):
    return (
        cosine * top_part + sine_part * bottom_part,
        cosine * bottom_part - sine_part * top_part,
    )


def pair_angles(top_root, bottom_root):
    pair_totals = (
        jnp.sum(top_root * top_root, axis=0),
        jnp.sum(bottom_root * bottom_root, axis=0),
        jnp.sum(top_root * bottom_root, axis=0),
    )
    angle_half = 0.5 * jnp.arctan2(2.0 * pair_totals[2], pair_totals[0] - pair_totals[1])
    return (jnp.cos(angle_half), jnp.sin(angle_half))


def turn_gradient(top_grad, bottom_grad, turn_list):
    for cosine, sine_part in turn_list:
        top_grad, bottom_grad = rotate_pair(top_grad, bottom_grad, cosine, sine_part)
        bottom_grad = jnp.roll(bottom_grad, -1, axis=1)
    return (top_grad, bottom_grad)


def body(root_rows, gradient):
    blocks = lax.axis_size("blk")
    rounds = max(2, blocks // 4)
    block_width = root_rows.shape[1] // 2
    top_root = root_rows[:, :block_width]
    bottom_root = root_rows[:, block_width:]
    grad_full = gradient.astype(jnp.float32)
    top_grad = grad_full[:, :block_width]
    bottom_grad = grad_full[:, block_width:]
    for round_index in range(rounds):
        turn_list = []
        for sweep_index in range(SWEEPS):
            cosine, sine_part = pair_angles(top_root, bottom_root)
            top_root, bottom_root = rotate_pair(top_root, bottom_root, cosine, sine_part)
            bottom_root = jnp.roll(bottom_root, -1, axis=1)
            turn_list.append((cosine, sine_part))
        moving = round_index + 1 < rounds
        top_grad, bottom_grad = turn_gradient(top_grad, bottom_grad, turn_list)
        if moving:
            top_root, top_grad = shifted((top_root, top_grad), "blk", 1)
            bottom_root, bottom_grad = shifted((bottom_root, bottom_grad), "blk", -1)
    total_moves = rounds * SWEEPS
    column_sums = jnp.concatenate(
        [
            jnp.sum(top_root * top_root, axis=0),
            jnp.roll(jnp.sum(bottom_root * bottom_root, axis=0), total_moves),
        ]
    )
    eigen_values = column_sums * (1.0 / ROOT_ROWS)
    bottom_grad = jnp.roll(bottom_grad, total_moves, axis=1)
    projected = jnp.concatenate([top_grad * top_grad, bottom_grad * bottom_grad], axis=1)
    return (eigen_values, projected)


def solution(mesh):
    return jax.shard_map(
        body,
        mesh=mesh,
        in_specs=(P(None, "blk"), P("rep", "blk")),
        out_specs=(P("blk"), P("rep", "blk")),
        check_vma=False,
    )
```

profile of v0, /device:TPU:1, one launch (start us, length us, event | category | flops | bytes accessed | tf_op | source)
XLA Modules:
  0.0 70.1 jit_solution(12149871730186350865)
XLA Ops:
  0.6 1.4 %multiply_reduce_fusion.48 = (f32[512]{0:T(512)S(1)}, f32[512]{0:T(512)S(1)}, f32[512]{0:T(512)S(1)}) fusion(f32[256,1024]{1,0:T(8,128)} %param.2), kind=kLoop, calls=%fused_computation.97 | loop fusion | flops 784896 | bytes 1054720 | tf_op jit(solution)/shard_map/reduce_sum | solution.py:26
  2.3 0.2 slice.298
  2.5 0.2 multiply_reduce_fusion.45
  3.0 0.2 slice.300
  3.2 0.3 multiply_reduce_fusion.42
  3.7 0.2 slice.302
  3.9 0.3 multiply_reduce_fusion.39
  4.5 3.1 %collective-permute-start = (f32[256,512]{1,0:T(8,128)S(1)}, f32[256,512]{1,0:T(8,128)S(1)}, u32[]{:S(2)}, u32[]{:S(2)}) collective-permute-start(f32[256,512]{1,0:T(8,128)S(1)} %get-tuple-element.77), channel_id=1, source_target_pairs={{0,16},{16,32},{32,48},{48,64},{64,80},{80,96},{96,112},{112,128},... | collective-permute-start | bytes 1572872 | tf_op jit(solution)/shard_map/ppermute | solution.py:12
  7.6 0.2 slice.304
  7.9 0.3 collective-permute-start.1
  8.2 0.5 copy-done.1
  9.7 1.1 %collective-permute-start.6 = (f32[128,512]{1,0:T(8,128)S(1)}, f32[128,512]{1,0:T(8,128)S(1)}, u32[]{:S(2)}, u32[]{:S(2)}) collective-permute-start(f32[128,512]{1,0:T(8,128)S(1)} %get-tuple-element.85), channel_id=1, source_target_pairs={{0,16},{16,32},{32,48},{48,64},{64,80},{80,96},{96,112},{112,128},... | collective-permute-start | bytes 786440 | tf_op jit(solution)/shard_map/ppermute | solution.py:12
  11.0 2.4 %collective-permute-start.7 = (f32[128,512]{1,0:T(8,128)S(1)}, f32[128,512]{1,0:T(8,128)S(1)}, u32[]{:S(2)}, u32[]{:S(2)}) collective-permute-start(f32[128,512]{1,0:T(8,128)S(1)} %pad_maximum_fusion.20), channel_id=1, source_target_pairs={{0,240},{16,0},{32,16},{48,32},{64,48},{80,64},{96,80},{112,96},{1... | collective-permute-start | bytes 786440 | tf_op jit(solution)/shard_map/ppermute | solution.py:12
  13.5 1.1 %collective-permute-done = f32[256,512]{1,0:T(8,128)S(1)} collective-permute-done((f32[256,512]{1,0:T(8,128)S(1)}, f32[256,512]{1,0:T(8,128)S(1)}, u32[]{:S(2)}, u32[]{:S(2)}) %collective-permute-start) | collective-permute-done | bytes 524320 | tf_op jit(solution)/shard_map/ppermute | solution.py:12
  14.6 8.0 %collective-permute-done.1 = f32[256,512]{1,0:T(8,128)S(1)} collective-permute-done((f32[256,512]{1,0:T(8,128)S(1)}, f32[256,512]{1,0:T(8,128)S(1)}, u32[]{:S(2)}, u32[]{:S(2)}) %collective-permute-start.1) | collective-permute-done | bytes 524320 | tf_op jit(solution)/shard_map/ppermute | solution.py:12
  22.9 0.2 slice.306
  23.1 0.2 multiply_reduce_fusion.33
  23.6 0.2 slice.308
  23.8 0.3 multiply_reduce_fusion.30
  24.4 0.2 slice.310
  24.6 0.3 multiply_reduce_fusion.27
  25.1 0.2 slice.312
  25.3 1.2 %collective-permute-done.7 = f32[128,512]{1,0:T(8,128)S(1)} collective-permute-done((f32[128,512]{1,0:T(8,128)S(1)}, f32[128,512]{1,0:T(8,128)S(1)}, u32[]{:S(2)}, u32[]{:S(2)}) %collective-permute-start.7) | collective-permute-done | bytes 262176 | tf_op jit(solution)/shard_map/ppermute | solution.py:12
  27.2 2.0 %collective-permute-start.3 = (f32[256,512]{1,0:T(8,128)S(1)}, f32[256,512]{1,0:T(8,128)S(1)}, u32[]{:S(2)}, u32[]{:S(2)}) collective-permute-start(f32[256,512]{1,0:T(8,128)S(1)} %pad_maximum_fusion.7), channel_id=1, source_target_pairs={{0,240},{16,0},{32,16},{48,32},{64,48},{80,64},{96,80},{112,96},{1... | collective-permute-start | bytes 1572872 | tf_op jit(solution)/shard_map/ppermute | solution.py:12
  30.0 4.1 %collective-permute-start.9 = (f32[128,512]{1,0:T(8,128)S(1)}, f32[128,512]{1,0:T(8,128)S(1)}, u32[]{:S(2)}, u32[]{:S(2)}) collective-permute-start(f32[128,512]{1,0:T(8,128)S(1)} %pad_maximum_fusion.24), channel_id=1, source_target_pairs={{0,240},{16,0},{32,16},{48,32},{64,48},{80,64},{96,80},{112,96},{1... | collective-permute-start | bytes 786440 | tf_op jit(solution)/shard_map/ppermute | solution.py:12
  34.1 7.7 %collective-permute-done.3 = f32[256,512]{1,0:T(8,128)S(1)} collective-permute-done((f32[256,512]{1,0:T(8,128)S(1)}, f32[256,512]{1,0:T(8,128)S(1)}, u32[]{:S(2)}, u32[]{:S(2)}) %collective-permute-start.3) | collective-permute-done | bytes 524320 | tf_op jit(solution)/shard_map/ppermute | solution.py:12
  42.1 0.2 slice.314
  42.3 0.2 multiply_reduce_fusion.21
  42.8 0.2 slice.316
  43.0 0.3 multiply_reduce_fusion.18
  43.6 0.2 slice.318
  43.8 0.3 multiply_reduce_fusion.15
  44.3 0.2 slice.320
  44.5 2.0 %collective-permute-done.9 = f32[128,512]{1,0:T(8,128)S(1)} collective-permute-done((f32[128,512]{1,0:T(8,128)S(1)}, f32[128,512]{1,0:T(8,128)S(1)}, u32[]{:S(2)}, u32[]{:S(2)}) %collective-permute-start.9) | collective-permute-done | bytes 262176 | tf_op jit(solution)/shard_map/ppermute | solution.py:12
  47.2 3.9 %collective-permute-start.5 = (f32[256,512]{1,0:T(8,128)S(1)}, f32[256,512]{1,0:T(8,128)S(1)}, u32[]{:S(2)}, u32[]{:S(2)}) collective-permute-start(f32[256,512]{1,0:T(8,128)S(1)} %pad_maximum_fusion.11), channel_id=1, source_target_pairs={{0,240},{16,0},{32,16},{48,32},{64,48},{80,64},{96,80},{112,96},{1... | collective-permute-start | bytes 1572872 | tf_op jit(solution)/shard_map/ppermute | solution.py:12
  51.9 3.9 %collective-permute-start.11 = (f32[128,512]{1,0:T(8,128)S(1)}, f32[128,512]{1,0:T(8,128)S(1)}, u32[]{:S(2)}, u32[]{:S(2)}) collective-permute-start(f32[128,512]{1,0:T(8,128)S(1)} %pad_maximum_fusion.28), channel_id=1, source_target_pairs={{0,240},{16,0},{32,16},{48,32},{64,48},{80,64},{96,80},{112,96},{1... | collective-permute-start | bytes 786440 | tf_op jit(solution)/shard_map/ppermute | solution.py:12
  55.8 5.9 %collective-permute-done.5 = f32[256,512]{1,0:T(8,128)S(1)} collective-permute-done((f32[256,512]{1,0:T(8,128)S(1)}, f32[256,512]{1,0:T(8,128)S(1)}, u32[]{:S(2)}, u32[]{:S(2)}) %collective-permute-start.5) | collective-permute-done | bytes 524320 | tf_op jit(solution)/shard_map/ppermute | solution.py:12
  62.1 0.2 slice.322
  62.3 0.2 multiply_reduce_fusion.9
  62.8 0.2 slice.324
  63.0 0.3 multiply_reduce_fusion.6
  63.5 0.2 slice.326
  63.7 0.3 multiply_reduce_fusion.3
  64.0 0.2 multiply_reduce_fusion
  64.3 0.2 slice.328
  64.5 2.5 %collective-permute-done.11 = f32[128,512]{1,0:T(8,128)S(1)} collective-permute-done((f32[128,512]{1,0:T(8,128)S(1)}, f32[128,512]{1,0:T(8,128)S(1)}, u32[]{:S(2)}, u32[]{:S(2)}) %collective-permute-start.11) | collective-permute-done | bytes 262176 | tf_op jit(solution)/shard_map/ppermute | solution.py:12
  68.6 0.8 %pad_maximum_fusion.15 = f32[128,1024]{1,0:T(8,128)} fusion(f32[128,512]{1,0:T(8,128)S(1)} %fusion.2, f32[128,512]{1,0:T(8,128)S(1)} %get-tuple-element.78), kind=kLoop, calls=%fused_computation.17 | loop fusion | flops 131072 | bytes 1048576 | tf_op jit(solution)/shard_map/concatenate | solution.py:69
  69.4 0.7 maximum_multiply_fusion.1
  (121 shorter events, 9.7 us)
Async XLA Ops:
  0.6 1.5 %copy-start = (f32[256,1024]{1,0:T(8,128)S(1)}, f32[256,1024]{1,0:T(8,128)}, u32[]{:S(2)}) copy-start(f32[256,1024]{1,0:T(8,128)} %param.2) | copy-start | bytes 3145732
  4.5 10.1 %collective-permute-start = (f32[256,512]{1,0:T(8,128)S(1)}, f32[256,512]{1,0:T(8,128)S(1)}, u32[]{:S(2)}, u32[]{:S(2)}) collective-permute-start(f32[256,512]{1,0:T(8,128)S(1)} %get-tuple-element.77), channel_id=1, source_target_pairs={{0,16},{16,32},{32,48},{48,64},{64,80},{80,96},{96,112},{112,128},... | collective-permute-start | bytes 1572872 | tf_op jit(solution)/shard_map/ppermute | solution.py:12
  7.8 1.0 %copy-start.1 = (bf16[128,1024]{1,0:T(8,128)(2,1)S(1)}, bf16[128,1024]{1,0:T(8,128)(2,1)}, u32[]{:S(2)}) copy-start(bf16[128,1024]{1,0:T(8,128)(2,1)} %param.3) | copy-start | bytes 786436
  7.9 14.7 %collective-permute-start.1 = (f32[256,512]{1,0:T(8,128)S(1)}, f32[256,512]{1,0:T(8,128)S(1)}, u32[]{:S(2)}, u32[]{:S(2)}) collective-permute-start(f32[256,512]{1,0:T(8,128)S(1)} %pad_maximum_fusion.3), channel_id=1, source_target_pairs={{0,240},{16,0},{32,16},{48,32},{64,48},{80,64},{96,80},{112,96},{1... | collective-permute-start | bytes 1572872 | tf_op jit(solution)/shard_map/ppermute | solution.py:12
  9.7 15.6 %collective-permute-start.6 = (f32[128,512]{1,0:T(8,128)S(1)}, f32[128,512]{1,0:T(8,128)S(1)}, u32[]{:S(2)}, u32[]{:S(2)}) collective-permute-start(f32[128,512]{1,0:T(8,128)S(1)} %get-tuple-element.85), channel_id=1, source_target_pairs={{0,16},{16,32},{32,48},{48,64},{64,80},{80,96},{96,112},{112,128},... | collective-permute-start | bytes 786440 | tf_op jit(solution)/shard_map/ppermute | solution.py:12
  11.0 15.5 %collective-permute-start.7 = (f32[128,512]{1,0:T(8,128)S(1)}, f32[128,512]{1,0:T(8,128)S(1)}, u32[]{:S(2)}, u32[]{:S(2)}) collective-permute-start(f32[128,512]{1,0:T(8,128)S(1)} %pad_maximum_fusion.20), channel_id=1, source_target_pairs={{0,240},{16,0},{32,16},{48,32},{64,48},{80,64},{96,80},{112,96},{1... | collective-permute-start | bytes 786440 | tf_op jit(solution)/shard_map/ppermute | solution.py:12
  27.0 7.1 %collective-permute-start.2 = (f32[256,512]{1,0:T(8,128)S(1)}, f32[256,512]{1,0:T(8,128)S(1)}, u32[]{:S(2)}, u32[]{:S(2)}) collective-permute-start(f32[256,512]{1,0:T(8,128)S(1)} %get-tuple-element.75), channel_id=1, source_target_pairs={{0,16},{16,32},{32,48},{48,64},{64,80},{80,96},{96,112},{112,128},... | collective-permute-start | bytes 1572872 | tf_op jit(solution)/shard_map/ppermute | solution.py:12
  27.2 14.6 %collective-permute-start.3 = (f32[256,512]{1,0:T(8,128)S(1)}, f32[256,512]{1,0:T(8,128)S(1)}, u32[]{:S(2)}, u32[]{:S(2)}) collective-permute-start(f32[256,512]{1,0:T(8,128)S(1)} %pad_maximum_fusion.7), channel_id=1, source_target_pairs={{0,240},{16,0},{32,16},{48,32},{64,48},{80,64},{96,80},{112,96},{1... | collective-permute-start | bytes 1572872 | tf_op jit(solution)/shard_map/ppermute | solution.py:12
  29.8 14.7 %collective-permute-start.8 = (f32[128,512]{1,0:T(8,128)S(1)}, f32[128,512]{1,0:T(8,128)S(1)}, u32[]{:S(2)}, u32[]{:S(2)}) collective-permute-start(f32[128,512]{1,0:T(8,128)S(1)} %get-tuple-element.83), channel_id=1, source_target_pairs={{0,16},{16,32},{32,48},{48,64},{64,80},{80,96},{96,112},{112,128},... | collective-permute-start | bytes 786440 | tf_op jit(solution)/shard_map/ppermute | solution.py:12
  30.0 16.5 %collective-permute-start.9 = (f32[128,512]{1,0:T(8,128)S(1)}, f32[128,512]{1,0:T(8,128)S(1)}, u32[]{:S(2)}, u32[]{:S(2)}) collective-permute-start(f32[128,512]{1,0:T(8,128)S(1)} %pad_maximum_fusion.24), channel_id=1, source_target_pairs={{0,240},{16,0},{32,16},{48,32},{64,48},{80,64},{96,80},{112,96},{1... | collective-permute-start | bytes 786440 | tf_op jit(solution)/shard_map/ppermute | solution.py:12
  47.0 8.8 %collective-permute-start.4 = (f32[256,512]{1,0:T(8,128)S(1)}, f32[256,512]{1,0:T(8,128)S(1)}, u32[]{:S(2)}, u32[]{:S(2)}) collective-permute-start(f32[256,512]{1,0:T(8,128)S(1)} %get-tuple-element.73), channel_id=1, source_target_pairs={{0,16},{16,32},{32,48},{48,64},{64,80},{80,96},{96,112},{112,128},... | collective-permute-start | bytes 1572872 | tf_op jit(solution)/shard_map/ppermute | solution.py:12
  47.2 14.5 %collective-permute-start.5 = (f32[256,512]{1,0:T(8,128)S(1)}, f32[256,512]{1,0:T(8,128)S(1)}, u32[]{:S(2)}, u32[]{:S(2)}) collective-permute-start(f32[256,512]{1,0:T(8,128)S(1)} %pad_maximum_fusion.11), channel_id=1, source_target_pairs={{0,240},{16,0},{32,16},{48,32},{64,48},{80,64},{96,80},{112,96},{1... | collective-permute-start | bytes 1572872 | tf_op jit(solution)/shard_map/ppermute | solution.py:12
  51.7 12.8 %collective-permute-start.10 = (f32[128,512]{1,0:T(8,128)S(1)}, f32[128,512]{1,0:T(8,128)S(1)}, u32[]{:S(2)}, u32[]{:S(2)}) collective-permute-start(f32[128,512]{1,0:T(8,128)S(1)} %get-tuple-element.81), channel_id=1, source_target_pairs={{0,16},{16,32},{32,48},{48,64},{64,80},{80,96},{96,112},{112,128},... | collective-permute-start | bytes 786440 | tf_op jit(solution)/shard_map/ppermute | solution.py:12
  51.9 15.1 %collective-permute-start.11 = (f32[128,512]{1,0:T(8,128)S(1)}, f32[128,512]{1,0:T(8,128)S(1)}, u32[]{:S(2)}, u32[]{:S(2)}) collective-permute-start(f32[128,512]{1,0:T(8,128)S(1)} %pad_maximum_fusion.28), channel_id=1, source_target_pairs={{0,240},{16,0},{32,16},{48,32},{64,48},{80,64},{96,80},{112,96},{1... | collective-permute-start | bytes 786440 | tf_op jit(solution)/shard_map/ppermute | solution.py:12
where the time goes:
time: 71 us; the launch traced here: 70.1 us
  waiting for transfers between devices  28.3 us (40%)
  starting transfers between devices  21.2 us (30%)
  other arithmetic  12.7 us (18%)
  local copies, waits for them, and re-layouts  6.41 us (9%)
  between operations  1.48 us (2%)
    ppermute x12, waiting for transfers between devices, shifted(): lax.ppermute(shard, axis, [(i, (i + by) % length) for i in range(length)])  28.3 us
    ppermute x12, starting transfers between devices, shifted(): lax.ppermute(shard, axis, [(i, (i + by) % length) for i in range(length)])  21.2 us
    reduce_sum x16, other arithmetic, pair_angles(): jnp.sum(top_root * bottom_root, axis=0)  4.79 us
    sub x30, other arithmetic, rotate_pair(): cosine * bottom_part - sine_part * top_part  3.88 us
    slice x32, local copies, waits for them, and re-layouts, body(): bottom_root = jnp.roll(bottom_root, -1, axis=1)  3.44 us
    slice x32, local copies, waits for them, and re-layouts, turn_gradient(): bottom_grad = jnp.roll(bottom_grad, -1, axis=1)  2.2 us
  transfers between devices with their start and end apart: 12, of which 7 were waited for; matrix products, arithmetic and copies ran while one was open for 16% of the time, Pallas kernels for 0%

commit v1 on v0

v1 whole, which is shorter than its diff:
```python
import functools
import jax
import jax.numpy as jnp
from jax import lax
from jax.experimental import pallas as pl
from jax.experimental.pallas import tpu as pltpu
from jax.sharding import PartitionSpec as P

ROOT_ROWS = 256
SWEEPS = 4
WIDTH = 512
LANES = 128
HALO = 16
GROUPS = LANES // HALO
HALO_ROWS = ROOT_ROWS // GROUPS
CHUNK_ROWS = ROOT_ROWS + HALO_ROWS
PARTS = WIDTH // LANES
ROUND_PAIRS = (((0, 0), (1, 1), (2, 2)), ((0, 1), (1, 2)), ((0, 2),))
STEPS = SWEEPS * sum(len(pairs) for pairs in ROUND_PAIRS)
EIGEN_ROW = 2 * STEPS
ANGLE_ROWS = 2 * STEPS + 8
MEGA = 1 << 20


def turn_of(tt, bb, tb):
    y = 2.0 * tb
    x = tt - bb
    ax = jnp.abs(x)
    ay = jnp.abs(y)
    top = jnp.maximum(ax, ay)
    none = top == 0.0
    scale = 1.0 / jnp.where(none, 1.0, top)
    xs = jnp.where(none, 1.0, ax * scale)
    ys = jnp.where(none, 0.0, ay * scale)
    inv = lax.rsqrt(xs * xs + ys * ys)
    big = jnp.sqrt(0.5 + 0.5 * (xs * inv))
    small = 0.5 * (ys * inv) / big
    forward = x >= 0.0
    cosine = jnp.where(forward, big, small)
    size = jnp.where(forward, small, big)
    return cosine, jnp.where(y < 0.0, -size, size)


def total8(acc):
    return jnp.sum(acc, axis=0, keepdims=True)


def first_kernel(root_ref, top_out, both_out, bottom_out, turn_out, top, bottom):
    tile = 8
    count = ROOT_ROWS // tile
    zero = jnp.zeros((tile, WIDTH), jnp.float32)

    def measure(i, acc):
        rows = pl.ds(pl.multiple_of(i * tile, tile), tile)
        t = root_ref[rows, pl.ds(0, WIDTH)]
        b = root_ref[rows, pl.ds(WIDTH, WIDTH)]
        top[rows, :] = t
        bottom[rows, :] = b
        return acc[0] + t * t, acc[1] + b * b, acc[2] + t * b

    sums = lax.fori_loop(0, count, measure, (zero, zero, zero), unroll=4)
    for step in range(SWEEPS):
        cosine, sine = turn_of(*(total8(a) for a in sums))
        turn_out[pl.ds(step, 1), :] = cosine
        turn_out[pl.ds(SWEEPS + step, 1), :] = sine
        cb = jnp.broadcast_to(cosine, (tile, WIDTH))
        sb = jnp.broadcast_to(sine, (tile, WIDTH))

        def rotate(i, acc, cb=cb, sb=sb):
            rows = pl.ds(pl.multiple_of(i * tile, tile), tile)
            t = top[rows, :]
            b = bottom[rows, :]
            t, b = cb * t + sb * b, cb * b - sb * t
            b = pltpu.roll(b, WIDTH - 1, 1)
            top[rows, :] = t
            bottom[rows, :] = b
            return acc[0] + t * t, acc[1] + b * b, acc[2] + t * b

        sums = lax.fori_loop(0, count, rotate, (zero, zero, zero), unroll=4)

    part = lax.axis_index("rep") // PARTS
    here = pl.ds(pl.multiple_of(part * LANES, LANES), LANES)
    after = pl.ds(pl.multiple_of(lax.rem(part + 1, PARTS) * LANES, LANES), LANES)
    lane_group = lax.broadcasted_iota(jnp.int32, (8, LANES), 1) // HALO

    def folded(block, q):
        out = block[pl.ds(8 * q, 8), after]
        for g in range(1, GROUPS):
            piece = block[pl.ds(g * HALO_ROWS + 8 * q, 8), after]
            out = jnp.where(lane_group == g, pltpu.roll(piece, g * HALO, 1), out)
        return out

    t = top[:, here]
    b = bottom[:, here]
    top_out[pl.ds(0, ROOT_ROWS), :] = t
    both_out[pl.ds(0, ROOT_ROWS), :] = t
    bottom_out[pl.ds(0, ROOT_ROWS), :] = b
    both_out[pl.ds(CHUNK_ROWS, ROOT_ROWS), :] = b
    for q in range(HALO_ROWS // 8):
        t = folded(top, q)
        b = folded(bottom, q)
        top_out[pl.ds(ROOT_ROWS + 8 * q, 8), :] = t
        both_out[pl.ds(ROOT_ROWS + 8 * q, 8), :] = t
        bottom_out[pl.ds(ROOT_ROWS + 8 * q, 8), :] = b
        both_out[pl.ds(CHUNK_ROWS + ROOT_ROWS + 8 * q, 8), :] = b


def gradient_first_kernel(grad_ref, turn_ref, top_out, both_out, bottom_out):
    tile = 16
    count = grad_ref.shape[0] // tile

    def body(i, carry):
        rows = pl.ds(pl.multiple_of(i * tile, tile), tile)
        t = grad_ref[rows, pl.ds(0, WIDTH)].astype(jnp.float32)
        b = grad_ref[rows, pl.ds(WIDTH, WIDTH)].astype(jnp.float32)
        for step in range(SWEEPS):
            c = turn_ref[pl.ds(step, 1), :]
            s = turn_ref[pl.ds(SWEEPS + step, 1), :]
            t, b = c * t + s * b, c * b - s * t
            b = pltpu.roll(b, WIDTH - 1, 1)
        top_out[rows, :] = t
        both_out[rows, :] = t
        bottom_out[rows, :] = b
        both_out[pl.ds(pl.multiple_of(i * tile + grad_ref.shape[0], tile), tile), :] = b
        return carry

    lax.fori_loop(0, count, body, 0)


def cone_kernel(top0, pair1, pair2, bottom2, turn_out, blocks):
    lane = lax.broadcasted_iota(jnp.int32, (8, LANES), 1)
    last = lane == LANES - 1
    main_count = ROOT_ROWS // 8
    halo_count = HALO_ROWS // 8
    zero = jnp.zeros((8, LANES), jnp.float32)
    blocks[0] = top0[...]
    blocks[1] = pair1[pl.ds(0, CHUNK_ROWS), :]
    blocks[3] = pair1[pl.ds(CHUNK_ROWS, CHUNK_ROWS), :]
    blocks[2] = pair2[pl.ds(0, CHUNK_ROWS), :]
    blocks[4] = pair2[pl.ds(CHUNK_ROWS, CHUNK_ROWS), :]
    blocks[5] = bottom2[...]

    def halo_total(acc):
        row = total8(acc)
        for by in (HALO, 2 * HALO, 4 * HALO):
            row = row + pltpu.roll(row, by, 1)
        return row

    def sums_of(pairs):
        out = []
        for ti, bi in pairs:
            for first, count, fold in ((0, main_count, total8), (main_count, halo_count, halo_total)):
                acc = (zero, zero, zero)
                for v in range(count):
                    rows = pl.ds(8 * (first + v), 8)
                    t = blocks[ti, rows, :]
                    b = blocks[3 + bi, rows, :]
                    acc = acc[0] + t * t, acc[1] + b * b, acc[2] + t * b
                out.append(tuple(fold(a) for a in acc))
        return out

    def stacked(sums):
        pad = [jnp.zeros((1, LANES), jnp.float32)] * (8 - len(sums))
        return tuple(jnp.concatenate([s[j] for s in sums] + pad, axis=0) for j in range(3))

    base = 0
    for pairs in ROUND_PAIRS:
        n = len(pairs)

        def step_body(k, sums, pairs=pairs, n=n, base=base):
            cosine, sine = turn_of(*sums)
            out = []
            for p, (ti, bi) in enumerate(pairs):
                row = base + p * SWEEPS + k
                turn_out[0, pl.ds(row, 1), :] = cosine[2 * p : 2 * p + 1]
                turn_out[0, pl.ds(STEPS + row, 1), :] = sine[2 * p : 2 * p + 1]
                c = jnp.broadcast_to(cosine[2 * p + 1 : 2 * p + 2], (8, LANES))
                s = jnp.broadcast_to(sine[2 * p + 1 : 2 * p + 2], (8, LANES))
                hacc = (zero, zero, zero)
                turned = []
                for v in range(halo_count):
                    rows = pl.ds(8 * (main_count + v), 8)
                    t = blocks[ti, rows, :]
                    b = blocks[3 + bi, rows, :]
                    t, b = c * t + s * b, c * b - s * t
                    turned.append(b)
                    b = pltpu.roll(b, LANES - 1, 1)
                    blocks[ti, rows, :] = t
                    blocks[3 + bi, rows, :] = b
                    hacc = hacc[0] + t * t, hacc[1] + b * b, hacc[2] + t * b
                c = jnp.broadcast_to(cosine[2 * p : 2 * p + 1], (8, LANES))
                s = jnp.broadcast_to(sine[2 * p : 2 * p + 1], (8, LANES))
                acc = (zero, zero, zero)
                for v in range(main_count):
                    rows = pl.ds(8 * v, 8)
                    t = blocks[ti, rows, :]
                    b = blocks[3 + bi, rows, :]
                    t, b = c * t + s * b, c * b - s * t
                    g, q = divmod(8 * v, HALO_ROWS)
                    entering = pltpu.roll(turned[q // 8], LANES - 1 - g * HALO, 1)
                    b = jnp.where(last, entering, pltpu.roll(b, LANES - 1, 1))
                    blocks[ti, rows, :] = t
                    blocks[3 + bi, rows, :] = b
                    acc = acc[0] + t * t, acc[1] + b * b, acc[2] + t * b
                out.append(tuple(total8(a) for a in acc))
                out.append(tuple(halo_total(a) for a in hacc))
            return stacked(out)

        sums = lax.fori_loop(0, SWEEPS, step_body, stacked(sums_of(pairs)))
        base += n * SWEEPS
    turn_out[0, pl.ds(EIGEN_ROW, 1), :] = sums[0][0:1] * (1.0 / ROOT_ROWS)
    turn_out[0, pl.ds(EIGEN_ROW + 1, 1), :] = sums[1][0:1] * (1.0 / ROOT_ROWS)
    turn_out[0, pl.ds(EIGEN_ROW + 2, 6), :] = jnp.zeros((6, LANES), jnp.float32)
    for copy in range(1, PARTS):
        turn_out[copy] = turn_out[0]


def last_kernel(top0, pair1, pair2, bottom2, turns, eigen_out, projected_out, wide):
    tile = 8
    rows_all = top0.shape[0]
    for part in range(PARTS):
        wide[:, pl.ds(part * LANES, LANES)] = turns[part]

    def body(i, carry):
        rows = pl.ds(pl.multiple_of(i * tile, tile), tile)
        low = pl.ds(pl.multiple_of(i * tile + rows_all, tile), tile)
        tops = [top0[rows, :], pair1[rows, :], pair2[rows, :]]
        bottoms = [pair1[low, :], pair2[low, :], bottom2[rows, :]]
        base = 0
        for pairs in ROUND_PAIRS:
            for k in range(SWEEPS):
                for p, (ti, bi) in enumerate(pairs):
                    row = base + p * SWEEPS + k
                    c = wide[pl.ds(row, 1), :]
                    s = wide[pl.ds(STEPS + row, 1), :]
                    t, b = tops[ti], bottoms[bi]
                    tops[ti], b = c * t + s * b, c * b - s * t
                    bottoms[bi] = pltpu.roll(b, WIDTH - 1, 1)
            base += len(pairs) * SWEEPS
        t = tops[0]
        b = pltpu.roll(bottoms[2], 4 * SWEEPS, 1)
        projected_out[rows, pl.ds(0, WIDTH)] = t * t
        projected_out[rows, pl.ds(WIDTH, WIDTH)] = b * b
        return carry

    lax.fori_loop(0, rows_all // tile, body, 0)
    eigen_out[pl.ds(0, 1), :] = wide[pl.ds(EIGEN_ROW, 1), :]
    eigen_out[pl.ds(1, 1), :] = pltpu.roll(wide[pl.ds(EIGEN_ROW + 1, 1), :], 4 * SWEEPS, 1)


def call(kernel, outs, scratch, args, flops):
    f32 = jnp.float32
    vmem = pl.BlockSpec(memory_space=pltpu.VMEM)
    shapes = tuple(jax.ShapeDtypeStruct(shape, f32) for shape in outs)
    moved = sum(a.size * a.dtype.itemsize for a in args) + sum(4 * s.size for s in shapes)
    return pl.pallas_call(
        kernel,
        out_shape=shapes,
        in_specs=[vmem] * len(args),
        out_specs=tuple(vmem for _ in shapes),
        scratch_shapes=[pltpu.VMEM(shape, f32) for shape in scratch],
        compiler_params=pltpu.CompilerParams(vmem_limit_bytes=24 * MEGA),
        cost_estimate=pl.CostEstimate(flops=flops, bytes_accessed=moved, transcendentals=0),
    )(*args)


def from_slot(shard, offset):
    length = lax.axis_size("blk")
    return lax.ppermute(shard, "blk", [((i + offset) % length, i) for i in range(length)])


def body(root_rows, gradient):
    rows = gradient.shape[0]
    top_root, both_root, bottom_root, turn0 = call(
        first_kernel,
        [(CHUNK_ROWS, LANES), (2 * CHUNK_ROWS, LANES), (CHUNK_ROWS, LANES), (2 * SWEEPS, WIDTH)],
        [(ROOT_ROWS, WIDTH), (ROOT_ROWS, WIDTH)],
        [root_rows],
        16 * ROOT_ROWS * WIDTH * SWEEPS,
    )
    root3 = from_slot(bottom_root, 3)
    root0 = from_slot(top_root, -3)
    root1 = from_slot(both_root, -1)
    root2 = from_slot(both_root, 1)
    top_grad, both_grad, bottom_grad = call(
        gradient_first_kernel,
        [(rows, WIDTH), (2 * rows, WIDTH), (rows, WIDTH)],
        [],
        [gradient, turn0],
        8 * rows * WIDTH * SWEEPS,
    )
    grad1 = from_slot(both_grad, -1)
    grad2 = from_slot(both_grad, 1)
    grad0 = from_slot(top_grad, -3)
    grad3 = from_slot(bottom_grad, 3)
    (turns,) = call(
        cone_kernel,
        [(PARTS, ANGLE_ROWS, LANES)],
        [(6, CHUNK_ROWS, LANES)],
        [root0, root1, root2, root3],
        16 * CHUNK_ROWS * LANES * STEPS,
    )
    reps = lax.axis_size("rep")
    near = reps // PARTS
    groups = [[x * near + z for x in range(PARTS)] for z in range(near)]
    turns = lax.all_to_all(turns, "rep", 0, 0, axis_index_groups=groups)
    eigen, projected = call(
        last_kernel,
        [(2, WIDTH), (rows, 2 * WIDTH)],
        [(ANGLE_ROWS, WIDTH)],
        [grad0, grad1, grad2, grad3, turns],
        8 * rows * WIDTH * STEPS,
    )
    return eigen.reshape(2 * WIDTH), projected


def solution(mesh):
    return jax.shard_map(
        body,
        mesh=mesh,
        in_specs=(P(None, "blk"), P("rep", "blk")),
        out_specs=(P("blk"), P("rep", "blk")),
        check_vma=False,
    )
```

time: 71 us -> 73.3 us (1.032)
  Pallas kernels: 0 us -> 33.9 us
  other arithmetic: 12.7 us -> 0 us
  waiting for transfers between devices: 28.3 us -> 17.1 us
  local copies, waits for them, and re-layouts: 6.41 us -> 1.81 us
  starting transfers between devices: 21.2 us -> 18.7 us
  between operations: 1.48 us -> 0.66 us
    pallas_call x0 -> x4, Pallas kernels: none -> 33.9 us  [call(): pl.pallas_call(kernel, out_shape=shapes, in_specs=[vmem] * len(args), out...]
    ppermute x12 -> x8, waiting for transfers between devices: 28.3 us -> 12.4 us  [from_slot(): lax.ppermute(shard, 'blk', [((i + offset) % length, i) for i in range(len...]
    ppermute x12 -> x8, starting transfers between devices: 21.2 us -> 14.7 us  [from_slot(): lax.ppermute(shard, 'blk', [((i + offset) % length, i) for i in range(len...]
    slice x66 -> x0, local copies, waits for them, and re-layouts: 5.85 us -> none  [the longest x32 3.44 us: body(): bottom_root = jnp.roll(bottom_root, -1, axis=1)]
    reduce_sum x18 -> x0, other arithmetic: 5.11 us -> none  [the longest x16 4.79 us: pair_angles(): jnp.sum(top_root * bottom_root, axis=0)]
    all_to_all x0 -> x1, waiting for transfers between devices: none -> 4.73 us  [body(): turns = lax.all_to_all(turns, 'rep', 0, 0, axis_index_groups=groups)]
    all_to_all x0 -> x1, starting transfers between devices: none -> 4.01 us  [body(): turns = lax.all_to_all(turns, 'rep', 0, 0, axis_index_groups=groups)]
    sub x30 -> x0, other arithmetic: 3.88 us -> none  [rotate_pair(): cosine * bottom_part - sine_part * top_part]
  transfers between devices with their start and end apart: 12 -> 9, of which waited for: 7 -> 3; matrix products, arithmetic and copies ran while one was open for 16% -> 0% of each run, Pallas kernels for 0% -> 11%
where the time goes in v1:
time: 73.3 us; the launch traced here: 72.2 us
  Pallas kernels  33.9 us (46%)
  starting transfers between devices  18.7 us (26%)
  waiting for transfers between devices  17.1 us (23%)
  local copies, waits for them, and re-layouts  1.81 us (2%)
    pallas_call x4, Pallas kernels, call(): pl.pallas_call(kernel, out_shape=shapes, in_specs=[vmem] * len(args), out...  33.9 us
    ppermute x8, starting transfers between devices, from_slot(): lax.ppermute(shard, 'blk', [((i + offset) % length, i) for i in range(len...  14.7 us
    ppermute x8, waiting for transfers between devices, from_slot(): lax.ppermute(shard, 'blk', [((i + offset) % length, i) for i in range(len...  12.4 us
    all_to_all x1, waiting for transfers between devices, body(): turns = lax.all_to_all(turns, 'rep', 0, 0, axis_index_groups=groups)  4.73 us
    all_to_all x1, starting transfers between devices, body(): turns = lax.all_to_all(turns, 'rep', 0, 0, axis_index_groups=groups)  4.01 us
    unnamed x5, local copies, waits for them, and re-layouts  1.81 us
  transfers between devices with their start and end apart: 9, of which 3 were waited for; matrix products, arithmetic and copies ran while one was open for 0% of the time, Pallas kernels for 11%

profile of v1, /device:TPU:1, one launch (start us, length us, event | category | flops | bytes accessed | tf_op | source)
XLA Modules:
  0.0 72.2 jit_solution(6188241571035187603)
XLA Ops:
  0.6 0.0 copy-start
  0.6 1.2 %copy-done = f32[256,1024]{1,0:T(8,128)S(1)} copy-done((f32[256,1024]{1,0:T(8,128)S(1)}, f32[256,1024]{1,0:T(8,128)}, u32[]{:S(2)}) %copy-start) | copy-done | bytes 1048600
  1.9 0.0 copy-start.1
  1.9 10.2 %shard_map.41 = (f32[288,128]{1,0:T(8,128)S(1)}, f32[576,128]{1,0:T(8,128)S(1)}, f32[288,128]{1,0:T(8,128)S(1)}, f32[8,512]{1,0:T(8,128)S(1)}) custom-call(f32[256,1024]{1,0:T(8,128)S(1)} %copy-done), custom_call_target="tpu_custom_call" | custom-call | flops 8388608 | bytes 1654784 | tf_op jit(solution)/shard_map/pallas_call | solution.py:256
  12.1 3.3 %collective-permute-start.6 = (f32[576,128]{1,0:T(8,128)S(1)}, f32[576,128]{1,0:T(8,128)S(1)}, u32[]{:S(2)}, u32[]{:S(2)}) collective-permute-start(f32[576,128]{1,0:T(8,128)S(1)} %get-tuple-element.16), channel_id=1, source_target_pairs={{16,0},{32,16},{48,32},{64,48},{80,64},{96,80},{112,96},{128,112},... | collective-permute-start | bytes 884744 | tf_op jit(solution)/shard_map/ppermute | solution.py:269
  15.4 0.7 collective-permute-start.4
  16.1 0.0 copy-done.1
  16.1 2.4 %shard_map.42 = (f32[128,512]{1,0:T(8,128)S(1)}, f32[256,512]{1,0:T(8,128)S(1)}, f32[128,512]{1,0:T(8,128)S(1)}) custom-call(bf16[128,1024]{1,0:T(8,128)(2,1)S(1)} %copy-done.1, f32[8,512]{1,0:T(8,128)S(1)} %get-tuple-element.11.turn_ref), custom_call_target="tpu_custom_call" | custom-call | flops 2097152 | bytes 1327104 | tf_op jit(solution)/shard_map/pallas_call | solution.py:256
  18.5 1.4 %collective-permute-start.2 = (f32[256,512]{1,0:T(8,128)S(1)}, f32[256,512]{1,0:T(8,128)S(1)}, u32[]{:S(2)}, u32[]{:S(2)}) collective-permute-start(f32[256,512]{1,0:T(8,128)S(1)} %get-tuple-element.13), channel_id=1, source_target_pairs={{16,0},{32,16},{48,32},{64,48},{80,64},{96,80},{112,96},{128,112},... | collective-permute-start | bytes 1572872 | tf_op jit(solution)/shard_map/ppermute | solution.py:269
  19.9 0.4 collective-permute-start.1
  20.3 3.7 %collective-permute-start.7 = (f32[288,128]{1,0:T(8,128)S(1)}, f32[288,128]{1,0:T(8,128)S(1)}, u32[]{:S(2)}, u32[]{:S(2)}) collective-permute-start(f32[288,128]{1,0:T(8,128)S(1)} %get-tuple-element.17), channel_id=1, source_target_pairs={{48,0},{64,16},{80,32},{96,48},{112,64},{128,80},{144,96},{160,112... | collective-permute-start | bytes 442376 | tf_op jit(solution)/shard_map/ppermute | solution.py:269
  23.9 0.0 collective-permute-done.4.top0
  23.9 0.7 collective-permute-start.5
  24.6 10.6 %collective-permute-done.7.bottom2 = f32[288,128]{1,0:T(8,128)S(1)} collective-permute-done((f32[288,128]{1,0:T(8,128)S(1)}, f32[288,128]{1,0:T(8,128)S(1)}, u32[]{:S(2)}, u32[]{:S(2)}) %collective-permute-start.7) | collective-permute-done | bytes 147488 | tf_op jit(solution)/shard_map/ppermute | solution.py:269
  35.2 1.0 %collective-permute-start = (f32[128,512]{1,0:T(8,128)S(1)}, f32[128,512]{1,0:T(8,128)S(1)}, u32[]{:S(2)}, u32[]{:S(2)}) collective-permute-start(f32[128,512]{1,0:T(8,128)S(1)} %get-tuple-element.12), channel_id=1, source_target_pairs={{208,0},{224,16},{240,32},{0,48},{16,64},{32,80},{48,96},{64,112},... | collective-permute-start | bytes 786440 | tf_op jit(solution)/shard_map/ppermute | solution.py:269
  36.2 0.0 collective-permute-done.6.pair2
  36.2 3.6 %collective-permute-start.3 = (f32[128,512]{1,0:T(8,128)S(1)}, f32[128,512]{1,0:T(8,128)S(1)}, u32[]{:S(2)}, u32[]{:S(2)}) collective-permute-start(f32[128,512]{1,0:T(8,128)S(1)} %get-tuple-element.14), channel_id=1, source_target_pairs={{48,0},{64,16},{80,32},{96,48},{112,64},{128,80},{144,96},{160,112... | collective-permute-start | bytes 786440 | tf_op jit(solution)/shard_map/ppermute | solution.py:269
  39.8 1.7 %collective-permute-done.5.pair1 = f32[576,128]{1,0:T(8,128)S(1)} collective-permute-done((f32[576,128]{1,0:T(8,128)S(1)}, f32[576,128]{1,0:T(8,128)S(1)}, u32[]{:S(2)}, u32[]{:S(2)}) %collective-permute-start.5) | collective-permute-done | bytes 294944 | tf_op jit(solution)/shard_map/ppermute | solution.py:269
  41.6 5.6 %shard_map.43 = f32[4,56,128]{2,1,0:T(8,128)} custom-call(f32[288,128]{1,0:T(8,128)S(1)} %collective-permute-done.4.top0, f32[576,128]{1,0:T(8,128)S(1)} %collective-permute-done.5.pair1, f32[576,128]{1,0:T(8,128)S(1)} %collective-permute-done.6.pair2, f32[288,128]{1,0:T(8,128)S(1)} %collective-permute-done.7.bottom2), custom_call_target="tpu_custom_call" | custom-call | flops 14155776 | bytes 999424 | tf_op jit(solution)/shard_map/pallas_call | solution.py:256
  47.2 4.0 %all-to-all-start = ((f32[4,56,128]{2,1,0:T(8,128)}), f32[4,56,128]{2,1,0:T(8,128)S(1)}, u32[]{:S(2)}, u32[]{:S(2)}) async-start(f32[4,56,128]{2,1,0:T(8,128)} %shard_map.43), calls=%async_computation | async-start | bytes 229376 | tf_op jit(solution)/shard_map/all_to_all | solution.py:306
  51.2 0.0 collective-permute-done.top0
  51.2 0.0 collective-permute-done.3.bottom2
  51.2 4.7 %all-to-all-done.turns = f32[4,56,128]{2,1,0:T(8,128)S(1)} async-done(((f32[4,56,128]{2,1,0:T(8,128)}), f32[4,56,128]{2,1,0:T(8,128)S(1)}, u32[]{:S(2)}, u32[]{:S(2)}) %all-to-all-start) | async-done | bytes 114720 | tf_op jit(solution)/shard_map/all_to_all | solution.py:306
  55.9 0.0 collective-permute-done.2.pair2
  55.9 0.0 collective-permute-done.1.pair1
  56.0 15.7 %shard_map.44 = (f32[2,512]{1,0:T(2,128)S(1)}, f32[128,1024]{1,0:T(8,128)}) custom-call(f32[128,512]{1,0:T(8,128)S(1)} %collective-permute-done.top0, f32[256,512]{1,0:T(8,128)S(1)} %collective-permute-done.1.pair1, f32[256,512]{1,0:T(8,128)S(1)} %collective-permute-done.2.pair2, f32[128,512]{1,0:T(8,128)S(1)} %collective-permute-done.3.bottom2, ...), custom_call_target="tpu_custom_call" | custom-call | flops 12582912 | bytes 2215936 | tf_op jit(solution)/shard_map/pallas_call | solution.py:256
  71.6 0.6 copy.4
Async XLA Ops:
  0.6 1.2 %copy-start = (f32[256,1024]{1,0:T(8,128)S(1)}, f32[256,1024]{1,0:T(8,128)}, u32[]{:S(2)}) copy-start(f32[256,1024]{1,0:T(8,128)} %root_ref.1) | copy-start | bytes 3145732
  1.9 14.2 %copy-start.1 = (bf16[128,1024]{1,0:T(8,128)(2,1)S(1)}, bf16[128,1024]{1,0:T(8,128)(2,1)}, u32[]{:S(2)}) copy-start(bf16[128,1024]{1,0:T(8,128)(2,1)} %grad_ref.1) | copy-start | bytes 786436
  12.1 24.1 %collective-permute-start.6 = (f32[576,128]{1,0:T(8,128)S(1)}, f32[576,128]{1,0:T(8,128)S(1)}, u32[]{:S(2)}, u32[]{:S(2)}) collective-permute-start(f32[576,128]{1,0:T(8,128)S(1)} %get-tuple-element.16), channel_id=1, source_target_pairs={{16,0},{32,16},{48,32},{64,48},{80,64},{96,80},{112,96},{128,112},... | collective-permute-start | bytes 884744 | tf_op jit(solution)/shard_map/ppermute | solution.py:269
  15.4 8.5 %collective-permute-start.4 = (f32[288,128]{1,0:T(8,128)S(1)}, f32[288,128]{1,0:T(8,128)S(1)}, u32[]{:S(2)}, u32[]{:S(2)}) collective-permute-start(f32[288,128]{1,0:T(8,128)S(1)} %get-tuple-element.15), channel_id=1, source_target_pairs={{208,0},{224,16},{240,32},{0,48},{16,64},{32,80},{48,96},{64,112},... | collective-permute-start | bytes 442376 | tf_op jit(solution)/shard_map/ppermute | solution.py:269
  18.5 37.5 %collective-permute-start.2 = (f32[256,512]{1,0:T(8,128)S(1)}, f32[256,512]{1,0:T(8,128)S(1)}, u32[]{:S(2)}, u32[]{:S(2)}) collective-permute-start(f32[256,512]{1,0:T(8,128)S(1)} %get-tuple-element.13), channel_id=1, source_target_pairs={{16,0},{32,16},{48,32},{64,48},{80,64},{96,80},{112,96},{128,112},... | collective-permute-start | bytes 1572872 | tf_op jit(solution)/shard_map/ppermute | solution.py:269
  19.9 36.0 %collective-permute-start.1 = (f32[256,512]{1,0:T(8,128)S(1)}, f32[256,512]{1,0:T(8,128)S(1)}, u32[]{:S(2)}, u32[]{:S(2)}) collective-permute-start(f32[256,512]{1,0:T(8,128)S(1)} %get-tuple-element.13), channel_id=1, source_target_pairs={{240,0},{0,16},{16,32},{32,48},{48,64},{64,80},{80,96},{96,112},{1... | collective-permute-start | bytes 1572872 | tf_op jit(solution)/shard_map/ppermute | solution.py:269
  20.3 15.0 %collective-permute-start.7 = (f32[288,128]{1,0:T(8,128)S(1)}, f32[288,128]{1,0:T(8,128)S(1)}, u32[]{:S(2)}, u32[]{:S(2)}) collective-permute-start(f32[288,128]{1,0:T(8,128)S(1)} %get-tuple-element.17), channel_id=1, source_target_pairs={{48,0},{64,16},{80,32},{96,48},{112,64},{128,80},{144,96},{160,112... | collective-permute-start | bytes 442376 | tf_op jit(solution)/shard_map/ppermute | solution.py:269
  23.9 17.6 %collective-permute-start.5 = (f32[576,128]{1,0:T(8,128)S(1)}, f32[576,128]{1,0:T(8,128)S(1)}, u32[]{:S(2)}, u32[]{:S(2)}) collective-permute-start(f32[576,128]{1,0:T(8,128)S(1)} %get-tuple-element.16), channel_id=1, source_target_pairs={{240,0},{0,16},{16,32},{32,48},{48,64},{64,80},{80,96},{96,112},{1... | collective-permute-start | bytes 884744 | tf_op jit(solution)/shard_map/ppermute | solution.py:269
  35.2 16.0 %collective-permute-start = (f32[128,512]{1,0:T(8,128)S(1)}, f32[128,512]{1,0:T(8,128)S(1)}, u32[]{:S(2)}, u32[]{:S(2)}) collective-permute-start(f32[128,512]{1,0:T(8,128)S(1)} %get-tuple-element.12), channel_id=1, source_target_pairs={{208,0},{224,16},{240,32},{0,48},{16,64},{32,80},{48,96},{64,112},... | collective-permute-start | bytes 786440 | tf_op jit(solution)/shard_map/ppermute | solution.py:269
  36.2 15.0 %collective-permute-start.3 = (f32[128,512]{1,0:T(8,128)S(1)}, f32[128,512]{1,0:T(8,128)S(1)}, u32[]{:S(2)}, u32[]{:S(2)}) collective-permute-start(f32[128,512]{1,0:T(8,128)S(1)} %get-tuple-element.14), channel_id=1, source_target_pairs={{48,0},{64,16},{80,32},{96,48},{112,64},{128,80},{144,96},{160,112... | collective-permute-start | bytes 786440 | tf_op jit(solution)/shard_map/ppermute | solution.py:269
  47.2 8.8 %all-to-all-start = ((f32[4,56,128]{2,1,0:T(8,128)}), f32[4,56,128]{2,1,0:T(8,128)S(1)}, u32[]{:S(2)}, u32[]{:S(2)}) async-start(f32[4,56,128]{2,1,0:T(8,128)} %shard_map.43), calls=%async_computation | async-start | bytes 229376 | tf_op jit(solution)/shard_map/all_to_all | solution.py:306

commit v2 on v1

v2 whole, which is shorter than its diff:
```python
import functools
import jax
import jax.numpy as jnp
from jax import lax
from jax.experimental import pallas as pl
from jax.experimental.pallas import tpu as pltpu
from jax.sharding import PartitionSpec as P

ROOT_ROWS = 256
SWEEPS = 4
WIDTH = 512
LANES = 128
HALO = 16
GROUPS = LANES // HALO
HALO_ROWS = ROOT_ROWS // GROUPS
CHUNK_ROWS = ROOT_ROWS + HALO_ROWS
PARTS = WIDTH // LANES
ROUND_PAIRS = (((0, 0), (1, 1), (2, 2)), ((0, 1), (1, 2)), ((0, 2),))
STEPS = SWEEPS * sum(len(pairs) for pairs in ROUND_PAIRS)
EIGEN_ROW = 2 * STEPS
ANGLE_ROWS = 2 * STEPS + 8
MEGA = 1 << 20


def turn_of(tt, bb, tb):
    y = 2.0 * tb
    x = tt - bb
    ax = jnp.abs(x)
    ay = jnp.abs(y)
    top = jnp.maximum(ax, ay)
    none = top == 0.0
    scale = 1.0 / jnp.where(none, 1.0, top)
    xs = jnp.where(none, 1.0, ax * scale)
    ys = jnp.where(none, 0.0, ay * scale)
    inv = lax.rsqrt(xs * xs + ys * ys)
    big = jnp.sqrt(0.5 + 0.5 * (xs * inv))
    small = 0.5 * (ys * inv) / big
    forward = x >= 0.0
    cosine = jnp.where(forward, big, small)
    size = jnp.where(forward, small, big)
    return cosine, jnp.where(y < 0.0, -size, size)


def total8(acc):
    return jnp.sum(acc, axis=0, keepdims=True)


def turned_sums(source, target, cosine, sine, count):
    acc = None
    if cosine is not None:
        cosine = jnp.broadcast_to(cosine, (8, WIDTH))
        sine = jnp.broadcast_to(sine, (8, WIDTH))
    for i in range(count):
        t, b = source(i)
        if cosine is not None:
            t, b = cosine * t + sine * b, cosine * b - sine * t
            b = pltpu.roll(b, WIDTH - 1, 1)
            target(i, t, b)
        new = t * t, b * b, t * b
        acc = new if acc is None else tuple(x + y for x, y in zip(acc, new))
    return tuple(total8(x) for x in acc)


def first_kernel(root_ref, top_out, both_out, bottom_out, turn_out, top, bottom):
    count = ROOT_ROWS // 8

    def given(i):
        rows = pl.ds(8 * i, 8)
        return root_ref[rows, pl.ds(0, WIDTH)], root_ref[rows, pl.ds(WIDTH, WIDTH)]

    def kept(i):
        rows = pl.ds(8 * i, 8)
        return top[rows, :], bottom[rows, :]

    def keep(i, t, b):
        rows = pl.ds(8 * i, 8)
        top[rows, :] = t
        bottom[rows, :] = b

    def turn(step, sums):
        cosine, sine = turn_of(*sums)
        turn_out[pl.ds(step, 1), :] = cosine
        turn_out[pl.ds(SWEEPS + step, 1), :] = sine
        return cosine, sine

    sums = turned_sums(given, None, None, None, count)
    sums = turned_sums(given, keep, *turn(0, sums), count)
    lax.fori_loop(
        1, SWEEPS, lambda step, sums: turned_sums(kept, keep, *turn(step, sums), count), sums
    )

    part = lax.axis_index("rep") // PARTS
    here = pl.ds(pl.multiple_of(part * LANES, LANES), LANES)
    after = pl.ds(pl.multiple_of(lax.rem(part + 1, PARTS) * LANES, LANES), LANES)
    lane_group = lax.broadcasted_iota(jnp.int32, (8, LANES), 1) // HALO

    def folded(block, q):
        out = block[pl.ds(8 * q, 8), after]
        for g in range(1, GROUPS):
            piece = block[pl.ds(g * HALO_ROWS + 8 * q, 8), after]
            out = jnp.where(lane_group == g, pltpu.roll(piece, g * HALO, 1), out)
        return out

    t = top[:, here]
    b = bottom[:, here]
    top_out[pl.ds(0, ROOT_ROWS), :] = t
    both_out[pl.ds(0, ROOT_ROWS), :] = t
    bottom_out[pl.ds(0, ROOT_ROWS), :] = b
    both_out[pl.ds(CHUNK_ROWS, ROOT_ROWS), :] = b
    for q in range(HALO_ROWS // 8):
        t = folded(top, q)
        b = folded(bottom, q)
        top_out[pl.ds(ROOT_ROWS + 8 * q, 8), :] = t
        both_out[pl.ds(ROOT_ROWS + 8 * q, 8), :] = t
        bottom_out[pl.ds(ROOT_ROWS + 8 * q, 8), :] = b
        both_out[pl.ds(CHUNK_ROWS + ROOT_ROWS + 8 * q, 8), :] = b


def gradient_first_kernel(grad_ref, turn_ref, top_out, both_out, bottom_out):
    rows_all = grad_ref.shape[0]
    tiles = [pl.ds(8 * i, 8) for i in range(rows_all // 8)]
    for step in range(SWEEPS):
        c = jnp.broadcast_to(turn_ref[pl.ds(step, 1), :], (8, WIDTH))
        s = jnp.broadcast_to(turn_ref[pl.ds(SWEEPS + step, 1), :], (8, WIDTH))
        for i, rows in enumerate(tiles):
            low = pl.ds(rows_all + 8 * i, 8)
            if step == 0:
                if i % 2 == 0:
                    pair = grad_ref[pl.ds(8 * i, 16), :].astype(jnp.float32)
                half = pair[:8] if i % 2 == 0 else pair[8:]
                t, b = half[:, :WIDTH], half[:, WIDTH:]
            else:
                t, b = top_out[rows, :], bottom_out[rows, :]
            t, b = c * t + s * b, c * b - s * t
            b = pltpu.roll(b, WIDTH - 1, 1)
            top_out[rows, :] = t
            bottom_out[rows, :] = b
            if step == SWEEPS - 1:
                both_out[rows, :] = t
                both_out[low, :] = b


def cone_kernel(top0, pair1, pair2, bottom2, turn_out, blocks):
    count = ROOT_ROWS // 8
    per_group = HALO_ROWS // 8
    lane = lax.broadcasted_iota(jnp.int32, (8, LANES), 1)
    last = lane == LANES - 1
    lane_group = lane // HALO
    homes = ((top0, 0), (pair1, 0), (pair2, 0), (pair1, CHUNK_ROWS), (pair2, CHUNK_ROWS), (bottom2, 0))

    def unfolded(places, i):
        g, q = divmod(i, per_group)
        out = None
        for p, (ref, first) in enumerate(places):
            piece = ref[pl.ds(first + ROOT_ROWS + 8 * q, 8), :]
            piece = pltpu.roll(piece, (p - g) * HALO % LANES, 1)
            out = piece if out is None else jnp.where(lane_group == p, piece, out)
        return out

    def given(index, i):
        rows = pl.ds(8 * i, 8)
        if index < 6:
            ref, first = homes[index]
            return ref[pl.ds(first + 8 * i, 8), :]
        return blocks[index, rows, :]

    for i in range(count):
        rows = pl.ds(8 * i, 8)
        blocks[6, rows, :] = unfolded(homes[:3], i)
        blocks[7, rows, :] = unfolded(homes[3:], i)

    def all_of(pairs):
        return [(ti, 3 + bi) for ti, bi in pairs] + [(6, 7)]

    def sums_of(pairs, fetch):
        acc = [None] * (len(pairs) + 1)
        for i in range(count):
            for p, (ti, bi) in enumerate(all_of(pairs)):
                t, b = fetch(ti, i), fetch(bi, i)
                new = t * t, b * b, t * b
                acc[p] = new if acc[p] is None else tuple(x + y for x, y in zip(acc[p], new))
        return stacked(acc)

    def stacked(acc):
        pad = [jnp.zeros((1, LANES), jnp.float32)] * (4 - len(acc))
        return tuple(jnp.concatenate([total8(a[j]) for a in acc] + pad, axis=0) for j in range(3))

    def stored(index, i):
        return blocks[index, pl.ds(8 * i, 8), :]

    def step(k, sums, pairs, base, fetch):
        n = len(pairs)
        cosine, sine = turn_of(*sums)
        for p in range(n):
            row = base + p * SWEEPS + k
            turn_out[0, pl.ds(row, 1), :] = cosine[p : p + 1]
            turn_out[0, pl.ds(STEPS + row, 1), :] = sine[p : p + 1]
        cs = [jnp.broadcast_to(cosine[p : p + 1], (8, LANES)) for p in range(n + 1)]
        sn = [jnp.broadcast_to(sine[p : p + 1], (8, LANES)) for p in range(n + 1)]
        acc = [None] * (n + 1)
        for i in range(count):
            rows = pl.ds(8 * i, 8)
            t, b = stored(6, i), stored(7, i)
            t, halo = cs[n] * t + sn[n] * b, cs[n] * b - sn[n] * t
            b = pltpu.roll(halo, LANES - 1, 1)
            turned = [(t, b)]
            for p, (ti, bi) in enumerate(all_of(pairs)[:n]):
                t, b = fetch(ti, i), fetch(bi, i)
                t, b = cs[p] * t + sn[p] * b, cs[p] * b - sn[p] * t
                entering = pltpu.roll(halo, LANES - 1 - p * HALO, 1)
                b = jnp.where(last, entering, pltpu.roll(b, LANES - 1, 1))
                turned.append((t, b))
            turned = turned[1:] + turned[:1]
            for p, (ti, bi) in enumerate(all_of(pairs)):
                t, b = turned[p]
                blocks[ti, rows, :] = t
                blocks[bi, rows, :] = b
                new = t * t, b * b, t * b
                acc[p] = new if acc[p] is None else tuple(x + y for x, y in zip(acc[p], new))
        return stacked(acc)

    base = 0
    for number, pairs in enumerate(ROUND_PAIRS):
        fetch = given if number == 0 else stored
        if number > 0:
            for i in range(count):
                rows = pl.ds(8 * i, 8)
                blocks[7, rows, :] = pltpu.roll(blocks[7, rows, :], LANES - HALO, 1)
        sums = sums_of(pairs, fetch)
        first = 0
        if number == 0:
            sums = step(0, sums, pairs, base, fetch)
            first = 1
        sums = lax.fori_loop(
            first,
            SWEEPS,
            functools.partial(step, pairs=pairs, base=base, fetch=stored),
            sums,
        )
        base += len(pairs) * SWEEPS
    turn_out[0, pl.ds(EIGEN_ROW, 1), :] = sums[0][0:1] * (1.0 / ROOT_ROWS)
    turn_out[0, pl.ds(EIGEN_ROW + 1, 1), :] = sums[1][0:1] * (1.0 / ROOT_ROWS)
    turn_out[0, pl.ds(EIGEN_ROW + 2, 6), :] = jnp.zeros((6, LANES), jnp.float32)
    for copy in range(1, PARTS):
        turn_out[copy] = turn_out[0]


def last_kernel(top0, pair1, pair2, bottom2, turns, eigen_out, projected_out, wide, blocks):
    rows_all = top0.shape[0]
    count = rows_all // 8
    for part in range(PARTS):
        wide[:, pl.ds(part * LANES, LANES)] = turns[part]

    def given(index, i):
        rows, low = pl.ds(8 * i, 8), pl.ds(rows_all + 8 * i, 8)
        return (
            lambda: top0[rows, :],
            lambda: pair1[rows, :],
            lambda: pair2[rows, :],
            lambda: pair1[low, :],
            lambda: pair2[low, :],
            lambda: bottom2[rows, :],
        )[index]()

    def one_step(base, pairs, k, fresh):
        for p, (ti, bi) in enumerate(pairs):
            row = base + p * SWEEPS + k
            c = jnp.broadcast_to(wide[pl.ds(row, 1), :], (8, WIDTH))
            s = jnp.broadcast_to(wide[pl.ds(STEPS + row, 1), :], (8, WIDTH))
            for i in range(count):
                rows = pl.ds(8 * i, 8)
                if fresh:
                    t, b = given(ti, i), given(3 + bi, i)
                else:
                    t, b = blocks[ti, rows, :], blocks[3 + bi, rows, :]
                t, b = c * t + s * b, c * b - s * t
                blocks[ti, rows, :] = t
                blocks[3 + bi, rows, :] = pltpu.roll(b, WIDTH - 1, 1)

    base = 0
    for number, pairs in enumerate(ROUND_PAIRS):
        first = 0
        if number == 0:
            one_step(base, pairs, 0, True)
            first = 1

        def body(k, carry, base=base, pairs=pairs):
            one_step(base, pairs, k, False)
            return carry

        lax.fori_loop(first, SWEEPS, body, 0)
        base += len(pairs) * SWEEPS
    for i in range(count):
        rows = pl.ds(8 * i, 8)
        t = blocks[0, rows, :]
        b = pltpu.roll(blocks[5, rows, :], 4 * SWEEPS, 1)
        projected_out[rows, pl.ds(0, WIDTH)] = t * t
        projected_out[rows, pl.ds(WIDTH, WIDTH)] = b * b
    eigen_out[pl.ds(0, 1), :] = wide[pl.ds(EIGEN_ROW, 1), :]
    eigen_out[pl.ds(1, 1), :] = pltpu.roll(wide[pl.ds(EIGEN_ROW + 1, 1), :], 4 * SWEEPS, 1)


def call(kernel, outs, scratch, args, flops):
    f32 = jnp.float32
    vmem = pl.BlockSpec(memory_space=pltpu.VMEM)
    shapes = tuple(jax.ShapeDtypeStruct(shape, f32) for shape in outs)
    moved = sum(a.size * a.dtype.itemsize for a in args) + sum(4 * s.size for s in shapes)
    return pl.pallas_call(
        kernel,
        out_shape=shapes,
        in_specs=[vmem] * len(args),
        out_specs=tuple(vmem for _ in shapes),
        scratch_shapes=[pltpu.VMEM(shape, f32) for shape in scratch],
        compiler_params=pltpu.CompilerParams(vmem_limit_bytes=24 * MEGA),
        cost_estimate=pl.CostEstimate(flops=flops, bytes_accessed=moved, transcendentals=0),
    )(*args)


def from_slot(shard, offset):
    length = lax.axis_size("blk")
    return lax.ppermute(shard, "blk", [((i + offset) % length, i) for i in range(length)])


def body(root_rows, gradient):
    rows = gradient.shape[0]
    top_root, both_root, bottom_root, turn0 = call(
        first_kernel,
        [(CHUNK_ROWS, LANES), (2 * CHUNK_ROWS, LANES), (CHUNK_ROWS, LANES), (2 * SWEEPS, WIDTH)],
        [(ROOT_ROWS, WIDTH), (ROOT_ROWS, WIDTH)],
        [root_rows],
        16 * ROOT_ROWS * WIDTH * SWEEPS,
    )
    root3 = from_slot(bottom_root, 3)
    root0 = from_slot(top_root, -3)
    root1 = from_slot(both_root, -1)
    root2 = from_slot(both_root, 1)
    turn0, root0 = lax.optimization_barrier((turn0, root0))
    top_grad, both_grad, bottom_grad = call(
        gradient_first_kernel,
        [(rows, WIDTH), (2 * rows, WIDTH), (rows, WIDTH)],
        [],
        [gradient, turn0],
        8 * rows * WIDTH * SWEEPS,
    )
    grad1 = from_slot(both_grad, -1)
    grad2 = from_slot(both_grad, 1)
    grad0 = from_slot(top_grad, -3)
    grad3 = from_slot(bottom_grad, 3)
    (turns,) = call(
        cone_kernel,
        [(PARTS, ANGLE_ROWS, LANES)],
        [(8, ROOT_ROWS, LANES)],
        [root0, root1, root2, root3],
        16 * CHUNK_ROWS * LANES * STEPS,
    )
    reps = lax.axis_size("rep")
    near = reps // PARTS
    groups = [[x * near + z for x in range(PARTS)] for z in range(near)]
    turns = lax.all_to_all(turns, "rep", 0, 0, axis_index_groups=groups)
    eigen, projected = call(
        last_kernel,
        [(2, WIDTH), (rows, 2 * WIDTH)],
        [(ANGLE_ROWS, WIDTH), (6, rows, WIDTH)],
        [grad0, grad1, grad2, grad3, turns],
        8 * rows * WIDTH * STEPS,
    )
    return eigen.reshape(2 * WIDTH), projected


def solution(mesh):
    return jax.shard_map(
        body,
        mesh=mesh,
        in_specs=(P(None, "blk"), P("rep", "blk")),
        out_specs=(P("blk"), P("rep", "blk")),
        check_vma=False,
    )
```

time: 73.3 us -> 49.1 us (0.67)
  Pallas kernels: 33.9 us -> 9.01 us
  blocking collectives: 0 us -> 7.98 us
  starting transfers between devices: 18.7 us -> 14.4 us
  waiting for transfers between devices: 17.1 us -> 14.4 us
    pallas_call x4, Pallas kernels: 33.9 us -> 9.01 us  [call(): pl.pallas_call(kernel, out_shape=shapes, in_specs=[vmem] * len(args), out...]
    all_to_all x0 -> x1, blocking collectives: none -> 7.98 us  [body(): turns = lax.all_to_all(turns, 'rep', 0, 0, axis_index_groups=groups)]
    all_to_all x1 -> x0, waiting for transfers between devices: 4.73 us -> none  [body(): turns = lax.all_to_all(turns, 'rep', 0, 0, axis_index_groups=groups)]
    all_to_all x1 -> x0, starting transfers between devices: 4.01 us -> none  [body(): turns = lax.all_to_all(turns, 'rep', 0, 0, axis_index_groups=groups)]
    ppermute x8, waiting for transfers between devices: 12.4 us -> 14.4 us  [from_slot(): lax.ppermute(shard, 'blk', [((i + offset) % length, i) for i in range(len...]
  transfers between devices with their start and end apart: 9 -> 8, of which waited for: 3 -> 2; matrix products, arithmetic and copies ran while one was open for 0% -> 0% of each run, Pallas kernels for 11% -> 8%
where the time goes in v2:
time: 49.1 us; the launch traced here: 48.2 us
  starting transfers between devices  14.4 us (29%)
  waiting for transfers between devices  14.4 us (29%)
  Pallas kernels  9.01 us (18%)
  blocking collectives  7.98 us (16%)
  local copies, waits for them, and re-layouts  1.81 us (4%)
  between operations  0.68 us (1%)
    ppermute x8, starting transfers between devices, from_slot(): lax.ppermute(shard, 'blk', [((i + offset) % length, i) for i in range(len...  14.4 us
    ppermute x8, waiting for transfers between devices, from_slot(): lax.ppermute(shard, 'blk', [((i + offset) % length, i) for i in range(len...  14.4 us
    pallas_call x4, Pallas kernels, call(): pl.pallas_call(kernel, out_shape=shapes, in_specs=[vmem] * len(args), out...  9.01 us
    all_to_all x1, blocking collectives, body(): turns = lax.all_to_all(turns, 'rep', 0, 0, axis_index_groups=groups)  7.98 us
    unnamed x5, local copies, waits for them, and re-layouts  1.81 us
  transfers between devices with their start and end apart: 8, of which 2 were waited for; matrix products, arithmetic and copies ran while one was open for 0% of the time, Pallas kernels for 8%

profile of v2, /device:TPU:1, one launch (start us, length us, event | category | flops | bytes accessed | tf_op | source)
XLA Modules:
  0.0 48.2 jit_solution(249868570603019643)
XLA Ops:
  0.6 0.0 copy-start
  0.6 1.2 %copy-done = f32[256,1024]{1,0:T(8,128)S(1)} copy-done((f32[256,1024]{1,0:T(8,128)S(1)}, f32[256,1024]{1,0:T(8,128)}, u32[]{:S(2)}) %copy-start) | copy-done | bytes 1048600
  1.9 0.0 copy-start.1
  1.9 1.5 %shard_map.41 = (f32[288,128]{1,0:T(8,128)S(1)}, f32[576,128]{1,0:T(8,128)S(1)}, f32[288,128]{1,0:T(8,128)S(1)}, f32[8,512]{1,0:T(8,128)S(1)}) custom-call(f32[256,1024]{1,0:T(8,128)S(1)} %copy-done), custom_call_target="tpu_custom_call" | custom-call | flops 8388608 | bytes 1654784 | tf_op jit(solution)/shard_map/pallas_call | solution.py:308
  3.3 2.8 %collective-permute-start = (f32[288,128]{1,0:T(8,128)S(1)}, f32[288,128]{1,0:T(8,128)S(1)}, u32[]{:S(2)}, u32[]{:S(2)}) collective-permute-start(f32[288,128]{1,0:T(8,128)S(1)} %get-tuple-element.14), channel_id=1, source_target_pairs={{208,0},{224,16},{240,32},{0,48},{16,64},{32,80},{48,96},{64,112},... | collective-permute-start | bytes 442376 | tf_op jit(solution)/shard_map/ppermute | solution.py:321
  6.1 0.6 %collective-permute-start.6 = (f32[576,128]{1,0:T(8,128)S(1)}, f32[576,128]{1,0:T(8,128)S(1)}, u32[]{:S(2)}, u32[]{:S(2)}) collective-permute-start(f32[576,128]{1,0:T(8,128)S(1)} %get-tuple-element.20), channel_id=1, source_target_pairs={{16,0},{32,16},{48,32},{64,48},{80,64},{96,80},{112,96},{128,112},... | collective-permute-start | bytes 884744 | tf_op jit(solution)/shard_map/ppermute | solution.py:321
  6.8 5.1 %collective-permute-done.top0 = f32[288,128]{1,0:T(8,128)S(1)} collective-permute-done((f32[288,128]{1,0:T(8,128)S(1)}, f32[288,128]{1,0:T(8,128)S(1)}, u32[]{:S(2)}, u32[]{:S(2)}) %collective-permute-start) | collective-permute-done | bytes 147488 | tf_op jit(solution)/shard_map/ppermute | solution.py:321
  11.8 0.0 copy-done.1
  11.8 0.4 shard_map.42
  12.2 2.2 %collective-permute-start.3 = (f32[256,512]{1,0:T(8,128)S(1)}, f32[256,512]{1,0:T(8,128)S(1)}, u32[]{:S(2)}, u32[]{:S(2)}) collective-permute-start(f32[256,512]{1,0:T(8,128)S(1)} %get-tuple-element.17), channel_id=1, source_target_pairs={{16,0},{32,16},{48,32},{64,48},{80,64},{96,80},{112,96},{128,112},... | collective-permute-start | bytes 1572872 | tf_op jit(solution)/shard_map/ppermute | solution.py:321
  14.4 0.0 collective-permute-start.2
  14.4 0.3 collective-permute-start.7
  14.8 3.8 %collective-permute-start.5 = (f32[576,128]{1,0:T(8,128)S(1)}, f32[576,128]{1,0:T(8,128)S(1)}, u32[]{:S(2)}, u32[]{:S(2)}) collective-permute-start(f32[576,128]{1,0:T(8,128)S(1)} %get-tuple-element.20), channel_id=1, source_target_pairs={{240,0},{0,16},{16,32},{32,48},{48,64},{64,80},{80,96},{96,112},{1... | collective-permute-start | bytes 884744 | tf_op jit(solution)/shard_map/ppermute | solution.py:321
  18.6 9.2 %collective-permute-done.7.bottom2 = f32[288,128]{1,0:T(8,128)S(1)} collective-permute-done((f32[288,128]{1,0:T(8,128)S(1)}, f32[288,128]{1,0:T(8,128)S(1)}, u32[]{:S(2)}, u32[]{:S(2)}) %collective-permute-start.7) | collective-permute-done | bytes 147488 | tf_op jit(solution)/shard_map/ppermute | solution.py:321
  27.8 0.2 collective-permute-start.1
  27.9 0.0 collective-permute-done.6.pair2
  28.0 4.4 %collective-permute-start.4 = (f32[128,512]{1,0:T(8,128)S(1)}, f32[128,512]{1,0:T(8,128)S(1)}, u32[]{:S(2)}, u32[]{:S(2)}) collective-permute-start(f32[128,512]{1,0:T(8,128)S(1)} %get-tuple-element.18), channel_id=1, source_target_pairs={{48,0},{64,16},{80,32},{96,48},{112,64},{128,80},{144,96},{160,112... | collective-permute-start | bytes 786440 | tf_op jit(solution)/shard_map/ppermute | solution.py:321
  32.4 0.0 collective-permute-done.5.pair1
  32.4 3.7 %shard_map.43 = f32[4,56,128]{2,1,0:T(8,128)S(1)} custom-call(f32[288,128]{1,0:T(8,128)S(1)} %collective-permute-done.top0, f32[576,128]{1,0:T(8,128)S(1)} %collective-permute-done.5.pair1, f32[576,128]{1,0:T(8,128)S(1)} %collective-permute-done.6.pair2, f32[288,128]{1,0:T(8,128)S(1)} %collective-permute-done.7.bottom2), custom_call_target="tpu_custom_call" | custom-call | flops 14155776 | bytes 999424 | tf_op jit(solution)/shard_map/pallas_call | solution.py:308
  36.1 8.0 %all_to_all.5.turns = f32[4,56,128]{2,1,0:T(8,128)S(1)} all-to-all(f32[4,56,128]{2,1,0:T(8,128)S(1)} %shard_map.43), channel_id=1, replica_groups={{0,4,8,12},{1,5,9,13},{2,6,10,14},{3,7,11,15},{16,20,24,28},{17,21,25,2..., dimensions={0} | all-to-all | bytes 229376 | tf_op jit(solution)/shard_map/all_to_all | solution.py:359
  44.1 0.0 collective-permute-done.1.top0
  44.1 0.0 collective-permute-done.4.bottom2
  44.1 0.0 collective-permute-done.3.pair2
  44.1 0.0 collective-permute-done.2.pair1
  44.1 3.5 %shard_map.44 = (f32[2,512]{1,0:T(2,128)S(1)}, f32[128,1024]{1,0:T(8,128)}) custom-call(f32[128,512]{1,0:T(8,128)S(1)} %collective-permute-done.1.top0, f32[256,512]{1,0:T(8,128)S(1)} %collective-permute-done.2.pair1, f32[256,512]{1,0:T(8,128)S(1)} %collective-permute-done.3.pair2, f32[128,512]{1,0:T(8,128)S(1)} %collective-permute-done.4.bottom2, ...), custom_call_target="tpu_custom_call" | custom-call | flops 12582912 | bytes 2215936 | tf_op jit(solution)/shard_map/pallas_call | solution.py:308
  47.6 0.6 %copy.4 = f32[1,4,2,128]{3,1,2,0:T(4,128)} copy(f32[1,4,2,128]{3,2,1,0:T(2,128)S(1)} %bitcast.2) | data formatting | bytes 8192
Async XLA Ops:
  0.6 1.2 %copy-start = (f32[256,1024]{1,0:T(8,128)S(1)}, f32[256,1024]{1,0:T(8,128)}, u32[]{:S(2)}) copy-start(f32[256,1024]{1,0:T(8,128)} %root_ref.1) | copy-start | bytes 3145732
  1.9 10.0 %copy-start.1 = (bf16[128,1024]{1,0:T(8,128)(2,1)S(1)}, bf16[128,1024]{1,0:T(8,128)(2,1)}, u32[]{:S(2)}) copy-start(bf16[128,1024]{1,0:T(8,128)(2,1)} %grad_ref.1) | copy-start | bytes 786436
  3.3 8.5 %collective-permute-start = (f32[288,128]{1,0:T(8,128)S(1)}, f32[288,128]{1,0:T(8,128)S(1)}, u32[]{:S(2)}, u32[]{:S(2)}) collective-permute-start(f32[288,128]{1,0:T(8,128)S(1)} %get-tuple-element.14), channel_id=1, source_target_pairs={{208,0},{224,16},{240,32},{0,48},{16,64},{32,80},{48,96},{64,112},... | collective-permute-start | bytes 442376 | tf_op jit(solution)/shard_map/ppermute | solution.py:321
  6.1 21.8 %collective-permute-start.6 = (f32[576,128]{1,0:T(8,128)S(1)}, f32[576,128]{1,0:T(8,128)S(1)}, u32[]{:S(2)}, u32[]{:S(2)}) collective-permute-start(f32[576,128]{1,0:T(8,128)S(1)} %get-tuple-element.20), channel_id=1, source_target_pairs={{16,0},{32,16},{48,32},{64,48},{80,64},{96,80},{112,96},{128,112},... | collective-permute-start | bytes 884744 | tf_op jit(solution)/shard_map/ppermute | solution.py:321
  12.2 31.9 %collective-permute-start.3 = (f32[256,512]{1,0:T(8,128)S(1)}, f32[256,512]{1,0:T(8,128)S(1)}, u32[]{:S(2)}, u32[]{:S(2)}) collective-permute-start(f32[256,512]{1,0:T(8,128)S(1)} %get-tuple-element.17), channel_id=1, source_target_pairs={{16,0},{32,16},{48,32},{64,48},{80,64},{96,80},{112,96},{128,112},... | collective-permute-start | bytes 1572872 | tf_op jit(solution)/shard_map/ppermute | solution.py:321
  14.4 29.6 %collective-permute-start.2 = (f32[256,512]{1,0:T(8,128)S(1)}, f32[256,512]{1,0:T(8,128)S(1)}, u32[]{:S(2)}, u32[]{:S(2)}) collective-permute-start(f32[256,512]{1,0:T(8,128)S(1)} %get-tuple-element.17), channel_id=1, source_target_pairs={{240,0},{0,16},{16,32},{32,48},{48,64},{64,80},{80,96},{96,112},{1... | collective-permute-start | bytes 1572872 | tf_op jit(solution)/shard_map/ppermute | solution.py:321
  14.4 13.3 %collective-permute-start.7 = (f32[288,128]{1,0:T(8,128)S(1)}, f32[288,128]{1,0:T(8,128)S(1)}, u32[]{:S(2)}, u32[]{:S(2)}) collective-permute-start(f32[288,128]{1,0:T(8,128)S(1)} %get-tuple-element.21), channel_id=1, source_target_pairs={{48,0},{64,16},{80,32},{96,48},{112,64},{128,80},{144,96},{160,112... | collective-permute-start | bytes 442376 | tf_op jit(solution)/shard_map/ppermute | solution.py:321
  14.8 17.6 %collective-permute-start.5 = (f32[576,128]{1,0:T(8,128)S(1)}, f32[576,128]{1,0:T(8,128)S(1)}, u32[]{:S(2)}, u32[]{:S(2)}) collective-permute-start(f32[576,128]{1,0:T(8,128)S(1)} %get-tuple-element.20), channel_id=1, source_target_pairs={{240,0},{0,16},{16,32},{32,48},{48,64},{64,80},{80,96},{96,112},{1... | collective-permute-start | bytes 884744 | tf_op jit(solution)/shard_map/ppermute | solution.py:321
  27.8 16.3 %collective-permute-start.1 = (f32[128,512]{1,0:T(8,128)S(1)}, f32[128,512]{1,0:T(8,128)S(1)}, u32[]{:S(2)}, u32[]{:S(2)}) collective-permute-start(f32[128,512]{1,0:T(8,128)S(1)} %get-tuple-element.16), channel_id=1, source_target_pairs={{208,0},{224,16},{240,32},{0,48},{16,64},{32,80},{48,96},{64,112},... | collective-permute-start | bytes 786440 | tf_op jit(solution)/shard_map/ppermute | solution.py:321
  28.0 16.1 %collective-permute-start.4 = (f32[128,512]{1,0:T(8,128)S(1)}, f32[128,512]{1,0:T(8,128)S(1)}, u32[]{:S(2)}, u32[]{:S(2)}) collective-permute-start(f32[128,512]{1,0:T(8,128)S(1)} %get-tuple-element.18), channel_id=1, source_target_pairs={{48,0},{64,16},{80,32},{96,48},{112,64},{128,80},{144,96},{160,112... | collective-permute-start | bytes 786440 | tf_op jit(solution)/shard_map/ppermute | solution.py:321

commit v3 on v2

v3 whole, which is shorter than its diff:
```python
import functools
import jax
import jax.numpy as jnp
from jax import lax
from jax.experimental import pallas as pl
from jax.experimental.pallas import tpu as pltpu
from jax.sharding import PartitionSpec as P

ROOT_ROWS = 256
SWEEPS = 4
WIDTH = 512
LANES = 128
HALO = 16
GROUPS = LANES // HALO
HALO_ROWS = ROOT_ROWS // GROUPS
CHUNK_ROWS = ROOT_ROWS + HALO_ROWS
PARTS = WIDTH // LANES
ROUND_PAIRS = (((0, 0), (1, 1), (2, 2)), ((0, 1), (1, 2)), ((0, 2),))
STEPS = SWEEPS * sum(len(pairs) for pairs in ROUND_PAIRS)
EIGEN_ROW = 2 * STEPS
ANGLE_ROWS = 2 * STEPS + 8
MEGA = 1 << 20


def turn_of(tt, bb, tb):
    y = 2.0 * tb
    x = tt - bb
    ax = jnp.abs(x)
    ay = jnp.abs(y)
    top = jnp.maximum(ax, ay)
    none = top == 0.0
    scale = 1.0 / jnp.where(none, 1.0, top)
    xs = jnp.where(none, 1.0, ax * scale)
    ys = jnp.where(none, 0.0, ay * scale)
    squares = xs * xs + ys * ys
    inv = lax.rsqrt(squares)
    big = jnp.sqrt(0.5 + 0.5 * (xs * inv))
    small = 0.5 * (ys * inv) / big
    forward = x >= 0.0
    cosine = jnp.where(forward, big, small)
    size = jnp.where(forward, small, big)
    larger = 0.5 * (tt + bb) + 0.5 * (top * (squares * inv))
    return cosine, jnp.where(y < 0.0, -size, size), larger


def total8(acc):
    return jnp.sum(acc, axis=0, keepdims=True)


def added(acc, *new):
    return list(new) if acc is None else [x + y for x, y in zip(acc, new)]


def wide8(row):
    return jnp.broadcast_to(row, (8, LANES))


def first_kernel(root_ref, top_out, both_out, bottom_out, turn_out, top, bottom, rolled):
    tiles = [pl.ds(8 * i, 8) for i in range(ROOT_ROWS // 8)]
    cols = [pl.ds(g * LANES, LANES) for g in range(PARTS)]
    low_cols = [pl.ds(WIDTH + g * LANES, LANES) for g in range(PARTS)]
    last = lax.broadcasted_iota(jnp.int32, (8, LANES), 1) == LANES - 1
    tt, bb, tb = ([None] * PARTS for _ in range(3))
    for g in range(PARTS):
        acc = None
        for rows in tiles:
            t, b = root_ref[rows, cols[g]], root_ref[rows, low_cols[g]]
            acc = added(acc, b * b, t * b, t * t)
        bb[g], tb[g], tt[g] = (total8(x) for x in acc)

    def rotate(step, g):
        cosine, sine, tt[g] = turn_of(tt[g], bb[g], tb[g])
        turn_out[pl.ds(step, 1), cols[g]] = cosine
        turn_out[pl.ds(SWEEPS + step, 1), cols[g]] = sine
        c, s = wide8(cosine), wide8(sine)
        for rows in tiles:
            if step == 0:
                t, b = root_ref[rows, cols[g]], root_ref[rows, low_cols[g]]
            else:
                t, b = top[rows, cols[g]], bottom[rows, cols[g]]
            top[rows, cols[g]] = c * t + s * b
            rolled[rows, cols[g]] = pltpu.roll(c * b - s * t, LANES - 1, 1)

    def shift(step, g):
        acc = None
        for rows in tiles:
            b = jnp.where(last, rolled[rows, cols[(g + 1) % PARTS]], rolled[rows, cols[g]])
            bottom[rows, cols[g]] = b
            if step + 1 < SWEEPS:
                acc = added(acc, b * b, top[rows, cols[g]] * b)
        if step + 1 < SWEEPS:
            bb[g], tb[g] = (total8(x) for x in acc)

    for step in range(SWEEPS):
        rotate(step, 0)
        for g in range(1, PARTS):
            rotate(step, g)
            shift(step, g - 1)
        shift(step, PARTS - 1)

    part = lax.axis_index("rep") // PARTS
    here = pl.ds(pl.multiple_of(part * LANES, LANES), LANES)
    after = pl.ds(pl.multiple_of(lax.rem(part + 1, PARTS) * LANES, LANES), LANES)
    lane_group = lax.broadcasted_iota(jnp.int32, (8, LANES), 1) // HALO

    def folded(block, q):
        out = block[pl.ds(8 * q, 8), after]
        for g in range(1, GROUPS):
            piece = block[pl.ds(g * HALO_ROWS + 8 * q, 8), after]
            out = jnp.where(lane_group == g, pltpu.roll(piece, g * HALO, 1), out)
        return out

    t = top[:, here]
    b = bottom[:, here]
    top_out[pl.ds(0, ROOT_ROWS), :] = t
    both_out[pl.ds(0, ROOT_ROWS), :] = t
    bottom_out[pl.ds(0, ROOT_ROWS), :] = b
    both_out[pl.ds(CHUNK_ROWS, ROOT_ROWS), :] = b
    for q in range(HALO_ROWS // 8):
        t = folded(top, q)
        b = folded(bottom, q)
        top_out[pl.ds(ROOT_ROWS + 8 * q, 8), :] = t
        both_out[pl.ds(ROOT_ROWS + 8 * q, 8), :] = t
        bottom_out[pl.ds(ROOT_ROWS + 8 * q, 8), :] = b
        both_out[pl.ds(CHUNK_ROWS + ROOT_ROWS + 8 * q, 8), :] = b


def gradient_first_kernel(grad_ref, turn_ref, top_out, both_out, bottom_out):
    rows_all = grad_ref.shape[0]
    tiles = [pl.ds(8 * i, 8) for i in range(rows_all // 8)]
    for step in range(SWEEPS):
        c = jnp.broadcast_to(turn_ref[pl.ds(step, 1), :], (8, WIDTH))
        s = jnp.broadcast_to(turn_ref[pl.ds(SWEEPS + step, 1), :], (8, WIDTH))
        for i, rows in enumerate(tiles):
            low = pl.ds(rows_all + 8 * i, 8)
            if step == 0:
                if i % 2 == 0:
                    pair = grad_ref[pl.ds(8 * i, 16), :].astype(jnp.float32)
                half = pair[:8] if i % 2 == 0 else pair[8:]
                t, b = half[:, :WIDTH], half[:, WIDTH:]
            else:
                t, b = top_out[rows, :], bottom_out[rows, :]
            t, b = c * t + s * b, c * b - s * t
            b = pltpu.roll(b, WIDTH - 1, 1)
            top_out[rows, :] = t
            bottom_out[rows, :] = b
            if step == SWEEPS - 1:
                both_out[rows, :] = t
                both_out[low, :] = b


def cone_kernel(top0, pair1, pair2, bottom2, turn_out, blocks):
    count = ROOT_ROWS // 8
    per_group = HALO_ROWS // 8
    lane = lax.broadcasted_iota(jnp.int32, (8, LANES), 1)
    lane_group = lane // HALO
    homes = ((top0, 0), (pair1, 0), (pair2, 0), (pair1, CHUNK_ROWS), (pair2, CHUNK_ROWS), (bottom2, 0))

    def unfolded(places, i):
        g, q = divmod(i, per_group)
        out = None
        for p, (ref, first) in enumerate(places):
            piece = ref[pl.ds(first + ROOT_ROWS + 8 * q, 8), :]
            piece = pltpu.roll(piece, (p - g) * HALO % LANES, 1)
            out = piece if out is None else jnp.where(lane_group == p, piece, out)
        return out

    def given(index, i):
        rows = pl.ds(8 * i, 8)
        if index < 6:
            ref, first = homes[index]
            return ref[pl.ds(first + 8 * i, 8), :]
        return blocks[index, rows, :]

    for i in range(count):
        rows = pl.ds(8 * i, 8)
        blocks[6, rows, :] = unfolded(homes[:3], i)
        blocks[7, rows, :] = unfolded(homes[3:], i)

    def stored(index, i):
        return blocks[index, pl.ds(8 * i, 8), :]

    tt, bb, tb = ({} for _ in range(3))
    for p, (ti, bi) in enumerate(ROUND_PAIRS[0] + ((6, 4),)):
        acc = None
        for i in range(count):
            rows = pl.ds(8 * i, 8)
            t, b = given(ti, i), given(3 + bi, i)
            if p < 3:
                t, b = pltpu.roll(t, p * HALO, 1), pltpu.roll(b, p * HALO, 1)
                blocks[ti, rows, :] = t
                blocks[3 + bi, rows, :] = b
            acc = added(acc, b * b, t * b, t * t)
        bb[p], tb[p], tt[p] = (total8(x) for x in acc)

    steps = SWEEPS * len(ROUND_PAIRS)
    turns = {}

    def angles(n, p):
        if n >= steps:
            return
        cosine, sine, tt[p] = turn_of(tt[p], bb[p], tb[p])
        if p < 3:
            number, k = divmod(n, SWEEPS)
            row = SWEEPS * sum(len(q) for q in ROUND_PAIRS[:number]) + p * SWEEPS + k
            turn_out[0, pl.ds(row, 1), :] = cosine
            turn_out[0, pl.ds(STEPS + row, 1), :] = sine
        turns[p] = wide8(cosine), wide8(sine)

    def shift_of(n):
        return LANES - 1 - (HALO if n % SWEEPS == SWEEPS - 1 and n + 1 < steps else 0)

    def turn_halo(n):
        if n >= steps:
            return
        c, s = turns[3]
        acc = None
        for i in range(count):
            rows = pl.ds(8 * i, 8)
            t, b = stored(6, i), stored(7 + n % 3, i)
            t, b = c * t + s * b, c * b - s * t
            b = pltpu.roll(b, shift_of(n), 1)
            blocks[6, rows, :] = t
            blocks[7 + (n + 1) % 3, rows, :] = b
            acc = added(acc, b * b, t * b)
        bb[3], tb[3] = (total8(x) for x in acc)

    def turn_pair(n, p):
        number, k = divmod(n, SWEEPS)
        pairs = ROUND_PAIRS[number]
        ti, bi = pairs[p]
        ends = k + 1 == SWEEPS
        final = ends and number + 1 == len(ROUND_PAIRS)
        c, s = turns[p]
        need_top = not ends or p + 1 < len(pairs) or final
        need_bottom = not ends or p > 0 or final
        q = p - 1 if ends and not final else p
        by = shift_of(n)
        enters = lane == (q * HALO - 1) % LANES
        acc = None
        for i in range(count):
            rows = pl.ds(8 * i, 8)
            t, b = stored(ti, i), stored(3 + bi, i)
            top = c * t + s * b
            if need_top and not final:
                blocks[ti, rows, :] = top
            if need_bottom:
                entering = stored(7 + (n + 1) % 3, i)
                b = jnp.where(enters, entering, pltpu.roll(c * b - s * t, by, 1))
                if not final:
                    blocks[3 + bi, rows, :] = b
                other = top if q == p else stored(pairs[q][0], i)
                acc = added(acc, b * b, other * b)
        if need_bottom:
            bb[q], tb[q] = (total8(x) for x in acc)

    angles(0, 3)
    turn_halo(0)
    angles(1, 3)
    for n in range(steps):
        n_pairs = len(ROUND_PAIRS[n // SWEEPS])
        angles(n, 0)
        turn_halo(n + 1)
        for p in range(n_pairs):
            if p + 1 < n_pairs:
                angles(n, p + 1)
            if p == n_pairs - 1:
                angles(n + 2, 3)
            turn_pair(n, p)
    base = 0
    for pairs in ROUND_PAIRS:
        for p in range(len(pairs)):
            for first in (base, STEPS + base):
                rows = pl.ds(first + p * SWEEPS, SWEEPS)
                if p:
                    turn_out[0, rows, :] = pltpu.roll(turn_out[0, rows, :], LANES - p * HALO, 1)
        base += len(pairs) * SWEEPS
    turn_out[0, pl.ds(EIGEN_ROW, 1), :] = tt[0] * (1.0 / ROOT_ROWS)
    turn_out[0, pl.ds(EIGEN_ROW + 1, 1), :] = bb[0] * (1.0 / ROOT_ROWS)
    turn_out[0, pl.ds(EIGEN_ROW + 2, 6), :] = jnp.zeros((6, LANES), jnp.float32)
    for copy in range(1, PARTS):
        turn_out[copy] = turn_out[0]


def last_kernel(top0, pair1, pair2, bottom2, turns, eigen_out, projected_out, wide, blocks):
    rows_all = top0.shape[0]
    count = rows_all // 8
    for part in range(PARTS):
        wide[:, pl.ds(part * LANES, LANES)] = turns[part]

    def given(index, i):
        rows, low = pl.ds(8 * i, 8), pl.ds(rows_all + 8 * i, 8)
        return (
            lambda: top0[rows, :],
            lambda: pair1[rows, :],
            lambda: pair2[rows, :],
            lambda: pair1[low, :],
            lambda: pair2[low, :],
            lambda: bottom2[rows, :],
        )[index]()

    def row_of(row):
        return jnp.broadcast_to(wide[pl.ds(row, 1), :], (8, WIDTH))

    fresh = set()
    base = 0
    for number, pairs in enumerate(ROUND_PAIRS):
        final = number + 1 == len(ROUND_PAIRS)
        for k in range(SWEEPS):
            ends = k + 1 == SWEEPS
            for p, (ti, bi) in enumerate(pairs):
                c = row_of(base + p * SWEEPS + k)
                s = row_of(STEPS + base + p * SWEEPS + k)
                need_top = not ends or p + 1 < len(pairs) or final
                need_bottom = not ends or p > 0 or final
                for i in range(count):
                    rows = pl.ds(8 * i, 8)
                    t = blocks[ti, rows, :] if ti in fresh else given(ti, i)
                    b = blocks[3 + bi, rows, :] if 3 + bi in fresh else given(3 + bi, i)
                    if need_top:
                        top = c * t + s * b
                    if need_bottom:
                        bottom = c * b - s * t
                    if final and ends:
                        bottom = pltpu.roll(bottom, 4 * SWEEPS - 1, 1)
                        projected_out[rows, pl.ds(0, WIDTH)] = top * top
                        projected_out[rows, pl.ds(WIDTH, WIDTH)] = bottom * bottom
                        continue
                    if need_top:
                        blocks[ti, rows, :] = top
                    if need_bottom:
                        blocks[3 + bi, rows, :] = pltpu.roll(bottom, WIDTH - 1, 1)
                fresh |= {ti, 3 + bi}
        base += len(pairs) * SWEEPS
    eigen_out[pl.ds(0, WIDTH)] = wide[EIGEN_ROW, :]
    bottom = pltpu.roll(wide[pl.ds(EIGEN_ROW + 1, 1), :], 4 * SWEEPS, 1)
    eigen_out[pl.ds(WIDTH, WIDTH)] = bottom[0]


def call(kernel, outs, scratch, args, flops):
    f32 = jnp.float32
    vmem = pl.BlockSpec(memory_space=pltpu.VMEM)
    shapes = tuple(jax.ShapeDtypeStruct(shape, f32) for shape in outs)
    moved = sum(a.size * a.dtype.itemsize for a in args) + sum(4 * s.size for s in shapes)
    return pl.pallas_call(
        kernel,
        out_shape=shapes,
        in_specs=[vmem] * len(args),
        out_specs=tuple(vmem for _ in shapes),
        scratch_shapes=[pltpu.VMEM(shape, f32) for shape in scratch],
        compiler_params=pltpu.CompilerParams(vmem_limit_bytes=24 * MEGA),
        cost_estimate=pl.CostEstimate(flops=flops, bytes_accessed=moved, transcendentals=0),
    )(*args)


def from_slot(shard, offset):
    length = lax.axis_size("blk")
    return lax.ppermute(shard, "blk", [((i + offset) % length, i) for i in range(length)])


def body(root_rows, gradient):
    rows = gradient.shape[0]
    top_root, both_root, bottom_root, turn0 = call(
        first_kernel,
        [(CHUNK_ROWS, LANES), (2 * CHUNK_ROWS, LANES), (CHUNK_ROWS, LANES), (2 * SWEEPS, WIDTH)],
        [(ROOT_ROWS, WIDTH)] * 3,
        [root_rows],
        16 * ROOT_ROWS * WIDTH * SWEEPS,
    )
    root3 = from_slot(bottom_root, 3)
    root0 = from_slot(top_root, -3)
    root1 = from_slot(both_root, -1)
    root2 = from_slot(both_root, 1)
    top_grad, both_grad, bottom_grad = call(
        gradient_first_kernel,
        [(rows, WIDTH), (2 * rows, WIDTH), (rows, WIDTH)],
        [],
        [gradient, turn0],
        8 * rows * WIDTH * SWEEPS,
    )
    def after(value, *others):
        return lax.optimization_barrier((value, *others))[0]

    grad1 = from_slot(after(both_grad, root0), -1)
    grad2 = from_slot(after(both_grad, root3), 1)
    grad0 = from_slot(after(top_grad, root1), -3)
    grad3 = from_slot(after(bottom_grad, root2), 3)
    (turns,) = call(
        cone_kernel,
        [(PARTS, ANGLE_ROWS, LANES)],
        [(10, ROOT_ROWS, LANES)],
        [root0, root1, root2, root3],
        16 * CHUNK_ROWS * LANES * STEPS,
    )
    reps = lax.axis_size("rep")
    near = reps // PARTS
    groups = [[x * near + z for x in range(PARTS)] for z in range(near)]
    turns = lax.all_to_all(turns, "rep", 0, 0, axis_index_groups=groups)
    eigen, projected = call(
        last_kernel,
        [(2 * WIDTH,), (rows, 2 * WIDTH)],
        [(ANGLE_ROWS, WIDTH), (6, rows, WIDTH)],
        [grad0, grad1, grad2, grad3, turns],
        8 * rows * WIDTH * STEPS,
    )
    return eigen, projected


def solution(mesh):
    return jax.shard_map(
        body,
        mesh=mesh,
        in_specs=(P(None, "blk"), P("rep", "blk")),
        out_specs=(P("blk"), P("rep", "blk")),
        check_vma=False,
    )
```

time: 49.1 us -> 40.4 us (0.82); the launches traced: 48.2 us -> 40.2 us
  starting transfers between devices: 14.4 us -> 11.1 us
  waiting for transfers between devices: 14.4 us -> 12.4 us
  Pallas kernels: 9.01 us -> 7.48 us
  blocking collectives: 7.98 us -> 7.35 us
  local copies, waits for them, and re-layouts: 1.81 us -> 1.22 us
    ppermute x8, starting transfers between devices: 14.4 us -> 11.1 us  [from_slot(): lax.ppermute(shard, 'blk', [((i + offset) % length, i) for i in range(len...]
    ppermute x8, waiting for transfers between devices: 14.4 us -> 12.4 us  [from_slot(): lax.ppermute(shard, 'blk', [((i + offset) % length, i) for i in range(len...]
    pallas_call x4, Pallas kernels: 9.01 us -> 7.48 us  [call(): pl.pallas_call(kernel, out_shape=shapes, in_specs=[vmem] * len(args), out...]
    all_to_all x1, blocking collectives: 7.98 us -> 7.35 us  [body(): turns = lax.all_to_all(turns, 'rep', 0, 0, axis_index_groups=groups)]
    unnamed x5 -> x4, local copies, waits for them, and re-layouts: 1.81 us -> 1.22 us
  transfers between devices with their start and end apart: 8 -> 8, of which waited for: 2 -> 5; matrix products, arithmetic and copies ran while one was open for 0% -> 0% of each run, Pallas kernels for 8% -> 8%
where the time goes in v3:
time: 40.4 us; the launch traced here: 40.2 us
  waiting for transfers between devices  12.4 us (31%)
  starting transfers between devices  11.1 us (27%)
  Pallas kernels  7.48 us (19%)
  blocking collectives  7.35 us (18%)
  local copies, waits for them, and re-layouts  1.22 us (3%)
  between operations  0.67 us (2%)
    ppermute x8, waiting for transfers between devices, from_slot(): lax.ppermute(shard, 'blk', [((i + offset) % length, i) for i in range(len...  12.4 us
    ppermute x8, starting transfers between devices, from_slot(): lax.ppermute(shard, 'blk', [((i + offset) % length, i) for i in range(len...  11.1 us
    pallas_call x4, Pallas kernels, call(): pl.pallas_call(kernel, out_shape=shapes, in_specs=[vmem] * len(args), out...  7.48 us
    all_to_all x1, blocking collectives, body(): turns = lax.all_to_all(turns, 'rep', 0, 0, axis_index_groups=groups)  7.35 us
    unnamed x4, local copies, waits for them, and re-layouts  1.22 us
  transfers between devices with their start and end apart: 8, of which 5 were waited for; matrix products, arithmetic and copies ran while one was open for 0% of the time, Pallas kernels for 8%

profile of v3, /device:TPU:1, one launch (start us, length us, event | category | flops | bytes accessed | tf_op | source)
XLA Modules:
  0.0 40.2 jit_solution(11144198229840584114)
XLA Ops:
  0.6 0.0 copy-start
  0.6 1.2 %copy-done = f32[256,1024]{1,0:T(8,128)S(1)} copy-done((f32[256,1024]{1,0:T(8,128)S(1)}, f32[256,1024]{1,0:T(8,128)}, u32[]{:S(2)}) %copy-start) | copy-done | bytes 1048600
  1.9 0.0 copy-start.1
  1.9 1.5 %shard_map.41 = (f32[288,128]{1,0:T(8,128)S(1)}, f32[576,128]{1,0:T(8,128)S(1)}, f32[288,128]{1,0:T(8,128)S(1)}, f32[8,512]{1,0:T(8,128)S(1)}) custom-call(f32[256,1024]{1,0:T(8,128)S(1)} %copy-done), custom_call_target="tpu_custom_call" | custom-call | flops 8388608 | bytes 1654784 | tf_op jit(solution)/shard_map/pallas_call | solution.py:345
  3.3 5.6 %collective-permute-start.4 = (f32[288,128]{1,0:T(8,128)S(1)}, f32[288,128]{1,0:T(8,128)S(1)}, u32[]{:S(2)}, u32[]{:S(2)}) collective-permute-start(f32[288,128]{1,0:T(8,128)S(1)} %get-tuple-element.20), channel_id=1, source_target_pairs={{48,0},{64,16},{80,32},{96,48},{112,64},{128,80},{144,96},{160,112... | collective-permute-start | bytes 442376 | tf_op jit(solution)/shard_map/ppermute | solution.py:358
  8.9 0.0 collective-permute-start.2
  8.9 0.2 collective-permute-start
  9.1 0.3 collective-permute-start.6
  9.4 0.0 copy-done.1
  9.4 0.4 shard_map.42
  9.8 2.5 %collective-permute-done.4.bottom2 = f32[288,128]{1,0:T(8,128)S(1)} collective-permute-done((f32[288,128]{1,0:T(8,128)S(1)}, f32[288,128]{1,0:T(8,128)S(1)}, u32[]{:S(2)}, u32[]{:S(2)}) %collective-permute-start.4) | collective-permute-done | bytes 147488 | tf_op jit(solution)/shard_map/ppermute | solution.py:358
  12.3 5.2 %collective-permute-done.2.top0 = f32[288,128]{1,0:T(8,128)S(1)} collective-permute-done((f32[288,128]{1,0:T(8,128)S(1)}, f32[288,128]{1,0:T(8,128)S(1)}, u32[]{:S(2)}, u32[]{:S(2)}) %collective-permute-start.2) | collective-permute-done | bytes 147488 | tf_op jit(solution)/shard_map/ppermute | solution.py:358
  17.5 0.0 collective-permute-start.3
  17.5 0.5 %collective-permute-start.5 = (f32[256,512]{1,0:T(8,128)S(1)}, f32[256,512]{1,0:T(8,128)S(1)}, u32[]{:S(2)}, u32[]{:S(2)}) collective-permute-start(f32[256,512]{1,0:T(8,128)S(1)} %get-tuple-element.21), channel_id=1, source_target_pairs={{16,0},{32,16},{48,32},{64,48},{80,64},{96,80},{112,96},{128,112},... | collective-permute-start | bytes 1572872 | tf_op jit(solution)/shard_map/ppermute | solution.py:358
  18.0 0.0 collective-permute-done.pair1
  18.0 0.8 %collective-permute-done.6.pair2 = f32[576,128]{1,0:T(8,128)S(1)} collective-permute-done((f32[576,128]{1,0:T(8,128)S(1)}, f32[576,128]{1,0:T(8,128)S(1)}, u32[]{:S(2)}, u32[]{:S(2)}) %collective-permute-start.6) | collective-permute-done | bytes 294944 | tf_op jit(solution)/shard_map/ppermute | solution.py:358
  18.8 4.6 %collective-permute-start.7 = (f32[128,512]{1,0:T(8,128)S(1)}, f32[128,512]{1,0:T(8,128)S(1)}, u32[]{:S(2)}, u32[]{:S(2)}) collective-permute-start(f32[128,512]{1,0:T(8,128)S(1)} %get-tuple-element.23), channel_id=1, source_target_pairs={{48,0},{64,16},{80,32},{96,48},{112,64},{128,80},{144,96},{160,112... | collective-permute-start | bytes 786440 | tf_op jit(solution)/shard_map/ppermute | solution.py:358
  23.3 0.0 collective-permute-start.1
  23.3 3.0 %shard_map.43 = f32[4,56,128]{2,1,0:T(8,128)S(1)} custom-call(f32[288,128]{1,0:T(8,128)S(1)} %collective-permute-done.2.top0, f32[576,128]{1,0:T(8,128)S(1)} %collective-permute-done.pair1, f32[576,128]{1,0:T(8,128)S(1)} %collective-permute-done.6.pair2, f32[288,128]{1,0:T(8,128)S(1)} %collective-permute-done.4.bottom2), custom_call_target="tpu_custom_call" | custom-call | flops 14155776 | bytes 999424 | tf_op jit(solution)/shard_map/pallas_call | solution.py:345
  26.3 7.3 %all_to_all.5.turns = f32[4,56,128]{2,1,0:T(8,128)S(1)} all-to-all(f32[4,56,128]{2,1,0:T(8,128)S(1)} %shard_map.43), channel_id=1, replica_groups={{0,4,8,12},{1,5,9,13},{2,6,10,14},{3,7,11,15},{16,20,24,28},{17,21,25,2..., dimensions={0} | all-to-all | bytes 229376 | tf_op jit(solution)/shard_map/all_to_all | solution.py:398
  33.7 1.2 %collective-permute-done.7.bottom2 = f32[128,512]{1,0:T(8,128)S(1)} collective-permute-done((f32[128,512]{1,0:T(8,128)S(1)}, f32[128,512]{1,0:T(8,128)S(1)}, u32[]{:S(2)}, u32[]{:S(2)}) %collective-permute-start.7) | collective-permute-done | bytes 262176 | tf_op jit(solution)/shard_map/ppermute | solution.py:358
  34.9 2.7 %collective-permute-done.1.top0 = f32[128,512]{1,0:T(8,128)S(1)} collective-permute-done((f32[128,512]{1,0:T(8,128)S(1)}, f32[128,512]{1,0:T(8,128)S(1)}, u32[]{:S(2)}, u32[]{:S(2)}) %collective-permute-start.1) | collective-permute-done | bytes 262176 | tf_op jit(solution)/shard_map/ppermute | solution.py:358
  37.6 0.0 collective-permute-done.3.pair1
  37.6 0.0 collective-permute-done.5.pair2
  37.6 2.7 %shard_map.44 = (f32[1024]{0:T(1024)}, f32[128,1024]{1,0:T(8,128)}) custom-call(f32[128,512]{1,0:T(8,128)S(1)} %collective-permute-done.1.top0, f32[256,512]{1,0:T(8,128)S(1)} %collective-permute-done.3.pair1, f32[256,512]{1,0:T(8,128)S(1)} %collective-permute-done.5.pair2, f32[128,512]{1,0:T(8,128)S(1)} %collective-permute-done.7.bottom2, ...), custom_call_target="tpu_custom_call" | custom-call | flops 12582912 | bytes 2215936 | tf_op jit(solution)/shard_map/pallas_call | solution.py:345
Async XLA Ops:
  0.6 1.2 %copy-start = (f32[256,1024]{1,0:T(8,128)S(1)}, f32[256,1024]{1,0:T(8,128)}, u32[]{:S(2)}) copy-start(f32[256,1024]{1,0:T(8,128)} %root_ref.1) | copy-start | bytes 3145732
  1.9 7.6 %copy-start.1 = (bf16[128,1024]{1,0:T(8,128)(2,1)S(1)}, bf16[128,1024]{1,0:T(8,128)(2,1)}, u32[]{:S(2)}) copy-start(bf16[128,1024]{1,0:T(8,128)(2,1)} %grad_ref.1) | copy-start | bytes 786436
  3.3 8.9 %collective-permute-start.4 = (f32[288,128]{1,0:T(8,128)S(1)}, f32[288,128]{1,0:T(8,128)S(1)}, u32[]{:S(2)}, u32[]{:S(2)}) collective-permute-start(f32[288,128]{1,0:T(8,128)S(1)} %get-tuple-element.20), channel_id=1, source_target_pairs={{48,0},{64,16},{80,32},{96,48},{112,64},{128,80},{144,96},{160,112... | collective-permute-start | bytes 442376 | tf_op jit(solution)/shard_map/ppermute | solution.py:358
  8.9 8.6 %collective-permute-start.2 = (f32[288,128]{1,0:T(8,128)S(1)}, f32[288,128]{1,0:T(8,128)S(1)}, u32[]{:S(2)}, u32[]{:S(2)}) collective-permute-start(f32[288,128]{1,0:T(8,128)S(1)} %get-tuple-element.18), channel_id=1, source_target_pairs={{208,0},{224,16},{240,32},{0,48},{16,64},{32,80},{48,96},{64,112},... | collective-permute-start | bytes 442376 | tf_op jit(solution)/shard_map/ppermute | solution.py:358
  8.9 9.1 %collective-permute-start = (f32[576,128]{1,0:T(8,128)S(1)}, f32[576,128]{1,0:T(8,128)S(1)}, u32[]{:S(2)}, u32[]{:S(2)}) collective-permute-start(f32[576,128]{1,0:T(8,128)S(1)} %get-tuple-element.15), channel_id=1, source_target_pairs={{240,0},{0,16},{16,32},{32,48},{48,64},{64,80},{80,96},{96,112},{1... | collective-permute-start | bytes 884744 | tf_op jit(solution)/shard_map/ppermute | solution.py:358
  9.1 9.7 %collective-permute-start.6 = (f32[576,128]{1,0:T(8,128)S(1)}, f32[576,128]{1,0:T(8,128)S(1)}, u32[]{:S(2)}, u32[]{:S(2)}) collective-permute-start(f32[576,128]{1,0:T(8,128)S(1)} %get-tuple-element.15), channel_id=1, source_target_pairs={{16,0},{32,16},{48,32},{64,48},{80,64},{96,80},{112,96},{128,112},... | collective-permute-start | bytes 884744 | tf_op jit(solution)/shard_map/ppermute | solution.py:358
  17.5 20.1 %collective-permute-start.3 = (f32[256,512]{1,0:T(8,128)S(1)}, f32[256,512]{1,0:T(8,128)S(1)}, u32[]{:S(2)}, u32[]{:S(2)}) collective-permute-start(f32[256,512]{1,0:T(8,128)S(1)} %get-tuple-element.21), channel_id=1, source_target_pairs={{240,0},{0,16},{16,32},{32,48},{48,64},{64,80},{80,96},{96,112},{1... | collective-permute-start | bytes 1572872 | tf_op jit(solution)/shard_map/ppermute | solution.py:358
  17.5 20.1 %collective-permute-start.5 = (f32[256,512]{1,0:T(8,128)S(1)}, f32[256,512]{1,0:T(8,128)S(1)}, u32[]{:S(2)}, u32[]{:S(2)}) collective-permute-start(f32[256,512]{1,0:T(8,128)S(1)} %get-tuple-element.21), channel_id=1, source_target_pairs={{16,0},{32,16},{48,32},{64,48},{80,64},{96,80},{112,96},{128,112},... | collective-permute-start | bytes 1572872 | tf_op jit(solution)/shard_map/ppermute | solution.py:358
  18.8 16.1 %collective-permute-start.7 = (f32[128,512]{1,0:T(8,128)S(1)}, f32[128,512]{1,0:T(8,128)S(1)}, u32[]{:S(2)}, u32[]{:S(2)}) collective-permute-start(f32[128,512]{1,0:T(8,128)S(1)} %get-tuple-element.23), channel_id=1, source_target_pairs={{48,0},{64,16},{80,32},{96,48},{112,64},{128,80},{144,96},{160,112... | collective-permute-start | bytes 786440 | tf_op jit(solution)/shard_map/ppermute | solution.py:358
  23.3 14.2 %collective-permute-start.1 = (f32[128,512]{1,0:T(8,128)S(1)}, f32[128,512]{1,0:T(8,128)S(1)}, u32[]{:S(2)}, u32[]{:S(2)}) collective-permute-start(f32[128,512]{1,0:T(8,128)S(1)} %get-tuple-element.16), channel_id=1, source_target_pairs={{208,0},{224,16},{240,32},{0,48},{16,64},{32,80},{48,96},{64,112},... | collective-permute-start | bytes 786440 | tf_op jit(solution)/shard_map/ppermute | solution.py:358

commit v4 on v3

--- a/solution.py
+++ b/solution.py
@@ -55,7 +55,11 @@
     return jnp.broadcast_to(row, (8, LANES))
 
 
-def first_kernel(root_ref, top_out, both_out, bottom_out, turn_out, top, bottom, rolled):
+def even_slot():
+    return lax.axis_index("blk") % 2 == 0
+
+
+def first_kernel(root_ref, back_out, both_out, ahead_out, turn_out, top, bottom, rolled):
     tiles = [pl.ds(8 * i, 8) for i in range(ROOT_ROWS // 8)]
     cols = [pl.ds(g * LANES, LANES) for g in range(PARTS)]
     low_cols = [pl.ds(WIDTH + g * LANES, LANES) for g in range(PARTS)]
@@ -110,22 +114,20 @@
             out = jnp.where(lane_group == g, pltpu.roll(piece, g * HALO, 1), out)
         return out
 
-    t = top[:, here]
-    b = bottom[:, here]
-    top_out[pl.ds(0, ROOT_ROWS), :] = t
-    both_out[pl.ds(0, ROOT_ROWS), :] = t
-    bottom_out[pl.ds(0, ROOT_ROWS), :] = b
-    both_out[pl.ds(CHUNK_ROWS, ROOT_ROWS), :] = b
-    for q in range(HALO_ROWS // 8):
-        t = folded(top, q)
-        b = folded(bottom, q)
-        top_out[pl.ds(ROOT_ROWS + 8 * q, 8), :] = t
-        both_out[pl.ds(ROOT_ROWS + 8 * q, 8), :] = t
-        bottom_out[pl.ds(ROOT_ROWS + 8 * q, 8), :] = b
-        both_out[pl.ds(CHUNK_ROWS + ROOT_ROWS + 8 * q, 8), :] = b
-
-
-def gradient_first_kernel(grad_ref, turn_ref, top_out, both_out, bottom_out):
+    even = even_slot()
+    for v in range(CHUNK_ROWS // 8):
+        if v < ROOT_ROWS // 8:
+            t, b = top[pl.ds(8 * v, 8), here], bottom[pl.ds(8 * v, 8), here]
+        else:
+            t, b = (folded(block, v - ROOT_ROWS // 8) for block in (top, bottom))
+        both_out[pl.ds(8 * v, 8), :] = t
+        both_out[pl.ds(CHUNK_ROWS + 8 * v, 8), :] = b
+        back_out[pl.ds(8 * v, 8), :] = jnp.where(even, b, t)
+        ahead_out[pl.ds(8 * v, 8), :] = jnp.where(even, t, b)
+
+
+def gradient_first_kernel(grad_ref, turn_ref, back_out, both_out, ahead_out):
+    even = even_slot()
     rows_all = grad_ref.shape[0]
     tiles = [pl.ds(8 * i, 8) for i in range(rows_all // 8)]
     for step in range(SWEEPS):
@@ -139,43 +141,52 @@
                 half = pair[:8] if i % 2 == 0 else pair[8:]
                 t, b = half[:, :WIDTH], half[:, WIDTH:]
             else:
-                t, b = top_out[rows, :], bottom_out[rows, :]
+                t, b = both_out[rows, :], both_out[low, :]
             t, b = c * t + s * b, c * b - s * t
             b = pltpu.roll(b, WIDTH - 1, 1)
-            top_out[rows, :] = t
-            bottom_out[rows, :] = b
+            both_out[rows, :] = t
+            both_out[low, :] = b
             if step == SWEEPS - 1:
-                both_out[rows, :] = t
-                both_out[low, :] = b
-
-
-def cone_kernel(top0, pair1, pair2, bottom2, turn_out, blocks):
+                back_out[rows, :] = jnp.where(even, b, t)
+                ahead_out[rows, :] = jnp.where(even, t, b)
+
+
+def cone_kernel(back, pair_out, pair_in, ahead, turn_out, blocks):
     count = ROOT_ROWS // 8
     per_group = HALO_ROWS // 8
     lane = lax.broadcasted_iota(jnp.int32, (8, LANES), 1)
     lane_group = lane // HALO
-    homes = ((top0, 0), (pair1, 0), (pair2, 0), (pair1, CHUNK_ROWS), (pair2, CHUNK_ROWS), (bottom2, 0))
+    even = even_slot()
+    homes = (
+        (back, ahead, 0),
+        (pair_out, pair_in, 0),
+        (pair_in, pair_out, 0),
+        (pair_out, pair_in, CHUNK_ROWS),
+        (pair_in, pair_out, CHUNK_ROWS),
+        (ahead, back, 0),
+    )
+
+    def home(index, row):
+        on_even, on_odd, first = homes[index]
+        rows = pl.ds(first + row, 8)
+        return jnp.where(even, on_even[rows, :], on_odd[rows, :])
 
     def unfolded(places, i):
         g, q = divmod(i, per_group)
         out = None
-        for p, (ref, first) in enumerate(places):
-            piece = ref[pl.ds(first + ROOT_ROWS + 8 * q, 8), :]
+        for p, index in enumerate(places):
+            piece = home(index, ROOT_ROWS + 8 * q)
             piece = pltpu.roll(piece, (p - g) * HALO % LANES, 1)
             out = piece if out is None else jnp.where(lane_group == p, piece, out)
         return out
 
     def given(index, i):
-        rows = pl.ds(8 * i, 8)
-        if index < 6:
-            ref, first = homes[index]
-            return ref[pl.ds(first + 8 * i, 8), :]
-        return blocks[index, rows, :]
+        return home(index, 8 * i) if index < 6 else blocks[index, pl.ds(8 * i, 8), :]
 
     for i in range(count):
         rows = pl.ds(8 * i, 8)
-        blocks[6, rows, :] = unfolded(homes[:3], i)
-        blocks[7, rows, :] = unfolded(homes[3:], i)
+        blocks[6, rows, :] = unfolded((0, 1, 2), i)
+        blocks[7, rows, :] = unfolded((3, 4, 5), i)
 
     def stored(index, i):
         return blocks[index, pl.ds(8 * i, 8), :]
@@ -282,22 +293,24 @@
         turn_out[copy] = turn_out[0]
 
 
-def last_kernel(top0, pair1, pair2, bottom2, turns, eigen_out, projected_out, wide, blocks):
-    rows_all = top0.shape[0]
+def last_kernel(back, pair_out, pair_in, ahead, turns, eigen_out, projected_out, wide, blocks):
+    rows_all = back.shape[0]
+    even = even_slot()
     count = rows_all // 8
     for part in range(PARTS):
         wide[:, pl.ds(part * LANES, LANES)] = turns[part]
 
     def given(index, i):
-        rows, low = pl.ds(8 * i, 8), pl.ds(rows_all + 8 * i, 8)
-        return (
-            lambda: top0[rows, :],
-            lambda: pair1[rows, :],
-            lambda: pair2[rows, :],
-            lambda: pair1[low, :],
-            lambda: pair2[low, :],
-            lambda: bottom2[rows, :],
-        )[index]()
+        on_even, on_odd, first = (
+            (back, ahead, 0),
+            (pair_out, pair_in, 0),
+            (pair_in, pair_out, 0),
+            (pair_out, pair_in, rows_all),
+            (pair_in, pair_out, rows_all),
+            (ahead, back, 0),
+        )[index]
+        rows = pl.ds(first + 8 * i, 8)
+        return jnp.where(even, on_even[rows, :], on_odd[rows, :])
 
     def row_of(row):
         return jnp.broadcast_to(wide[pl.ds(row, 1), :], (8, WIDTH))
@@ -353,25 +366,27 @@
     )(*args)
 
 
-def from_slot(shard, offset):
+def swapped(shard, by):
     length = lax.axis_size("blk")
-    return lax.ppermute(shard, "blk", [((i + offset) % length, i) for i in range(length)])
+    return lax.ppermute(
+        shard, "blk", [((i + (by if i % 2 == 0 else -by)) % length, i) for i in range(length)]
+    )
 
 
 def body(root_rows, gradient):
     rows = gradient.shape[0]
-    top_root, both_root, bottom_root, turn0 = call(
+    back_root, both_root, ahead_root, turn0 = call(
         first_kernel,
         [(CHUNK_ROWS, LANES), (2 * CHUNK_ROWS, LANES), (CHUNK_ROWS, LANES), (2 * SWEEPS, WIDTH)],
         [(ROOT_ROWS, WIDTH)] * 3,
         [root_rows],
         16 * ROOT_ROWS * WIDTH * SWEEPS,
     )
-    root3 = from_slot(bottom_root, 3)
-    root0 = from_slot(top_root, -3)
-    root1 = from_slot(both_root, -1)
-    root2 = from_slot(both_root, 1)
-    top_grad, both_grad, bottom_grad = call(
+    root3 = swapped(ahead_root, 3)
+    root0 = swapped(back_root, -3)
+    root1 = swapped(both_root, -1)
+    root2 = swapped(both_root, 1)
+    back_grad, both_grad, ahead_grad = call(
         gradient_first_kernel,
         [(rows, WIDTH), (2 * rows, WIDTH), (rows, WIDTH)],
         [],
@@ -381,10 +396,10 @@
     def after(value, *others):
         return lax.optimization_barrier((value, *others))[0]
 
-    grad1 = from_slot(after(both_grad, root0), -1)
-    grad2 = from_slot(after(both_grad, root3), 1)
-    grad0 = from_slot(after(top_grad, root1), -3)
-    grad3 = from_slot(after(bottom_grad, root2), 3)
+    grad1 = swapped(after(both_grad, root0), -1)
+    grad2 = swapped(after(both_grad, root3), 1)
+    grad0 = swapped(after(back_grad, root1), -3)
+    grad3 = swapped(after(ahead_grad, root2), 3)
     (turns,) = call(
         cone_kernel,
         [(PARTS, ANGLE_ROWS, LANES)],

time: 40.4 us -> 37.8 us (0.936)
  waiting for transfers between devices: 12.4 us -> 5.33 us
  starting transfers between devices: 11.1 us -> 14.4 us
  blocking collectives: 7.35 us -> 8.56 us
    ppermute x8, waiting for transfers between devices: 12.4 us -> 5.33 us  [swapped(): lax.ppermute(shard, 'blk', [((i + (by if i % 2 == 0 else -by)) % length,...]
    ppermute x8, starting transfers between devices: 11.1 us -> 14.4 us  [swapped(): lax.ppermute(shard, 'blk', [((i + (by if i % 2 == 0 else -by)) % length,...]
    all_to_all x1, blocking collectives: 7.35 us -> 8.56 us  [body(): turns = lax.all_to_all(turns, 'rep', 0, 0, axis_index_groups=groups)]
  transfers between devices with their start and end apart: 8 -> 8, of which waited for: 5 -> 3; matrix products, arithmetic and copies ran while one was open for 0% -> 0% of each run, Pallas kernels for 8% -> 9%
where the time goes in v4:
time: 37.8 us; the launch traced here: 37.7 us
  starting transfers between devices  14.4 us (38%)
  blocking collectives  8.56 us (23%)
  Pallas kernels  7.56 us (20%)
  waiting for transfers between devices  5.33 us (14%)
  local copies, waits for them, and re-layouts  1.22 us (3%)
  between operations  0.66 us (2%)
    ppermute x8, starting transfers between devices, swapped(): lax.ppermute(shard, 'blk', [((i + (by if i % 2 == 0 else -by)) % length,...  14.4 us
    all_to_all x1, blocking collectives, body(): turns = lax.all_to_all(turns, 'rep', 0, 0, axis_index_groups=groups)  8.56 us
    pallas_call x4, Pallas kernels, call(): pl.pallas_call(kernel, out_shape=shapes, in_specs=[vmem] * len(args), out...  7.56 us
    ppermute x8, waiting for transfers between devices, swapped(): lax.ppermute(shard, 'blk', [((i + (by if i % 2 == 0 else -by)) % length,...  5.33 us
    unnamed x4, local copies, waits for them, and re-layouts  1.22 us
  transfers between devices with their start and end apart: 8, of which 3 were waited for; matrix products, arithmetic and copies ran while one was open for 0% of the time, Pallas kernels for 9%

profile of v4, /device:TPU:1, one launch (start us, length us, event | category | flops | bytes accessed | tf_op | source)
XLA Modules:
  0.0 37.7 jit_solution(14996936213662365859)
XLA Ops:
  0.6 0.0 copy-start
  0.6 1.2 %copy-done = f32[256,1024]{1,0:T(8,128)S(1)} copy-done((f32[256,1024]{1,0:T(8,128)S(1)}, f32[256,1024]{1,0:T(8,128)}, u32[]{:S(2)}) %copy-start) | copy-done | bytes 1048600
  1.9 0.0 copy-start.1
  1.9 1.5 %shard_map.41 = (f32[288,128]{1,0:T(8,128)S(1)}, f32[576,128]{1,0:T(8,128)S(1)}, f32[288,128]{1,0:T(8,128)S(1)}, f32[8,512]{1,0:T(8,128)S(1)}) custom-call(f32[256,1024]{1,0:T(8,128)S(1)} %copy-done), custom_call_target="tpu_custom_call" | custom-call | flops 8388608 | bytes 1654784 | tf_op jit(solution)/shard_map/pallas_call | solution.py:358
  3.3 5.6 %collective-permute-start.4 = (f32[288,128]{1,0:T(8,128)S(1)}, f32[288,128]{1,0:T(8,128)S(1)}, u32[]{:S(2)}, u32[]{:S(2)}) collective-permute-start(f32[288,128]{1,0:T(8,128)S(1)} %get-tuple-element.20), channel_id=1, source_target_pairs={{48,0},{224,16},{80,32},{0,48},{112,64},{32,80},{144,96},{64,112},... | collective-permute-start | bytes 442376 | tf_op jit(solution)/shard_map/ppermute | solution.py:371
  8.9 0.0 collective-permute-start.2
  8.9 0.4 %collective-permute-start = (f32[576,128]{1,0:T(8,128)S(1)}, f32[576,128]{1,0:T(8,128)S(1)}, u32[]{:S(2)}, u32[]{:S(2)}) collective-permute-start(f32[576,128]{1,0:T(8,128)S(1)} %get-tuple-element.15), channel_id=1, source_target_pairs={{240,0},{32,16},{16,32},{64,48},{48,64},{96,80},{80,96},{128,112},... | collective-permute-start | bytes 884744 | tf_op jit(solution)/shard_map/ppermute | solution.py:371
  9.3 0.5 %collective-permute-start.6 = (f32[576,128]{1,0:T(8,128)S(1)}, f32[576,128]{1,0:T(8,128)S(1)}, u32[]{:S(2)}, u32[]{:S(2)}) collective-permute-start(f32[576,128]{1,0:T(8,128)S(1)} %get-tuple-element.15), channel_id=1, source_target_pairs={{16,0},{0,16},{48,32},{32,48},{80,64},{64,80},{112,96},{96,112},{1... | collective-permute-start | bytes 884744 | tf_op jit(solution)/shard_map/ppermute | solution.py:371
  9.8 0.0 copy-done.1
  9.8 0.4 shard_map.42
  10.2 2.8 %collective-permute-done.4.ahead = f32[288,128]{1,0:T(8,128)S(1)} collective-permute-done((f32[288,128]{1,0:T(8,128)S(1)}, f32[288,128]{1,0:T(8,128)S(1)}, u32[]{:S(2)}, u32[]{:S(2)}) %collective-permute-start.4) | collective-permute-done | bytes 147488 | tf_op jit(solution)/shard_map/ppermute | solution.py:371
  12.9 0.7 %collective-permute-done.2.back = f32[288,128]{1,0:T(8,128)S(1)} collective-permute-done((f32[288,128]{1,0:T(8,128)S(1)}, f32[288,128]{1,0:T(8,128)S(1)}, u32[]{:S(2)}, u32[]{:S(2)}) %collective-permute-start.2) | collective-permute-done | bytes 147488 | tf_op jit(solution)/shard_map/ppermute | solution.py:371
  13.7 1.3 %collective-permute-start.3 = (f32[256,512]{1,0:T(8,128)S(1)}, f32[256,512]{1,0:T(8,128)S(1)}, u32[]{:S(2)}, u32[]{:S(2)}) collective-permute-start(f32[256,512]{1,0:T(8,128)S(1)} %get-tuple-element.21), channel_id=1, source_target_pairs={{240,0},{32,16},{16,32},{64,48},{48,64},{96,80},{80,96},{128,112},... | collective-permute-start | bytes 1572872 | tf_op jit(solution)/shard_map/ppermute | solution.py:371
  15.0 3.1 %collective-permute-start.5 = (f32[256,512]{1,0:T(8,128)S(1)}, f32[256,512]{1,0:T(8,128)S(1)}, u32[]{:S(2)}, u32[]{:S(2)}) collective-permute-start(f32[256,512]{1,0:T(8,128)S(1)} %get-tuple-element.21), channel_id=1, source_target_pairs={{16,0},{0,16},{48,32},{32,48},{80,64},{64,80},{112,96},{96,112},{1... | collective-permute-start | bytes 1572872 | tf_op jit(solution)/shard_map/ppermute | solution.py:371
  18.1 0.0 collective-permute-done.pair_out
  18.1 0.0 collective-permute-done.6.pair_in
  18.1 3.5 %collective-permute-start.7 = (f32[128,512]{1,0:T(8,128)S(1)}, f32[128,512]{1,0:T(8,128)S(1)}, u32[]{:S(2)}, u32[]{:S(2)}) collective-permute-start(f32[128,512]{1,0:T(8,128)S(1)} %get-tuple-element.23), channel_id=1, source_target_pairs={{48,0},{224,16},{80,32},{0,48},{112,64},{32,80},{144,96},{64,112},... | collective-permute-start | bytes 786440 | tf_op jit(solution)/shard_map/ppermute | solution.py:371
  21.6 0.0 collective-permute-start.1
  21.6 3.0 %shard_map.43 = f32[4,56,128]{2,1,0:T(8,128)S(1)} custom-call(f32[288,128]{1,0:T(8,128)S(1)} %collective-permute-done.2.back, f32[576,128]{1,0:T(8,128)S(1)} %collective-permute-done.pair_out, f32[576,128]{1,0:T(8,128)S(1)} %collective-permute-done.6.pair_in, f32[288,128]{1,0:T(8,128)S(1)} %collective-permute-done.4.ahead), custom_call_target="tpu_custom_call" | custom-call | flops 14155776 | bytes 999424 | tf_op jit(solution)/shard_map/pallas_call | solution.py:358
  24.6 8.6 %all_to_all.5.turns = f32[4,56,128]{2,1,0:T(8,128)S(1)} all-to-all(f32[4,56,128]{2,1,0:T(8,128)S(1)} %shard_map.43), channel_id=1, replica_groups={{0,4,8,12},{1,5,9,13},{2,6,10,14},{3,7,11,15},{16,20,24,28},{17,21,25,2..., dimensions={0} | all-to-all | bytes 229376 | tf_op jit(solution)/shard_map/all_to_all | solution.py:413
  33.1 1.8 %collective-permute-done.7.ahead = f32[128,512]{1,0:T(8,128)S(1)} collective-permute-done((f32[128,512]{1,0:T(8,128)S(1)}, f32[128,512]{1,0:T(8,128)S(1)}, u32[]{:S(2)}, u32[]{:S(2)}) %collective-permute-start.7) | collective-permute-done | bytes 262176 | tf_op jit(solution)/shard_map/ppermute | solution.py:371
  35.0 0.0 collective-permute-done.1.back
  35.0 0.0 collective-permute-done.3.pair_out
  35.0 0.0 collective-permute-done.5.pair_in
  35.0 2.7 %shard_map.44 = (f32[1024]{0:T(1024)}, f32[128,1024]{1,0:T(8,128)}) custom-call(f32[128,512]{1,0:T(8,128)S(1)} %collective-permute-done.1.back, f32[256,512]{1,0:T(8,128)S(1)} %collective-permute-done.3.pair_out, f32[256,512]{1,0:T(8,128)S(1)} %collective-permute-done.5.pair_in, f32[128,512]{1,0:T(8,128)S(1)} %collective-permute-done.7.ahead, ...), custom_call_target="tpu_custom_call" | custom-call | flops 12582912 | bytes 2215936 | tf_op jit(solution)/shard_map/pallas_call | solution.py:358
Async XLA Ops:
  0.6 1.2 %copy-start = (f32[256,1024]{1,0:T(8,128)S(1)}, f32[256,1024]{1,0:T(8,128)}, u32[]{:S(2)}) copy-start(f32[256,1024]{1,0:T(8,128)} %root_ref.1) | copy-start | bytes 3145732
  1.9 8.0 %copy-start.1 = (bf16[128,1024]{1,0:T(8,128)(2,1)S(1)}, bf16[128,1024]{1,0:T(8,128)(2,1)}, u32[]{:S(2)}) copy-start(bf16[128,1024]{1,0:T(8,128)(2,1)} %grad_ref.1) | copy-start | bytes 786436
  3.3 9.6 %collective-permute-start.4 = (f32[288,128]{1,0:T(8,128)S(1)}, f32[288,128]{1,0:T(8,128)S(1)}, u32[]{:S(2)}, u32[]{:S(2)}) collective-permute-start(f32[288,128]{1,0:T(8,128)S(1)} %get-tuple-element.20), channel_id=1, source_target_pairs={{48,0},{224,16},{80,32},{0,48},{112,64},{32,80},{144,96},{64,112},... | collective-permute-start | bytes 442376 | tf_op jit(solution)/shard_map/ppermute | solution.py:371
  8.9 4.7 %collective-permute-start.2 = (f32[288,128]{1,0:T(8,128)S(1)}, f32[288,128]{1,0:T(8,128)S(1)}, u32[]{:S(2)}, u32[]{:S(2)}) collective-permute-start(f32[288,128]{1,0:T(8,128)S(1)} %get-tuple-element.18), channel_id=1, source_target_pairs={{208,0},{64,16},{240,32},{96,48},{16,64},{128,80},{48,96},{160,112... | collective-permute-start | bytes 442376 | tf_op jit(solution)/shard_map/ppermute | solution.py:371
  8.9 9.2 %collective-permute-start = (f32[576,128]{1,0:T(8,128)S(1)}, f32[576,128]{1,0:T(8,128)S(1)}, u32[]{:S(2)}, u32[]{:S(2)}) collective-permute-start(f32[576,128]{1,0:T(8,128)S(1)} %get-tuple-element.15), channel_id=1, source_target_pairs={{240,0},{32,16},{16,32},{64,48},{48,64},{96,80},{80,96},{128,112},... | collective-permute-start | bytes 884744 | tf_op jit(solution)/shard_map/ppermute | solution.py:371
  9.3 8.8 %collective-permute-start.6 = (f32[576,128]{1,0:T(8,128)S(1)}, f32[576,128]{1,0:T(8,128)S(1)}, u32[]{:S(2)}, u32[]{:S(2)}) collective-permute-start(f32[576,128]{1,0:T(8,128)S(1)} %get-tuple-element.15), channel_id=1, source_target_pairs={{16,0},{0,16},{48,32},{32,48},{80,64},{64,80},{112,96},{96,112},{1... | collective-permute-start | bytes 884744 | tf_op jit(solution)/shard_map/ppermute | solution.py:371
  13.7 21.3 %collective-permute-start.3 = (f32[256,512]{1,0:T(8,128)S(1)}, f32[256,512]{1,0:T(8,128)S(1)}, u32[]{:S(2)}, u32[]{:S(2)}) collective-permute-start(f32[256,512]{1,0:T(8,128)S(1)} %get-tuple-element.21), channel_id=1, source_target_pairs={{240,0},{32,16},{16,32},{64,48},{48,64},{96,80},{80,96},{128,112},... | collective-permute-start | bytes 1572872 | tf_op jit(solution)/shard_map/ppermute | solution.py:371
  15.0 20.0 %collective-permute-start.5 = (f32[256,512]{1,0:T(8,128)S(1)}, f32[256,512]{1,0:T(8,128)S(1)}, u32[]{:S(2)}, u32[]{:S(2)}) collective-permute-start(f32[256,512]{1,0:T(8,128)S(1)} %get-tuple-element.21), channel_id=1, source_target_pairs={{16,0},{0,16},{48,32},{32,48},{80,64},{64,80},{112,96},{96,112},{1... | collective-permute-start | bytes 1572872 | tf_op jit(solution)/shard_map/ppermute | solution.py:371
  18.1 16.9 %collective-permute-start.7 = (f32[128,512]{1,0:T(8,128)S(1)}, f32[128,512]{1,0:T(8,128)S(1)}, u32[]{:S(2)}, u32[]{:S(2)}) collective-permute-start(f32[128,512]{1,0:T(8,128)S(1)} %get-tuple-element.23), channel_id=1, source_target_pairs={{48,0},{224,16},{80,32},{0,48},{112,64},{32,80},{144,96},{64,112},... | collective-permute-start | bytes 786440 | tf_op jit(solution)/shard_map/ppermute | solution.py:371
  21.6 13.4 %collective-permute-start.1 = (f32[128,512]{1,0:T(8,128)S(1)}, f32[128,512]{1,0:T(8,128)S(1)}, u32[]{:S(2)}, u32[]{:S(2)}) collective-permute-start(f32[128,512]{1,0:T(8,128)S(1)} %get-tuple-element.16), channel_id=1, source_target_pairs={{208,0},{64,16},{240,32},{96,48},{16,64},{128,80},{48,96},{160,112... | collective-permute-start | bytes 786440 | tf_op jit(solution)/shard_map/ppermute | solution.py:371

commit v5 on v4

--- a/solution.py
+++ b/solution.py
@@ -293,61 +293,110 @@
         turn_out[copy] = turn_out[0]
 
 
-def last_kernel(back, pair_out, pair_in, ahead, turns, eigen_out, projected_out, wide, blocks):
-    rows_all = back.shape[0]
-    even = even_slot()
-    count = rows_all // 8
+def widened(turns, wide):
     for part in range(PARTS):
         wide[:, pl.ds(part * LANES, LANES)] = turns[part]
 
-    def given(index, i):
-        on_even, on_odd, first = (
-            (back, ahead, 0),
-            (pair_out, pair_in, 0),
-            (pair_in, pair_out, 0),
-            (pair_out, pair_in, rows_all),
-            (pair_in, pair_out, rows_all),
-            (ahead, back, 0),
-        )[index]
-        rows = pl.ds(first + 8 * i, 8)
-        return jnp.where(even, on_even[rows, :], on_odd[rows, :])
-
-    def row_of(row):
-        return jnp.broadcast_to(wide[pl.ds(row, 1), :], (8, WIDTH))
-
-    fresh = set()
-    base = 0
-    for number, pairs in enumerate(ROUND_PAIRS):
-        final = number + 1 == len(ROUND_PAIRS)
-        for k in range(SWEEPS):
-            ends = k + 1 == SWEEPS
-            for p, (ti, bi) in enumerate(pairs):
-                c = row_of(base + p * SWEEPS + k)
-                s = row_of(STEPS + base + p * SWEEPS + k)
-                need_top = not ends or p + 1 < len(pairs) or final
-                need_bottom = not ends or p > 0 or final
-                for i in range(count):
-                    rows = pl.ds(8 * i, 8)
-                    t = blocks[ti, rows, :] if ti in fresh else given(ti, i)
-                    b = blocks[3 + bi, rows, :] if 3 + bi in fresh else given(3 + bi, i)
-                    if need_top:
-                        top = c * t + s * b
-                    if need_bottom:
-                        bottom = c * b - s * t
-                    if final and ends:
-                        bottom = pltpu.roll(bottom, 4 * SWEEPS - 1, 1)
-                        projected_out[rows, pl.ds(0, WIDTH)] = top * top
-                        projected_out[rows, pl.ds(WIDTH, WIDTH)] = bottom * bottom
-                        continue
-                    if need_top:
-                        blocks[ti, rows, :] = top
-                    if need_bottom:
-                        blocks[3 + bi, rows, :] = pltpu.roll(bottom, WIDTH - 1, 1)
-                fresh |= {ti, 3 + bi}
-        base += len(pairs) * SWEEPS
+
+def turned_pair(wide, row, source, target, count, finish):
+    for k in range(SWEEPS):
+        c = jnp.broadcast_to(wide[pl.ds(row + k, 1), :], (8, WIDTH))
+        s = jnp.broadcast_to(wide[pl.ds(STEPS + row + k, 1), :], (8, WIDTH))
+        for i in range(count):
+            rows = pl.ds(8 * i, 8)
+            t, b = source(i) if k == 0 else (target[0][rows, :], target[1][rows, :])
+            t, b = c * t + s * b, c * b - s * t
+            if k + 1 == SWEEPS:
+                finish(i, t, b)
+            else:
+                target[0][rows, :] = t
+                target[1][rows, :] = pltpu.roll(b, WIDTH - 1, 1)
+
+
+def row_of(pair_round, even_pair, odd_pair):
+    base = SWEEPS * sum(len(pairs) for pairs in ROUND_PAIRS[:pair_round])
+    return jnp.where(even_slot(), base + SWEEPS * even_pair, base + SWEEPS * odd_pair)
+
+
+def middle_kernel(back, pair_out, pair_in, turns, eigen_out, near_out, done_out, wide, t0, b0, t1, b1):
+    rows_all = back.shape[0]
+    count = rows_all // 8
+    even = even_slot()
+    widened(turns, wide)
+
+    def parts(i):
+        rows, low = pl.ds(8 * i, 8), pl.ds(rows_all + 8 * i, 8)
+        return rows, low
+
+    def outer(i):
+        rows, low = parts(i)
+        far = back[rows, :]
+        return jnp.where(even, far, pair_out[rows, :]), jnp.where(even, pair_out[low, :], far)
+
+    def inner(i):
+        rows, low = parts(i)
+        return (
+            jnp.where(even, pair_out[rows, :], pair_in[rows, :]),
+            jnp.where(even, pair_in[low, :], pair_out[low, :]),
+        )
+
+    def keep_outer(i, t, b):
+        t0[parts(i)[0], :] = jnp.where(even, t, pltpu.roll(b, WIDTH - 1, 1))
+
+    def keep_inner(i, t, b):
+        rows = parts(i)[0]
+        t1[rows, :] = t
+        b1[rows, :] = pltpu.roll(b, WIDTH - 1, 1)
+        near_out[rows, :] = jnp.where(even, t, b1[rows, :])
+
+    def second(i):
+        rows = parts(i)[0]
+        kept = t0[rows, :]
+        return jnp.where(even, kept, t1[rows, :]), jnp.where(even, b1[rows, :], kept)
+
+    def keep_second(i, t, b):
+        done_out[parts(i)[0], :] = jnp.where(even, t, pltpu.roll(b, WIDTH - 1, 1))
+
+    turned_pair(wide, row_of(0, 0, 2), outer, (t0, b0), count, keep_outer)
+    turned_pair(wide, row_of(0, 1, 1), inner, (t1, b1), count, keep_inner)
+    turned_pair(wide, row_of(1, 0, 1), second, (t1, b1), count, keep_second)
+
     eigen_out[pl.ds(0, WIDTH)] = wide[EIGEN_ROW, :]
     bottom = pltpu.roll(wide[pl.ds(EIGEN_ROW + 1, 1), :], 4 * SWEEPS, 1)
     eigen_out[pl.ds(WIDTH, WIDTH)] = bottom[0]
+
+
+def last_kernel(pair_in, ahead, near, done, turns, projected_out, wide, t0, b0):
+    rows_all = ahead.shape[0]
+    count = rows_all // 8
+    even = even_slot()
+    widened(turns, wide)
+
+    def first(i):
+        rows, low = pl.ds(8 * i, 8), pl.ds(rows_all + 8 * i, 8)
+        far = ahead[rows, :]
+        return jnp.where(even, pair_in[rows, :], far), jnp.where(even, far, pair_in[low, :])
+
+    def keep(i, t, b):
+        t0[pl.ds(8 * i, 8), :] = jnp.where(even, pltpu.roll(b, WIDTH - 1, 1), t)
+
+    def with_kept(other):
+        def source(i):
+            rows = pl.ds(8 * i, 8)
+            kept, held = t0[rows, :], other[rows, :]
+            return jnp.where(even, held, kept), jnp.where(even, kept, held)
+
+        return source
+
+    def write(i, t, b):
+        rows = pl.ds(8 * i, 8)
+        b = pltpu.roll(b, 4 * SWEEPS - 1, 1)
+        projected_out[rows, pl.ds(0, WIDTH)] = t * t
+        projected_out[rows, pl.ds(WIDTH, WIDTH)] = b * b
+
+    turned_pair(wide, row_of(0, 2, 0), first, (t0, b0), count, keep)
+    turned_pair(wide, row_of(1, 1, 0), with_kept(near), (t0, b0), count, keep)
+    turned_pair(wide, row_of(2, 0, 0), with_kept(done), (t0, b0), count, write)
 
 
 def call(kernel, outs, scratch, args, flops):
@@ -411,12 +460,20 @@
     near = reps // PARTS
     groups = [[x * near + z for x in range(PARTS)] for z in range(near)]
     turns = lax.all_to_all(turns, "rep", 0, 0, axis_index_groups=groups)
-    eigen, projected = call(
+    block, angles = (rows, WIDTH), (ANGLE_ROWS, WIDTH)
+    eigen, near_block, done_block = call(
+        middle_kernel,
+        [(2 * WIDTH,), block, block],
+        [angles] + [block] * 4,
+        [grad0, grad1, grad2, turns],
+        4 * rows * WIDTH * STEPS,
+    )
+    (projected,) = call(
         last_kernel,
-        [(2 * WIDTH,), (rows, 2 * WIDTH)],
-        [(ANGLE_ROWS, WIDTH), (6, rows, WIDTH)],
-        [grad0, grad1, grad2, grad3, turns],
-        8 * rows * WIDTH * STEPS,
+        [(rows, 2 * WIDTH)],
+        [angles] + [block] * 2,
+        [grad2, grad3, near_block, done_block, turns],
+        4 * rows * WIDTH * STEPS,
     )
     return eigen, projected
 

time: 37.8 us -> 37.4 us (0.989)
  waiting for transfers between devices: 5.33 us -> 3.5 us
  Pallas kernels: 7.56 us -> 8.17 us
  starting transfers between devices: 14.4 us -> 14.9 us
    ppermute x8, waiting for transfers between devices: 5.33 us -> 3.5 us  [swapped(): lax.ppermute(shard, 'blk', [((i + (by if i % 2 == 0 else -by)) % length,...]
    pallas_call x4 -> x5, Pallas kernels: 7.56 us -> 8.17 us  [call(): pl.pallas_call(kernel, out_shape=shapes, in_specs=[vmem] * len(args), out...]
    ppermute x8, starting transfers between devices: 14.4 us -> 14.9 us  [swapped(): lax.ppermute(shard, 'blk', [((i + (by if i % 2 == 0 else -by)) % length,...]
  transfers between devices with their start and end apart: 8 -> 8, of which waited for: 3 -> 2; matrix products, arithmetic and copies ran while one was open for 0% -> 0% of each run, Pallas kernels for 9% -> 13%
where the time goes in v5:
time: 37.4 us; the launch traced here: 37.3 us
  starting transfers between devices  14.9 us (40%)
  blocking collectives  8.78 us (23%)
  Pallas kernels  8.17 us (22%)
  waiting for transfers between devices  3.5 us (9%)
  local copies, waits for them, and re-layouts  1.22 us (3%)
  between operations  0.67 us (2%)
    ppermute x8, starting transfers between devices, swapped(): lax.ppermute(shard, 'blk', [((i + (by if i % 2 == 0 else -by)) % length,...  14.9 us
    all_to_all x1, blocking collectives, body(): turns = lax.all_to_all(turns, 'rep', 0, 0, axis_index_groups=groups)  8.78 us
    pallas_call x5, Pallas kernels, call(): pl.pallas_call(kernel, out_shape=shapes, in_specs=[vmem] * len(args), out...  8.17 us
    ppermute x8, waiting for transfers between devices, swapped(): lax.ppermute(shard, 'blk', [((i + (by if i % 2 == 0 else -by)) % length,...  3.5 us
    unnamed x4, local copies, waits for them, and re-layouts  1.22 us
  transfers between devices with their start and end apart: 8, of which 2 were waited for; matrix products, arithmetic and copies ran while one was open for 0% of the time, Pallas kernels for 13%

profile of v5, /device:TPU:1, one launch (start us, length us, event | category | flops | bytes accessed | tf_op | source)
XLA Modules:
  0.0 37.3 jit_solution(10560659446663538172)
XLA Ops:
  0.6 0.0 copy-start
  0.6 1.2 %copy-done = f32[256,1024]{1,0:T(8,128)S(1)} copy-done((f32[256,1024]{1,0:T(8,128)S(1)}, f32[256,1024]{1,0:T(8,128)}, u32[]{:S(2)}) %copy-start) | copy-done | bytes 1048600
  1.9 0.0 copy-start.1
  1.9 1.5 %shard_map.41 = (f32[288,128]{1,0:T(8,128)S(1)}, f32[576,128]{1,0:T(8,128)S(1)}, f32[288,128]{1,0:T(8,128)S(1)}, f32[8,512]{1,0:T(8,128)S(1)}) custom-call(f32[256,1024]{1,0:T(8,128)S(1)} %copy-done), custom_call_target="tpu_custom_call" | custom-call | flops 8388608 | bytes 1654784 | tf_op jit(solution)/shard_map/pallas_call | solution.py:407
  3.3 5.6 %collective-permute-start.4 = (f32[288,128]{1,0:T(8,128)S(1)}, f32[288,128]{1,0:T(8,128)S(1)}, u32[]{:S(2)}, u32[]{:S(2)}) collective-permute-start(f32[288,128]{1,0:T(8,128)S(1)} %get-tuple-element.23), channel_id=1, source_target_pairs={{48,0},{224,16},{80,32},{0,48},{112,64},{32,80},{144,96},{64,112},... | collective-permute-start | bytes 442376 | tf_op jit(solution)/shard_map/ppermute | solution.py:420
  8.9 0.0 collective-permute-start.2
  8.9 0.4 %collective-permute-start = (f32[576,128]{1,0:T(8,128)S(1)}, f32[576,128]{1,0:T(8,128)S(1)}, u32[]{:S(2)}, u32[]{:S(2)}) collective-permute-start(f32[576,128]{1,0:T(8,128)S(1)} %get-tuple-element.18), channel_id=1, source_target_pairs={{240,0},{32,16},{16,32},{64,48},{48,64},{96,80},{80,96},{128,112},... | collective-permute-start | bytes 884744 | tf_op jit(solution)/shard_map/ppermute | solution.py:420
  9.3 0.5 %collective-permute-start.6 = (f32[576,128]{1,0:T(8,128)S(1)}, f32[576,128]{1,0:T(8,128)S(1)}, u32[]{:S(2)}, u32[]{:S(2)}) collective-permute-start(f32[576,128]{1,0:T(8,128)S(1)} %get-tuple-element.18), channel_id=1, source_target_pairs={{16,0},{0,16},{48,32},{32,48},{80,64},{64,80},{112,96},{96,112},{1... | collective-permute-start | bytes 884744 | tf_op jit(solution)/shard_map/ppermute | solution.py:420
  9.8 0.0 copy-done.1
  9.8 0.4 shard_map.42
  10.2 2.8 %collective-permute-done.4.ahead = f32[288,128]{1,0:T(8,128)S(1)} collective-permute-done((f32[288,128]{1,0:T(8,128)S(1)}, f32[288,128]{1,0:T(8,128)S(1)}, u32[]{:S(2)}, u32[]{:S(2)}) %collective-permute-start.4) | collective-permute-done | bytes 147488 | tf_op jit(solution)/shard_map/ppermute | solution.py:420
  12.9 0.7 %collective-permute-done.2.back = f32[288,128]{1,0:T(8,128)S(1)} collective-permute-done((f32[288,128]{1,0:T(8,128)S(1)}, f32[288,128]{1,0:T(8,128)S(1)}, u32[]{:S(2)}, u32[]{:S(2)}) %collective-permute-start.2) | collective-permute-done | bytes 147488 | tf_op jit(solution)/shard_map/ppermute | solution.py:420
  13.7 1.3 %collective-permute-start.3 = (f32[256,512]{1,0:T(8,128)S(1)}, f32[256,512]{1,0:T(8,128)S(1)}, u32[]{:S(2)}, u32[]{:S(2)}) collective-permute-start(f32[256,512]{1,0:T(8,128)S(1)} %get-tuple-element.24), channel_id=1, source_target_pairs={{240,0},{32,16},{16,32},{64,48},{48,64},{96,80},{80,96},{128,112},... | collective-permute-start | bytes 1572872 | tf_op jit(solution)/shard_map/ppermute | solution.py:420
  15.0 3.1 %collective-permute-start.5 = (f32[256,512]{1,0:T(8,128)S(1)}, f32[256,512]{1,0:T(8,128)S(1)}, u32[]{:S(2)}, u32[]{:S(2)}) collective-permute-start(f32[256,512]{1,0:T(8,128)S(1)} %get-tuple-element.24), channel_id=1, source_target_pairs={{16,0},{0,16},{48,32},{32,48},{80,64},{64,80},{112,96},{96,112},{1... | collective-permute-start | bytes 1572872 | tf_op jit(solution)/shard_map/ppermute | solution.py:420
  18.1 0.0 collective-permute-done.pair_out
  18.1 2.8 %collective-permute-start.1 = (f32[128,512]{1,0:T(8,128)S(1)}, f32[128,512]{1,0:T(8,128)S(1)}, u32[]{:S(2)}, u32[]{:S(2)}) collective-permute-start(f32[128,512]{1,0:T(8,128)S(1)} %get-tuple-element.19), channel_id=1, source_target_pairs={{208,0},{64,16},{240,32},{96,48},{16,64},{128,80},{48,96},{160,112... | collective-permute-start | bytes 786440 | tf_op jit(solution)/shard_map/ppermute | solution.py:420
  20.8 0.0 collective-permute-done.6.pair_in
  20.8 1.3 %collective-permute-start.7 = (f32[128,512]{1,0:T(8,128)S(1)}, f32[128,512]{1,0:T(8,128)S(1)}, u32[]{:S(2)}, u32[]{:S(2)}) collective-permute-start(f32[128,512]{1,0:T(8,128)S(1)} %get-tuple-element.27), channel_id=1, source_target_pairs={{48,0},{224,16},{80,32},{0,48},{112,64},{32,80},{144,96},{64,112},... | collective-permute-start | bytes 786440 | tf_op jit(solution)/shard_map/ppermute | solution.py:420
  22.1 3.0 %shard_map.43 = f32[4,56,128]{2,1,0:T(8,128)S(1)} custom-call(f32[288,128]{1,0:T(8,128)S(1)} %collective-permute-done.2.back, f32[576,128]{1,0:T(8,128)S(1)} %collective-permute-done.pair_out, f32[576,128]{1,0:T(8,128)S(1)} %collective-permute-done.6.pair_in, f32[288,128]{1,0:T(8,128)S(1)} %collective-permute-done.4.ahead), custom_call_target="tpu_custom_call" | custom-call | flops 14155776 | bytes 999424 | tf_op jit(solution)/shard_map/pallas_call | solution.py:407
  25.1 8.8 %all_to_all.5.turns = f32[4,56,128]{2,1,0:T(8,128)S(1)} all-to-all(f32[4,56,128]{2,1,0:T(8,128)S(1)} %shard_map.43), channel_id=1, replica_groups={{0,4,8,12},{1,5,9,13},{2,6,10,14},{3,7,11,15},{16,20,24,28},{17,21,25,2..., dimensions={0} | all-to-all | bytes 229376 | tf_op jit(solution)/shard_map/all_to_all | solution.py:462
  33.9 0.0 collective-permute-done.1.back
  33.9 0.0 collective-permute-done.3.pair_out
  33.9 0.0 collective-permute-done.5.pair_in
  33.9 1.6 %shard_map.44 = (f32[1024]{0:T(1024)}, f32[128,512]{1,0:T(8,128)S(1)}, f32[128,512]{1,0:T(8,128)S(1)}) custom-call(f32[128,512]{1,0:T(8,128)S(1)} %collective-permute-done.1.back, f32[256,512]{1,0:T(8,128)S(1)} %collective-permute-done.3.pair_out, f32[256,512]{1,0:T(8,128)S(1)} %collective-permute-done.5.pair_in, f32[4,56,128]{2,1,0:T(8,128)S(1)} %all_to_all.5.turns), custom_call_target="tpu_custom_call" | custom-call | flops 6291456 | bytes 1953792 | tf_op jit(solution)/shard_map/pallas_call | solution.py:407
  35.5 0.0 collective-permute-done.7.ahead
  35.5 1.8 %shard_map.45 = f32[128,1024]{1,0:T(8,128)} custom-call(f32[256,512]{1,0:T(8,128)S(1)} %collective-permute-done.5.pair_in, f32[128,512]{1,0:T(8,128)S(1)} %collective-permute-done.7.ahead, f32[128,512]{1,0:T(8,128)S(1)} %get-tuple-element.28.near, f32[128,512]{1,0:T(8,128)S(1)} %get-tuple-element.29.done, f32[4,56,128]{2,1,0:T(8,128)S(1)} %all_to_all.5.turns), custom_call_target="tpu_custom_call" | custom-call | flops 6291456 | bytes 1949696 | tf_op jit(solution)/shard_map/pallas_call | solution.py:407
Async XLA Ops:
  0.6 1.2 %copy-start = (f32[256,1024]{1,0:T(8,128)S(1)}, f32[256,1024]{1,0:T(8,128)}, u32[]{:S(2)}) copy-start(f32[256,1024]{1,0:T(8,128)} %root_ref.1) | copy-start | bytes 3145732
  1.9 8.0 %copy-start.1 = (bf16[128,1024]{1,0:T(8,128)(2,1)S(1)}, bf16[128,1024]{1,0:T(8,128)(2,1)}, u32[]{:S(2)}) copy-start(bf16[128,1024]{1,0:T(8,128)(2,1)} %grad_ref.1) | copy-start | bytes 786436
  3.3 9.6 %collective-permute-start.4 = (f32[288,128]{1,0:T(8,128)S(1)}, f32[288,128]{1,0:T(8,128)S(1)}, u32[]{:S(2)}, u32[]{:S(2)}) collective-permute-start(f32[288,128]{1,0:T(8,128)S(1)} %get-tuple-element.23), channel_id=1, source_target_pairs={{48,0},{224,16},{80,32},{0,48},{112,64},{32,80},{144,96},{64,112},... | collective-permute-start | bytes 442376 | tf_op jit(solution)/shard_map/ppermute | solution.py:420
  8.9 4.7 %collective-permute-start.2 = (f32[288,128]{1,0:T(8,128)S(1)}, f32[288,128]{1,0:T(8,128)S(1)}, u32[]{:S(2)}, u32[]{:S(2)}) collective-permute-start(f32[288,128]{1,0:T(8,128)S(1)} %get-tuple-element.21), channel_id=1, source_target_pairs={{208,0},{64,16},{240,32},{96,48},{16,64},{128,80},{48,96},{160,112... | collective-permute-start | bytes 442376 | tf_op jit(solution)/shard_map/ppermute | solution.py:420
  8.9 9.2 %collective-permute-start = (f32[576,128]{1,0:T(8,128)S(1)}, f32[576,128]{1,0:T(8,128)S(1)}, u32[]{:S(2)}, u32[]{:S(2)}) collective-permute-start(f32[576,128]{1,0:T(8,128)S(1)} %get-tuple-element.18), channel_id=1, source_target_pairs={{240,0},{32,16},{16,32},{64,48},{48,64},{96,80},{80,96},{128,112},... | collective-permute-start | bytes 884744 | tf_op jit(solution)/shard_map/ppermute | solution.py:420
  9.3 11.5 %collective-permute-start.6 = (f32[576,128]{1,0:T(8,128)S(1)}, f32[576,128]{1,0:T(8,128)S(1)}, u32[]{:S(2)}, u32[]{:S(2)}) collective-permute-start(f32[576,128]{1,0:T(8,128)S(1)} %get-tuple-element.18), channel_id=1, source_target_pairs={{16,0},{0,16},{48,32},{32,48},{80,64},{64,80},{112,96},{96,112},{1... | collective-permute-start | bytes 884744 | tf_op jit(solution)/shard_map/ppermute | solution.py:420
  13.7 20.2 %collective-permute-start.3 = (f32[256,512]{1,0:T(8,128)S(1)}, f32[256,512]{1,0:T(8,128)S(1)}, u32[]{:S(2)}, u32[]{:S(2)}) collective-permute-start(f32[256,512]{1,0:T(8,128)S(1)} %get-tuple-element.24), channel_id=1, source_target_pairs={{240,0},{32,16},{16,32},{64,48},{48,64},{96,80},{80,96},{128,112},... | collective-permute-start | bytes 1572872 | tf_op jit(solution)/shard_map/ppermute | solution.py:420
  15.0 18.9 %collective-permute-start.5 = (f32[256,512]{1,0:T(8,128)S(1)}, f32[256,512]{1,0:T(8,128)S(1)}, u32[]{:S(2)}, u32[]{:S(2)}) collective-permute-start(f32[256,512]{1,0:T(8,128)S(1)} %get-tuple-element.24), channel_id=1, source_target_pairs={{16,0},{0,16},{48,32},{32,48},{80,64},{64,80},{112,96},{96,112},{1... | collective-permute-start | bytes 1572872 | tf_op jit(solution)/shard_map/ppermute | solution.py:420
  18.1 15.8 %collective-permute-start.1 = (f32[128,512]{1,0:T(8,128)S(1)}, f32[128,512]{1,0:T(8,128)S(1)}, u32[]{:S(2)}, u32[]{:S(2)}) collective-permute-start(f32[128,512]{1,0:T(8,128)S(1)} %get-tuple-element.19), channel_id=1, source_target_pairs={{208,0},{64,16},{240,32},{96,48},{16,64},{128,80},{48,96},{160,112... | collective-permute-start | bytes 786440 | tf_op jit(solution)/shard_map/ppermute | solution.py:420
  20.8 14.6 %collective-permute-start.7 = (f32[128,512]{1,0:T(8,128)S(1)}, f32[128,512]{1,0:T(8,128)S(1)}, u32[]{:S(2)}, u32[]{:S(2)}) collective-permute-start(f32[128,512]{1,0:T(8,128)S(1)} %get-tuple-element.27), channel_id=1, source_target_pairs={{48,0},{224,16},{80,32},{0,48},{112,64},{32,80},{144,96},{64,112},... | collective-permute-start | bytes 786440 | tf_op jit(solution)/shard_map/ppermute | solution.py:420

commit v6 on v5

--- a/solution.py
+++ b/solution.py
@@ -59,7 +59,7 @@
     return lax.axis_index("blk") % 2 == 0
 
 
-def first_kernel(root_ref, back_out, both_out, ahead_out, turn_out, top, bottom, rolled):
+def first_kernel(root_ref, back_out, both_out, ahead_out, turn_out, top, bottom, rolled, window):
     tiles = [pl.ds(8 * i, 8) for i in range(ROOT_ROWS // 8)]
     cols = [pl.ds(g * LANES, LANES) for g in range(PARTS)]
     low_cols = [pl.ds(WIDTH + g * LANES, LANES) for g in range(PARTS)]
@@ -90,36 +90,48 @@
         for rows in tiles:
             b = jnp.where(last, rolled[rows, cols[(g + 1) % PARTS]], rolled[rows, cols[g]])
             bottom[rows, cols[g]] = b
-            if step + 1 < SWEEPS:
-                acc = added(acc, b * b, top[rows, cols[g]] * b)
-        if step + 1 < SWEEPS:
-            bb[g], tb[g] = (total8(x) for x in acc)
-
-    for step in range(SWEEPS):
+            acc = added(acc, b * b, top[rows, cols[g]] * b)
+        bb[g], tb[g] = (total8(x) for x in acc)
+
+    for step in range(SWEEPS - 1):
         rotate(step, 0)
         for g in range(1, PARTS):
             rotate(step, g)
             shift(step, g - 1)
         shift(step, PARTS - 1)
+    for g in range(PARTS):
+        cosine, sine, _ = turn_of(tt[g], bb[g], tb[g])
+        turn_out[pl.ds(SWEEPS - 1, 1), cols[g]] = cosine
+        turn_out[pl.ds(2 * SWEEPS - 1, 1), cols[g]] = sine
 
     part = lax.axis_index("rep") // PARTS
     here = pl.ds(pl.multiple_of(part * LANES, LANES), LANES)
     after = pl.ds(pl.multiple_of(lax.rem(part + 1, PARTS) * LANES, LANES), LANES)
     lane_group = lax.broadcasted_iota(jnp.int32, (8, LANES), 1) // HALO
 
+    own, behind = pl.ds(0, LANES), pl.ds(LANES, LANES)
+    for source, target in ((here, own), (after, behind)):
+        c = wide8(turn_out[pl.ds(SWEEPS - 1, 1), source])
+        s = wide8(turn_out[pl.ds(2 * SWEEPS - 1, 1), source])
+        for rows in tiles:
+            t, b = top[rows, source], bottom[rows, source]
+            window[rows, target] = c * t + s * b
+            rolled[rows, target] = pltpu.roll(c * b - s * t, LANES - 1, 1)
+
     def folded(block, q):
-        out = block[pl.ds(8 * q, 8), after]
+        out = block[pl.ds(8 * q, 8), behind]
         for g in range(1, GROUPS):
-            piece = block[pl.ds(g * HALO_ROWS + 8 * q, 8), after]
+            piece = block[pl.ds(g * HALO_ROWS + 8 * q, 8), behind]
             out = jnp.where(lane_group == g, pltpu.roll(piece, g * HALO, 1), out)
         return out
 
     even = even_slot()
     for v in range(CHUNK_ROWS // 8):
         if v < ROOT_ROWS // 8:
-            t, b = top[pl.ds(8 * v, 8), here], bottom[pl.ds(8 * v, 8), here]
+            rows = pl.ds(8 * v, 8)
+            t, b = window[rows, own], jnp.where(last, rolled[rows, behind], rolled[rows, own])
         else:
-            t, b = (folded(block, v - ROOT_ROWS // 8) for block in (top, bottom))
+            t, b = (folded(block, v - ROOT_ROWS // 8) for block in (window, rolled))
         both_out[pl.ds(8 * v, 8), :] = t
         both_out[pl.ds(CHUNK_ROWS + 8 * v, 8), :] = b
         back_out[pl.ds(8 * v, 8), :] = jnp.where(even, b, t)
@@ -427,7 +439,7 @@
     back_root, both_root, ahead_root, turn0 = call(
         first_kernel,
         [(CHUNK_ROWS, LANES), (2 * CHUNK_ROWS, LANES), (CHUNK_ROWS, LANES), (2 * SWEEPS, WIDTH)],
-        [(ROOT_ROWS, WIDTH)] * 3,
+        [(ROOT_ROWS, WIDTH)] * 3 + [(ROOT_ROWS, 2 * LANES)],
         [root_rows],
         16 * ROOT_ROWS * WIDTH * SWEEPS,
     )

time: 37.4 us -> 37.2 us (level)
  no operation moved by 1% of the time
where the time goes in v6:
time: 37.2 us; the launch traced here: 37 us
  starting transfers between devices  14.9 us (40%)
  blocking collectives  8.78 us (24%)
  Pallas kernels  7.93 us (21%)
  waiting for transfers between devices  3.5 us (9%)
  local copies, waits for them, and re-layouts  1.22 us (3%)
  between operations  0.67 us (2%)
    ppermute x8, starting transfers between devices, swapped(): lax.ppermute(shard, 'blk', [((i + (by if i % 2 == 0 else -by)) % length,...  14.9 us
    all_to_all x1, blocking collectives, body(): turns = lax.all_to_all(turns, 'rep', 0, 0, axis_index_groups=groups)  8.78 us
    pallas_call x5, Pallas kernels, call(): pl.pallas_call(kernel, out_shape=shapes, in_specs=[vmem] * len(args), out...  7.93 us
    ppermute x8, waiting for transfers between devices, swapped(): lax.ppermute(shard, 'blk', [((i + (by if i % 2 == 0 else -by)) % length,...  3.5 us
    unnamed x4, local copies, waits for them, and re-layouts  1.22 us
  transfers between devices with their start and end apart: 8, of which 2 were waited for; matrix products, arithmetic and copies ran while one was open for 0% of the time, Pallas kernels for 13%

profile of v6, /device:TPU:1, one launch (start us, length us, event | category | flops | bytes accessed | tf_op | source)
XLA Modules:
  0.0 37.0 jit_solution(12128730369284667723)
XLA Ops:
  0.6 0.0 copy-start
  0.6 1.2 %copy-done = f32[256,1024]{1,0:T(8,128)S(1)} copy-done((f32[256,1024]{1,0:T(8,128)S(1)}, f32[256,1024]{1,0:T(8,128)}, u32[]{:S(2)}) %copy-start) | copy-done | bytes 1048600
  1.9 0.0 copy-start.1
  1.9 1.2 %shard_map.41 = (f32[288,128]{1,0:T(8,128)S(1)}, f32[576,128]{1,0:T(8,128)S(1)}, f32[288,128]{1,0:T(8,128)S(1)}, f32[8,512]{1,0:T(8,128)S(1)}) custom-call(f32[256,1024]{1,0:T(8,128)S(1)} %copy-done), custom_call_target="tpu_custom_call" | custom-call | flops 8388608 | bytes 1654784 | tf_op jit(solution)/shard_map/pallas_call | solution.py:419
  3.1 5.6 %collective-permute-start.4 = (f32[288,128]{1,0:T(8,128)S(1)}, f32[288,128]{1,0:T(8,128)S(1)}, u32[]{:S(2)}, u32[]{:S(2)}) collective-permute-start(f32[288,128]{1,0:T(8,128)S(1)} %get-tuple-element.23), channel_id=1, source_target_pairs={{48,0},{224,16},{80,32},{0,48},{112,64},{32,80},{144,96},{64,112},... | collective-permute-start | bytes 442376 | tf_op jit(solution)/shard_map/ppermute | solution.py:432
  8.7 0.0 collective-permute-start.2
  8.7 0.4 %collective-permute-start = (f32[576,128]{1,0:T(8,128)S(1)}, f32[576,128]{1,0:T(8,128)S(1)}, u32[]{:S(2)}, u32[]{:S(2)}) collective-permute-start(f32[576,128]{1,0:T(8,128)S(1)} %get-tuple-element.18), channel_id=1, source_target_pairs={{240,0},{32,16},{16,32},{64,48},{48,64},{96,80},{80,96},{128,112},... | collective-permute-start | bytes 884744 | tf_op jit(solution)/shard_map/ppermute | solution.py:432
  9.1 0.5 %collective-permute-start.6 = (f32[576,128]{1,0:T(8,128)S(1)}, f32[576,128]{1,0:T(8,128)S(1)}, u32[]{:S(2)}, u32[]{:S(2)}) collective-permute-start(f32[576,128]{1,0:T(8,128)S(1)} %get-tuple-element.18), channel_id=1, source_target_pairs={{16,0},{0,16},{48,32},{32,48},{80,64},{64,80},{112,96},{96,112},{1... | collective-permute-start | bytes 884744 | tf_op jit(solution)/shard_map/ppermute | solution.py:432
  9.6 0.0 copy-done.1
  9.6 0.4 shard_map.42
  9.9 2.8 %collective-permute-done.4.ahead = f32[288,128]{1,0:T(8,128)S(1)} collective-permute-done((f32[288,128]{1,0:T(8,128)S(1)}, f32[288,128]{1,0:T(8,128)S(1)}, u32[]{:S(2)}, u32[]{:S(2)}) %collective-permute-start.4) | collective-permute-done | bytes 147488 | tf_op jit(solution)/shard_map/ppermute | solution.py:432
  12.7 0.7 %collective-permute-done.2.back = f32[288,128]{1,0:T(8,128)S(1)} collective-permute-done((f32[288,128]{1,0:T(8,128)S(1)}, f32[288,128]{1,0:T(8,128)S(1)}, u32[]{:S(2)}, u32[]{:S(2)}) %collective-permute-start.2) | collective-permute-done | bytes 147488 | tf_op jit(solution)/shard_map/ppermute | solution.py:432
  13.4 1.3 %collective-permute-start.3 = (f32[256,512]{1,0:T(8,128)S(1)}, f32[256,512]{1,0:T(8,128)S(1)}, u32[]{:S(2)}, u32[]{:S(2)}) collective-permute-start(f32[256,512]{1,0:T(8,128)S(1)} %get-tuple-element.24), channel_id=1, source_target_pairs={{240,0},{32,16},{16,32},{64,48},{48,64},{96,80},{80,96},{128,112},... | collective-permute-start | bytes 1572872 | tf_op jit(solution)/shard_map/ppermute | solution.py:432
  14.7 3.1 %collective-permute-start.5 = (f32[256,512]{1,0:T(8,128)S(1)}, f32[256,512]{1,0:T(8,128)S(1)}, u32[]{:S(2)}, u32[]{:S(2)}) collective-permute-start(f32[256,512]{1,0:T(8,128)S(1)} %get-tuple-element.24), channel_id=1, source_target_pairs={{16,0},{0,16},{48,32},{32,48},{80,64},{64,80},{112,96},{96,112},{1... | collective-permute-start | bytes 1572872 | tf_op jit(solution)/shard_map/ppermute | solution.py:432
  17.8 0.0 collective-permute-done.pair_out
  17.8 2.8 %collective-permute-start.1 = (f32[128,512]{1,0:T(8,128)S(1)}, f32[128,512]{1,0:T(8,128)S(1)}, u32[]{:S(2)}, u32[]{:S(2)}) collective-permute-start(f32[128,512]{1,0:T(8,128)S(1)} %get-tuple-element.19), channel_id=1, source_target_pairs={{208,0},{64,16},{240,32},{96,48},{16,64},{128,80},{48,96},{160,112... | collective-permute-start | bytes 786440 | tf_op jit(solution)/shard_map/ppermute | solution.py:432
  20.6 0.0 collective-permute-done.6.pair_in
  20.6 1.3 %collective-permute-start.7 = (f32[128,512]{1,0:T(8,128)S(1)}, f32[128,512]{1,0:T(8,128)S(1)}, u32[]{:S(2)}, u32[]{:S(2)}) collective-permute-start(f32[128,512]{1,0:T(8,128)S(1)} %get-tuple-element.27), channel_id=1, source_target_pairs={{48,0},{224,16},{80,32},{0,48},{112,64},{32,80},{144,96},{64,112},... | collective-permute-start | bytes 786440 | tf_op jit(solution)/shard_map/ppermute | solution.py:432
  21.9 3.0 %shard_map.43 = f32[4,56,128]{2,1,0:T(8,128)S(1)} custom-call(f32[288,128]{1,0:T(8,128)S(1)} %collective-permute-done.2.back, f32[576,128]{1,0:T(8,128)S(1)} %collective-permute-done.pair_out, f32[576,128]{1,0:T(8,128)S(1)} %collective-permute-done.6.pair_in, f32[288,128]{1,0:T(8,128)S(1)} %collective-permute-done.4.ahead), custom_call_target="tpu_custom_call" | custom-call | flops 14155776 | bytes 999424 | tf_op jit(solution)/shard_map/pallas_call | solution.py:419
  24.9 8.8 %all_to_all.5.turns = f32[4,56,128]{2,1,0:T(8,128)S(1)} all-to-all(f32[4,56,128]{2,1,0:T(8,128)S(1)} %shard_map.43), channel_id=1, replica_groups={{0,4,8,12},{1,5,9,13},{2,6,10,14},{3,7,11,15},{16,20,24,28},{17,21,25,2..., dimensions={0} | all-to-all | bytes 229376 | tf_op jit(solution)/shard_map/all_to_all | solution.py:474
  33.7 0.0 collective-permute-done.1.back
  33.7 0.0 collective-permute-done.3.pair_out
  33.7 0.0 collective-permute-done.5.pair_in
  33.7 1.6 %shard_map.44 = (f32[1024]{0:T(1024)}, f32[128,512]{1,0:T(8,128)S(1)}, f32[128,512]{1,0:T(8,128)S(1)}) custom-call(f32[128,512]{1,0:T(8,128)S(1)} %collective-permute-done.1.back, f32[256,512]{1,0:T(8,128)S(1)} %collective-permute-done.3.pair_out, f32[256,512]{1,0:T(8,128)S(1)} %collective-permute-done.5.pair_in, f32[4,56,128]{2,1,0:T(8,128)S(1)} %all_to_all.5.turns), custom_call_target="tpu_custom_call" | custom-call | flops 6291456 | bytes 1953792 | tf_op jit(solution)/shard_map/pallas_call | solution.py:419
  35.2 0.0 collective-permute-done.7.ahead
  35.2 1.8 %shard_map.45 = f32[128,1024]{1,0:T(8,128)} custom-call(f32[256,512]{1,0:T(8,128)S(1)} %collective-permute-done.5.pair_in, f32[128,512]{1,0:T(8,128)S(1)} %collective-permute-done.7.ahead, f32[128,512]{1,0:T(8,128)S(1)} %get-tuple-element.28.near, f32[128,512]{1,0:T(8,128)S(1)} %get-tuple-element.29.done, f32[4,56,128]{2,1,0:T(8,128)S(1)} %all_to_all.5.turns), custom_call_target="tpu_custom_call" | custom-call | flops 6291456 | bytes 1949696 | tf_op jit(solution)/shard_map/pallas_call | solution.py:419
Async XLA Ops:
  0.6 1.2 %copy-start = (f32[256,1024]{1,0:T(8,128)S(1)}, f32[256,1024]{1,0:T(8,128)}, u32[]{:S(2)}) copy-start(f32[256,1024]{1,0:T(8,128)} %root_ref.1) | copy-start | bytes 3145732
  1.9 7.7 %copy-start.1 = (bf16[128,1024]{1,0:T(8,128)(2,1)S(1)}, bf16[128,1024]{1,0:T(8,128)(2,1)}, u32[]{:S(2)}) copy-start(bf16[128,1024]{1,0:T(8,128)(2,1)} %grad_ref.1) | copy-start | bytes 786436
  3.1 9.6 %collective-permute-start.4 = (f32[288,128]{1,0:T(8,128)S(1)}, f32[288,128]{1,0:T(8,128)S(1)}, u32[]{:S(2)}, u32[]{:S(2)}) collective-permute-start(f32[288,128]{1,0:T(8,128)S(1)} %get-tuple-element.23), channel_id=1, source_target_pairs={{48,0},{224,16},{80,32},{0,48},{112,64},{32,80},{144,96},{64,112},... | collective-permute-start | bytes 442376 | tf_op jit(solution)/shard_map/ppermute | solution.py:432
  8.7 4.7 %collective-permute-start.2 = (f32[288,128]{1,0:T(8,128)S(1)}, f32[288,128]{1,0:T(8,128)S(1)}, u32[]{:S(2)}, u32[]{:S(2)}) collective-permute-start(f32[288,128]{1,0:T(8,128)S(1)} %get-tuple-element.21), channel_id=1, source_target_pairs={{208,0},{64,16},{240,32},{96,48},{16,64},{128,80},{48,96},{160,112... | collective-permute-start | bytes 442376 | tf_op jit(solution)/shard_map/ppermute | solution.py:432
  8.7 9.2 %collective-permute-start = (f32[576,128]{1,0:T(8,128)S(1)}, f32[576,128]{1,0:T(8,128)S(1)}, u32[]{:S(2)}, u32[]{:S(2)}) collective-permute-start(f32[576,128]{1,0:T(8,128)S(1)} %get-tuple-element.18), channel_id=1, source_target_pairs={{240,0},{32,16},{16,32},{64,48},{48,64},{96,80},{80,96},{128,112},... | collective-permute-start | bytes 884744 | tf_op jit(solution)/shard_map/ppermute | solution.py:432
  9.1 11.5 %collective-permute-start.6 = (f32[576,128]{1,0:T(8,128)S(1)}, f32[576,128]{1,0:T(8,128)S(1)}, u32[]{:S(2)}, u32[]{:S(2)}) collective-permute-start(f32[576,128]{1,0:T(8,128)S(1)} %get-tuple-element.18), channel_id=1, source_target_pairs={{16,0},{0,16},{48,32},{32,48},{80,64},{64,80},{112,96},{96,112},{1... | collective-permute-start | bytes 884744 | tf_op jit(solution)/shard_map/ppermute | solution.py:432
  13.4 20.2 %collective-permute-start.3 = (f32[256,512]{1,0:T(8,128)S(1)}, f32[256,512]{1,0:T(8,128)S(1)}, u32[]{:S(2)}, u32[]{:S(2)}) collective-permute-start(f32[256,512]{1,0:T(8,128)S(1)} %get-tuple-element.24), channel_id=1, source_target_pairs={{240,0},{32,16},{16,32},{64,48},{48,64},{96,80},{80,96},{128,112},... | collective-permute-start | bytes 1572872 | tf_op jit(solution)/shard_map/ppermute | solution.py:432
  14.7 18.9 %collective-permute-start.5 = (f32[256,512]{1,0:T(8,128)S(1)}, f32[256,512]{1,0:T(8,128)S(1)}, u32[]{:S(2)}, u32[]{:S(2)}) collective-permute-start(f32[256,512]{1,0:T(8,128)S(1)} %get-tuple-element.24), channel_id=1, source_target_pairs={{16,0},{0,16},{48,32},{32,48},{80,64},{64,80},{112,96},{96,112},{1... | collective-permute-start | bytes 1572872 | tf_op jit(solution)/shard_map/ppermute | solution.py:432
  17.8 15.8 %collective-permute-start.1 = (f32[128,512]{1,0:T(8,128)S(1)}, f32[128,512]{1,0:T(8,128)S(1)}, u32[]{:S(2)}, u32[]{:S(2)}) collective-permute-start(f32[128,512]{1,0:T(8,128)S(1)} %get-tuple-element.19), channel_id=1, source_target_pairs={{208,0},{64,16},{240,32},{96,48},{16,64},{128,80},{48,96},{160,112... | collective-permute-start | bytes 786440 | tf_op jit(solution)/shard_map/ppermute | solution.py:432
  20.6 14.6 %collective-permute-start.7 = (f32[128,512]{1,0:T(8,128)S(1)}, f32[128,512]{1,0:T(8,128)S(1)}, u32[]{:S(2)}, u32[]{:S(2)}) collective-permute-start(f32[128,512]{1,0:T(8,128)S(1)} %get-tuple-element.27), channel_id=1, source_target_pairs={{48,0},{224,16},{80,32},{0,48},{112,64},{32,80},{144,96},{64,112},... | collective-permute-start | bytes 786440 | tf_op jit(solution)/shard_map/ppermute | solution.py:432

commit v7 on v6

--- a/solution.py
+++ b/solution.py
@@ -8,6 +8,8 @@
 
 ROOT_ROWS = 256
 SWEEPS = 4
+OUT_COPIES = 4
+LAST_PARTS = 1
 WIDTH = 512
 LANES = 128
 HALO = 16
@@ -310,11 +312,11 @@
         wide[:, pl.ds(part * LANES, LANES)] = turns[part]
 
 
-def turned_pair(wide, row, source, target, count, finish):
+def turned_pair(wide, row, source, target, tiles, finish):
     for k in range(SWEEPS):
         c = jnp.broadcast_to(wide[pl.ds(row + k, 1), :], (8, WIDTH))
         s = jnp.broadcast_to(wide[pl.ds(STEPS + row + k, 1), :], (8, WIDTH))
-        for i in range(count):
+        for i in tiles:
             rows = pl.ds(8 * i, 8)
             t, b = source(i) if k == 0 else (target[0][rows, :], target[1][rows, :])
             t, b = c * t + s * b, c * b - s * t
@@ -369,20 +371,19 @@
     def keep_second(i, t, b):
         done_out[parts(i)[0], :] = jnp.where(even, t, pltpu.roll(b, WIDTH - 1, 1))
 
-    turned_pair(wide, row_of(0, 0, 2), outer, (t0, b0), count, keep_outer)
-    turned_pair(wide, row_of(0, 1, 1), inner, (t1, b1), count, keep_inner)
-    turned_pair(wide, row_of(1, 0, 1), second, (t1, b1), count, keep_second)
+    turned_pair(wide, row_of(0, 0, 2), outer, (t0, b0), range(count), keep_outer)
+    turned_pair(wide, row_of(0, 1, 1), inner, (t1, b1), range(count), keep_inner)
+    turned_pair(wide, row_of(1, 0, 1), second, (t1, b1), range(count), keep_second)
 
     eigen_out[pl.ds(0, WIDTH)] = wide[EIGEN_ROW, :]
     bottom = pltpu.roll(wide[pl.ds(EIGEN_ROW + 1, 1), :], 4 * SWEEPS, 1)
     eigen_out[pl.ds(WIDTH, WIDTH)] = bottom[0]
 
 
-def last_kernel(pair_in, ahead, near, done, turns, projected_out, wide, t0, b0):
+def last_kernel(pair_in, ahead, near, done, wide, projected_out, t0, b0, result, left):
     rows_all = ahead.shape[0]
     count = rows_all // 8
     even = even_slot()
-    widened(turns, wide)
 
     def first(i):
         rows, low = pl.ds(8 * i, 8), pl.ds(rows_all + 8 * i, 8)
@@ -403,15 +404,30 @@
     def write(i, t, b):
         rows = pl.ds(8 * i, 8)
         b = pltpu.roll(b, 4 * SWEEPS - 1, 1)
-        projected_out[rows, pl.ds(0, WIDTH)] = t * t
-        projected_out[rows, pl.ds(WIDTH, WIDTH)] = b * b
-
-    turned_pair(wide, row_of(0, 2, 0), first, (t0, b0), count, keep)
-    turned_pair(wide, row_of(1, 1, 0), with_kept(near), (t0, b0), count, keep)
-    turned_pair(wide, row_of(2, 0, 0), with_kept(done), (t0, b0), count, write)
-
-
-def call(kernel, outs, scratch, args, flops):
+        result[rows, pl.ds(0, WIDTH)] = t * t
+        result[rows, pl.ds(WIDTH, WIDTH)] = b * b
+        if (i + 1) % per_copy == 0:
+            copies[i // per_copy].start()
+
+    per_copy = count // OUT_COPIES
+    size = 8 * per_copy
+    copies = [
+        pltpu.make_async_copy(
+            result.at[pl.ds(j * size, size), :], projected_out.at[pl.ds(j * size, size), :], left.at[j]
+        )
+        for j in range(OUT_COPIES)
+    ]
+    turned_pair(wide, row_of(0, 2, 0), first, (t0, b0), range(count), keep)
+    turned_pair(wide, row_of(1, 1, 0), with_kept(near), (t0, b0), range(count), keep)
+    each = count // LAST_PARTS
+    for first_tile in range(0, count, each):
+        tiles = range(first_tile, first_tile + each)
+        turned_pair(wide, row_of(2, 0, 0), with_kept(done), (t0, b0), tiles, write)
+    for copy in copies:
+        copy.wait()
+
+
+def call(kernel, outs, scratch, args, flops, copies=0):
     f32 = jnp.float32
     vmem = pl.BlockSpec(memory_space=pltpu.VMEM)
     shapes = tuple(jax.ShapeDtypeStruct(shape, f32) for shape in outs)
@@ -420,8 +436,9 @@
         kernel,
         out_shape=shapes,
         in_specs=[vmem] * len(args),
-        out_specs=tuple(vmem for _ in shapes),
-        scratch_shapes=[pltpu.VMEM(shape, f32) for shape in scratch],
+        out_specs=tuple(pl.BlockSpec(memory_space=pl.ANY) if copies else vmem for _ in shapes),
+        scratch_shapes=[pltpu.VMEM(shape, f32) for shape in scratch]
+        + ([pltpu.SemaphoreType.DMA((copies,))] if copies else []),
         compiler_params=pltpu.CompilerParams(vmem_limit_bytes=24 * MEGA),
         cost_estimate=pl.CostEstimate(flops=flops, bytes_accessed=moved, transcendentals=0),
     )(*args)
@@ -473,19 +490,20 @@
     groups = [[x * near + z for x in range(PARTS)] for z in range(near)]
     turns = lax.all_to_all(turns, "rep", 0, 0, axis_index_groups=groups)
     block, angles = (rows, WIDTH), (ANGLE_ROWS, WIDTH)
-    eigen, near_block, done_block = call(
+    eigen, near_block, done_block, wide_turns = call(
         middle_kernel,
-        [(2 * WIDTH,), block, block],
-        [angles] + [block] * 4,
+        [(2 * WIDTH,), block, block, angles],
+        [block] * 4,
         [grad0, grad1, grad2, turns],
         4 * rows * WIDTH * STEPS,
     )
     (projected,) = call(
         last_kernel,
         [(rows, 2 * WIDTH)],
-        [angles] + [block] * 2,
-        [grad2, grad3, near_block, done_block, turns],
+        [block] * 2 + [(rows, 2 * WIDTH)],
+        [grad2, grad3, near_block, done_block, wide_turns],
         4 * rows * WIDTH * STEPS,
+        copies=OUT_COPIES,
     )
     return eigen, projected
 

time: 37.2 us -> 37.1 us (level)
  no operation moved by 1% of the time
where the time goes in v7:
time: 37.1 us; the launch traced here: 36.9 us
  starting transfers between devices  14.9 us (40%)
  blocking collectives  8.78 us (24%)
  Pallas kernels  7.86 us (21%)
  waiting for transfers between devices  3.5 us (9%)
  local copies, waits for them, and re-layouts  1.22 us (3%)
  between operations  0.67 us (2%)
    ppermute x8, starting transfers between devices, swapped(): lax.ppermute(shard, 'blk', [((i + (by if i % 2 == 0 else -by)) % length,...  14.9 us
    all_to_all x1, blocking collectives, body(): turns = lax.all_to_all(turns, 'rep', 0, 0, axis_index_groups=groups)  8.78 us
    pallas_call x5, Pallas kernels, call(): pl.pallas_call(kernel, out_shape=shapes, in_specs=[vmem] * len(args), out...  7.86 us
    ppermute x8, waiting for transfers between devices, swapped(): lax.ppermute(shard, 'blk', [((i + (by if i % 2 == 0 else -by)) % length,...  3.5 us
    unnamed x4, local copies, waits for them, and re-layouts  1.22 us
  transfers between devices with their start and end apart: 8, of which 2 were waited for; matrix products, arithmetic and copies ran while one was open for 0% of the time, Pallas kernels for 13%

profile of v7, /device:TPU:1, one launch (start us, length us, event | category | flops | bytes accessed | tf_op | source)
XLA Modules:
  0.0 36.9 jit_solution(9751731995559888455)
XLA Ops:
  0.6 0.0 copy-start
  0.6 1.2 %copy-done = f32[256,1024]{1,0:T(8,128)S(1)} copy-done((f32[256,1024]{1,0:T(8,128)S(1)}, f32[256,1024]{1,0:T(8,128)}, u32[]{:S(2)}) %copy-start) | copy-done | bytes 1048600
  1.9 0.0 copy-start.1
  1.9 1.2 %shard_map.41 = (f32[288,128]{1,0:T(8,128)S(1)}, f32[576,128]{1,0:T(8,128)S(1)}, f32[288,128]{1,0:T(8,128)S(1)}, f32[8,512]{1,0:T(8,128)S(1)}) custom-call(f32[256,1024]{1,0:T(8,128)S(1)} %copy-done), custom_call_target="tpu_custom_call" | custom-call | flops 8388608 | bytes 1654784 | tf_op jit(solution)/shard_map/pallas_call | solution.py:435
  3.1 5.6 %collective-permute-start.4 = (f32[288,128]{1,0:T(8,128)S(1)}, f32[288,128]{1,0:T(8,128)S(1)}, u32[]{:S(2)}, u32[]{:S(2)}) collective-permute-start(f32[288,128]{1,0:T(8,128)S(1)} %get-tuple-element.24), channel_id=1, source_target_pairs={{48,0},{224,16},{80,32},{0,48},{112,64},{32,80},{144,96},{64,112},... | collective-permute-start | bytes 442376 | tf_op jit(solution)/shard_map/ppermute | solution.py:449
  8.7 0.0 collective-permute-start.2
  8.7 0.4 %collective-permute-start = (f32[576,128]{1,0:T(8,128)S(1)}, f32[576,128]{1,0:T(8,128)S(1)}, u32[]{:S(2)}, u32[]{:S(2)}) collective-permute-start(f32[576,128]{1,0:T(8,128)S(1)} %get-tuple-element.19), channel_id=1, source_target_pairs={{240,0},{32,16},{16,32},{64,48},{48,64},{96,80},{80,96},{128,112},... | collective-permute-start | bytes 884744 | tf_op jit(solution)/shard_map/ppermute | solution.py:449
  9.1 0.5 %collective-permute-start.6 = (f32[576,128]{1,0:T(8,128)S(1)}, f32[576,128]{1,0:T(8,128)S(1)}, u32[]{:S(2)}, u32[]{:S(2)}) collective-permute-start(f32[576,128]{1,0:T(8,128)S(1)} %get-tuple-element.19), channel_id=1, source_target_pairs={{16,0},{0,16},{48,32},{32,48},{80,64},{64,80},{112,96},{96,112},{1... | collective-permute-start | bytes 884744 | tf_op jit(solution)/shard_map/ppermute | solution.py:449
  9.6 0.0 copy-done.1
  9.6 0.4 shard_map.42
  9.9 2.8 %collective-permute-done.4.ahead = f32[288,128]{1,0:T(8,128)S(1)} collective-permute-done((f32[288,128]{1,0:T(8,128)S(1)}, f32[288,128]{1,0:T(8,128)S(1)}, u32[]{:S(2)}, u32[]{:S(2)}) %collective-permute-start.4) | collective-permute-done | bytes 147488 | tf_op jit(solution)/shard_map/ppermute | solution.py:449
  12.7 0.7 %collective-permute-done.2.back = f32[288,128]{1,0:T(8,128)S(1)} collective-permute-done((f32[288,128]{1,0:T(8,128)S(1)}, f32[288,128]{1,0:T(8,128)S(1)}, u32[]{:S(2)}, u32[]{:S(2)}) %collective-permute-start.2) | collective-permute-done | bytes 147488 | tf_op jit(solution)/shard_map/ppermute | solution.py:449
  13.4 1.3 %collective-permute-start.3 = (f32[256,512]{1,0:T(8,128)S(1)}, f32[256,512]{1,0:T(8,128)S(1)}, u32[]{:S(2)}, u32[]{:S(2)}) collective-permute-start(f32[256,512]{1,0:T(8,128)S(1)} %get-tuple-element.25), channel_id=1, source_target_pairs={{240,0},{32,16},{16,32},{64,48},{48,64},{96,80},{80,96},{128,112},... | collective-permute-start | bytes 1572872 | tf_op jit(solution)/shard_map/ppermute | solution.py:449
  14.7 3.1 %collective-permute-start.5 = (f32[256,512]{1,0:T(8,128)S(1)}, f32[256,512]{1,0:T(8,128)S(1)}, u32[]{:S(2)}, u32[]{:S(2)}) collective-permute-start(f32[256,512]{1,0:T(8,128)S(1)} %get-tuple-element.25), channel_id=1, source_target_pairs={{16,0},{0,16},{48,32},{32,48},{80,64},{64,80},{112,96},{96,112},{1... | collective-permute-start | bytes 1572872 | tf_op jit(solution)/shard_map/ppermute | solution.py:449
  17.8 0.0 collective-permute-done.pair_out
  17.8 2.8 %collective-permute-start.1 = (f32[128,512]{1,0:T(8,128)S(1)}, f32[128,512]{1,0:T(8,128)S(1)}, u32[]{:S(2)}, u32[]{:S(2)}) collective-permute-start(f32[128,512]{1,0:T(8,128)S(1)} %get-tuple-element.20), channel_id=1, source_target_pairs={{208,0},{64,16},{240,32},{96,48},{16,64},{128,80},{48,96},{160,112... | collective-permute-start | bytes 786440 | tf_op jit(solution)/shard_map/ppermute | solution.py:449
  20.6 0.0 collective-permute-done.6.pair_in
  20.6 1.3 %collective-permute-start.7 = (f32[128,512]{1,0:T(8,128)S(1)}, f32[128,512]{1,0:T(8,128)S(1)}, u32[]{:S(2)}, u32[]{:S(2)}) collective-permute-start(f32[128,512]{1,0:T(8,128)S(1)} %get-tuple-element.28), channel_id=1, source_target_pairs={{48,0},{224,16},{80,32},{0,48},{112,64},{32,80},{144,96},{64,112},... | collective-permute-start | bytes 786440 | tf_op jit(solution)/shard_map/ppermute | solution.py:449
  21.9 3.0 %shard_map.43 = f32[4,56,128]{2,1,0:T(8,128)S(1)} custom-call(f32[288,128]{1,0:T(8,128)S(1)} %collective-permute-done.2.back, f32[576,128]{1,0:T(8,128)S(1)} %collective-permute-done.pair_out, f32[576,128]{1,0:T(8,128)S(1)} %collective-permute-done.6.pair_in, f32[288,128]{1,0:T(8,128)S(1)} %collective-permute-done.4.ahead), custom_call_target="tpu_custom_call" | custom-call | flops 14155776 | bytes 999424 | tf_op jit(solution)/shard_map/pallas_call | solution.py:435
  24.9 8.8 %all_to_all.5.turns = f32[4,56,128]{2,1,0:T(8,128)S(1)} all-to-all(f32[4,56,128]{2,1,0:T(8,128)S(1)} %shard_map.43), channel_id=1, replica_groups={{0,4,8,12},{1,5,9,13},{2,6,10,14},{3,7,11,15},{16,20,24,28},{17,21,25,2..., dimensions={0} | all-to-all | bytes 229376 | tf_op jit(solution)/shard_map/all_to_all | solution.py:491
  33.7 0.0 collective-permute-done.1.back
  33.7 0.0 collective-permute-done.3.pair_out
  33.7 0.0 collective-permute-done.5.pair_in
  33.7 1.5 %shard_map.44 = (f32[1024]{0:T(1024)}, f32[128,512]{1,0:T(8,128)S(1)}, f32[128,512]{1,0:T(8,128)S(1)}, f32[56,512]{1,0:T(8,128)S(1)}) custom-call(f32[128,512]{1,0:T(8,128)S(1)} %collective-permute-done.1.back, f32[256,512]{1,0:T(8,128)S(1)} %collective-permute-done.3.pair_out, f32[256,512]{1,0:T(8,128)S(1)} %collective-permute-done.5.pair_in, ...), custom_call_target="tpu_custom_call" | custom-call | flops 6291456 | bytes 2068480 | tf_op jit(solution)/shard_map/pallas_call | solution.py:435
  35.2 0.0 collective-permute-done.7.ahead
  35.2 1.7 %shard_map.45 = f32[128,1024]{1,0:T(8,128)} custom-call(f32[256,512]{1,0:T(8,128)S(1)} %collective-permute-done.5.pair_in, f32[128,512]{1,0:T(8,128)S(1)} %collective-permute-done.7.ahead, f32[128,512]{1,0:T(8,128)S(1)} %get-tuple-element.29.near, f32[128,512]{1,0:T(8,128)S(1)} %get-tuple-element.30.done, f32[56,512]{1,0:T(8,128)S(1)} %get-tuple-element.31.wide), custom_call_target="tpu_custom_call" | custom-call | flops 6291456 | bytes 1949696 | tf_op jit(solution)/shard_map/pallas_call | solution.py:435
Async XLA Ops:
  0.6 1.2 %copy-start = (f32[256,1024]{1,0:T(8,128)S(1)}, f32[256,1024]{1,0:T(8,128)}, u32[]{:S(2)}) copy-start(f32[256,1024]{1,0:T(8,128)} %root_ref.1) | copy-start | bytes 3145732
  1.9 7.7 %copy-start.1 = (bf16[128,1024]{1,0:T(8,128)(2,1)S(1)}, bf16[128,1024]{1,0:T(8,128)(2,1)}, u32[]{:S(2)}) copy-start(bf16[128,1024]{1,0:T(8,128)(2,1)} %grad_ref.1) | copy-start | bytes 786436
  3.1 9.6 %collective-permute-start.4 = (f32[288,128]{1,0:T(8,128)S(1)}, f32[288,128]{1,0:T(8,128)S(1)}, u32[]{:S(2)}, u32[]{:S(2)}) collective-permute-start(f32[288,128]{1,0:T(8,128)S(1)} %get-tuple-element.24), channel_id=1, source_target_pairs={{48,0},{224,16},{80,32},{0,48},{112,64},{32,80},{144,96},{64,112},... | collective-permute-start | bytes 442376 | tf_op jit(solution)/shard_map/ppermute | solution.py:449
  8.7 4.7 %collective-permute-start.2 = (f32[288,128]{1,0:T(8,128)S(1)}, f32[288,128]{1,0:T(8,128)S(1)}, u32[]{:S(2)}, u32[]{:S(2)}) collective-permute-start(f32[288,128]{1,0:T(8,128)S(1)} %get-tuple-element.22), channel_id=1, source_target_pairs={{208,0},{64,16},{240,32},{96,48},{16,64},{128,80},{48,96},{160,112... | collective-permute-start | bytes 442376 | tf_op jit(solution)/shard_map/ppermute | solution.py:449
  8.7 9.2 %collective-permute-start = (f32[576,128]{1,0:T(8,128)S(1)}, f32[576,128]{1,0:T(8,128)S(1)}, u32[]{:S(2)}, u32[]{:S(2)}) collective-permute-start(f32[576,128]{1,0:T(8,128)S(1)} %get-tuple-element.19), channel_id=1, source_target_pairs={{240,0},{32,16},{16,32},{64,48},{48,64},{96,80},{80,96},{128,112},... | collective-permute-start | bytes 884744 | tf_op jit(solution)/shard_map/ppermute | solution.py:449
  9.1 11.5 %collective-permute-start.6 = (f32[576,128]{1,0:T(8,128)S(1)}, f32[576,128]{1,0:T(8,128)S(1)}, u32[]{:S(2)}, u32[]{:S(2)}) collective-permute-start(f32[576,128]{1,0:T(8,128)S(1)} %get-tuple-element.19), channel_id=1, source_target_pairs={{16,0},{0,16},{48,32},{32,48},{80,64},{64,80},{112,96},{96,112},{1... | collective-permute-start | bytes 884744 | tf_op jit(solution)/shard_map/ppermute | solution.py:449
  13.4 20.2 %collective-permute-start.3 = (f32[256,512]{1,0:T(8,128)S(1)}, f32[256,512]{1,0:T(8,128)S(1)}, u32[]{:S(2)}, u32[]{:S(2)}) collective-permute-start(f32[256,512]{1,0:T(8,128)S(1)} %get-tuple-element.25), channel_id=1, source_target_pairs={{240,0},{32,16},{16,32},{64,48},{48,64},{96,80},{80,96},{128,112},... | collective-permute-start | bytes 1572872 | tf_op jit(solution)/shard_map/ppermute | solution.py:449
  14.7 18.9 %collective-permute-start.5 = (f32[256,512]{1,0:T(8,128)S(1)}, f32[256,512]{1,0:T(8,128)S(1)}, u32[]{:S(2)}, u32[]{:S(2)}) collective-permute-start(f32[256,512]{1,0:T(8,128)S(1)} %get-tuple-element.25), channel_id=1, source_target_pairs={{16,0},{0,16},{48,32},{32,48},{80,64},{64,80},{112,96},{96,112},{1... | collective-permute-start | bytes 1572872 | tf_op jit(solution)/shard_map/ppermute | solution.py:449
  17.8 15.8 %collective-permute-start.1 = (f32[128,512]{1,0:T(8,128)S(1)}, f32[128,512]{1,0:T(8,128)S(1)}, u32[]{:S(2)}, u32[]{:S(2)}) collective-permute-start(f32[128,512]{1,0:T(8,128)S(1)} %get-tuple-element.20), channel_id=1, source_target_pairs={{208,0},{64,16},{240,32},{96,48},{16,64},{128,80},{48,96},{160,112... | collective-permute-start | bytes 786440 | tf_op jit(solution)/shard_map/ppermute | solution.py:449
  20.6 14.6 %collective-permute-start.7 = (f32[128,512]{1,0:T(8,128)S(1)}, f32[128,512]{1,0:T(8,128)S(1)}, u32[]{:S(2)}, u32[]{:S(2)}) collective-permute-start(f32[128,512]{1,0:T(8,128)S(1)} %get-tuple-element.28), channel_id=1, source_target_pairs={{48,0},{224,16},{80,32},{0,48},{112,64},{32,80},{144,96},{64,112},... | collective-permute-start | bytes 786440 | tf_op jit(solution)/shard_map/ppermute | solution.py:449

commit v8 on v6

--- a/solution.py
+++ b/solution.py
@@ -460,7 +460,7 @@
     grad1 = swapped(after(both_grad, root0), -1)
     grad2 = swapped(after(both_grad, root3), 1)
     grad0 = swapped(after(back_grad, root1), -3)
-    grad3 = swapped(after(ahead_grad, root2), 3)
+    grad3 = swapped(after(ahead_grad, root1), 3)
     (turns,) = call(
         cone_kernel,
         [(PARTS, ANGLE_ROWS, LANES)],

time: 37.2 us -> 37.2 us (level)
  starting transfers between devices: 14.9 us -> 14.4 us
  waiting for transfers between devices: 3.5 us -> 4 us
    ppermute x8, starting transfers between devices: 14.9 us -> 14.4 us  [swapped(): lax.ppermute(shard, 'blk', [((i + (by if i % 2 == 0 else -by)) % length,...]
    ppermute x8, waiting for transfers between devices: 3.5 us -> 4 us  [swapped(): lax.ppermute(shard, 'blk', [((i + (by if i % 2 == 0 else -by)) % length,...]
where the time goes in v8:
time: 37.2 us; the launch traced here: 37 us
  starting transfers between devices  14.4 us (39%)
  blocking collectives  8.77 us (24%)
  Pallas kernels  7.94 us (21%)
  waiting for transfers between devices  4 us (11%)
  local copies, waits for them, and re-layouts  1.22 us (3%)
  between operations  0.67 us (2%)
    ppermute x8, starting transfers between devices, swapped(): lax.ppermute(shard, 'blk', [((i + (by if i % 2 == 0 else -by)) % length,...  14.4 us
    all_to_all x1, blocking collectives, body(): turns = lax.all_to_all(turns, 'rep', 0, 0, axis_index_groups=groups)  8.77 us
    pallas_call x5, Pallas kernels, call(): pl.pallas_call(kernel, out_shape=shapes, in_specs=[vmem] * len(args), out...  7.94 us
    ppermute x8, waiting for transfers between devices, swapped(): lax.ppermute(shard, 'blk', [((i + (by if i % 2 == 0 else -by)) % length,...  4 us
    unnamed x4, local copies, waits for them, and re-layouts  1.22 us
  transfers between devices with their start and end apart: 8, of which 2 were waited for; matrix products, arithmetic and copies ran while one was open for 0% of the time, Pallas kernels for 13%

profile of v8, /device:TPU:1, one launch (start us, length us, event | category | flops | bytes accessed | tf_op | source)
XLA Modules:
  0.0 37.0 jit_solution(14952300790224118107)
XLA Ops:
  0.6 0.0 copy-start
  0.6 1.2 %copy-done = f32[256,1024]{1,0:T(8,128)S(1)} copy-done((f32[256,1024]{1,0:T(8,128)S(1)}, f32[256,1024]{1,0:T(8,128)}, u32[]{:S(2)}) %copy-start) | copy-done | bytes 1048600
  1.9 0.0 copy-start.1
  1.9 1.2 %shard_map.41 = (f32[288,128]{1,0:T(8,128)S(1)}, f32[576,128]{1,0:T(8,128)S(1)}, f32[288,128]{1,0:T(8,128)S(1)}, f32[8,512]{1,0:T(8,128)S(1)}) custom-call(f32[256,1024]{1,0:T(8,128)S(1)} %copy-done), custom_call_target="tpu_custom_call" | custom-call | flops 8388608 | bytes 1654784 | tf_op jit(solution)/shard_map/pallas_call | solution.py:419
  3.1 5.6 %collective-permute-start.4 = (f32[288,128]{1,0:T(8,128)S(1)}, f32[288,128]{1,0:T(8,128)S(1)}, u32[]{:S(2)}, u32[]{:S(2)}) collective-permute-start(f32[288,128]{1,0:T(8,128)S(1)} %get-tuple-element.23), channel_id=1, source_target_pairs={{48,0},{224,16},{80,32},{0,48},{112,64},{32,80},{144,96},{64,112},... | collective-permute-start | bytes 442376 | tf_op jit(solution)/shard_map/ppermute | solution.py:432
  8.7 0.0 collective-permute-start.2
  8.7 0.4 %collective-permute-start = (f32[576,128]{1,0:T(8,128)S(1)}, f32[576,128]{1,0:T(8,128)S(1)}, u32[]{:S(2)}, u32[]{:S(2)}) collective-permute-start(f32[576,128]{1,0:T(8,128)S(1)} %get-tuple-element.18), channel_id=1, source_target_pairs={{240,0},{32,16},{16,32},{64,48},{48,64},{96,80},{80,96},{128,112},... | collective-permute-start | bytes 884744 | tf_op jit(solution)/shard_map/ppermute | solution.py:432
  9.1 0.0 copy-done.1
  9.1 0.4 shard_map.42
  9.4 3.3 %collective-permute-done.4.ahead = f32[288,128]{1,0:T(8,128)S(1)} collective-permute-done((f32[288,128]{1,0:T(8,128)S(1)}, f32[288,128]{1,0:T(8,128)S(1)}, u32[]{:S(2)}, u32[]{:S(2)}) %collective-permute-start.4) | collective-permute-done | bytes 147488 | tf_op jit(solution)/shard_map/ppermute | solution.py:432
  12.7 0.7 %collective-permute-done.2.back = f32[288,128]{1,0:T(8,128)S(1)} collective-permute-done((f32[288,128]{1,0:T(8,128)S(1)}, f32[288,128]{1,0:T(8,128)S(1)}, u32[]{:S(2)}, u32[]{:S(2)}) %collective-permute-start.2) | collective-permute-done | bytes 147488 | tf_op jit(solution)/shard_map/ppermute | solution.py:432
  13.4 1.3 %collective-permute-start.3 = (f32[256,512]{1,0:T(8,128)S(1)}, f32[256,512]{1,0:T(8,128)S(1)}, u32[]{:S(2)}, u32[]{:S(2)}) collective-permute-start(f32[256,512]{1,0:T(8,128)S(1)} %get-tuple-element.24), channel_id=1, source_target_pairs={{240,0},{32,16},{16,32},{64,48},{48,64},{96,80},{80,96},{128,112},... | collective-permute-start | bytes 1572872 | tf_op jit(solution)/shard_map/ppermute | solution.py:432
  14.7 3.1 %collective-permute-start.5 = (f32[256,512]{1,0:T(8,128)S(1)}, f32[256,512]{1,0:T(8,128)S(1)}, u32[]{:S(2)}, u32[]{:S(2)}) collective-permute-start(f32[256,512]{1,0:T(8,128)S(1)} %get-tuple-element.24), channel_id=1, source_target_pairs={{16,0},{0,16},{48,32},{32,48},{80,64},{64,80},{112,96},{96,112},{1... | collective-permute-start | bytes 1572872 | tf_op jit(solution)/shard_map/ppermute | solution.py:432
  17.8 0.0 collective-permute-start.6
  17.8 0.0 collective-permute-done.pair_out
  17.8 2.8 %collective-permute-start.1 = (f32[128,512]{1,0:T(8,128)S(1)}, f32[128,512]{1,0:T(8,128)S(1)}, u32[]{:S(2)}, u32[]{:S(2)}) collective-permute-start(f32[128,512]{1,0:T(8,128)S(1)} %get-tuple-element.19), channel_id=1, source_target_pairs={{208,0},{64,16},{240,32},{96,48},{16,64},{128,80},{48,96},{160,112... | collective-permute-start | bytes 786440 | tf_op jit(solution)/shard_map/ppermute | solution.py:432
  20.6 1.3 %collective-permute-start.7 = (f32[128,512]{1,0:T(8,128)S(1)}, f32[128,512]{1,0:T(8,128)S(1)}, u32[]{:S(2)}, u32[]{:S(2)}) collective-permute-start(f32[128,512]{1,0:T(8,128)S(1)} %get-tuple-element.27), channel_id=1, source_target_pairs={{48,0},{224,16},{80,32},{0,48},{112,64},{32,80},{144,96},{64,112},... | collective-permute-start | bytes 786440 | tf_op jit(solution)/shard_map/ppermute | solution.py:432
  21.9 0.0 collective-permute-done.6.pair_in
  21.9 3.0 %shard_map.43 = f32[4,56,128]{2,1,0:T(8,128)S(1)} custom-call(f32[288,128]{1,0:T(8,128)S(1)} %collective-permute-done.2.back, f32[576,128]{1,0:T(8,128)S(1)} %collective-permute-done.pair_out, f32[576,128]{1,0:T(8,128)S(1)} %collective-permute-done.6.pair_in, f32[288,128]{1,0:T(8,128)S(1)} %collective-permute-done.4.ahead), custom_call_target="tpu_custom_call" | custom-call | flops 14155776 | bytes 999424 | tf_op jit(solution)/shard_map/pallas_call | solution.py:419
  24.9 8.8 %all_to_all.5.turns = f32[4,56,128]{2,1,0:T(8,128)S(1)} all-to-all(f32[4,56,128]{2,1,0:T(8,128)S(1)} %shard_map.43), channel_id=1, replica_groups={{0,4,8,12},{1,5,9,13},{2,6,10,14},{3,7,11,15},{16,20,24,28},{17,21,25,2..., dimensions={0} | all-to-all | bytes 229376 | tf_op jit(solution)/shard_map/all_to_all | solution.py:474
  33.6 0.0 collective-permute-done.1.back
  33.7 0.0 collective-permute-done.3.pair_out
  33.7 0.0 collective-permute-done.5.pair_in
  33.7 1.6 %shard_map.44 = (f32[1024]{0:T(1024)}, f32[128,512]{1,0:T(8,128)S(1)}, f32[128,512]{1,0:T(8,128)S(1)}) custom-call(f32[128,512]{1,0:T(8,128)S(1)} %collective-permute-done.1.back, f32[256,512]{1,0:T(8,128)S(1)} %collective-permute-done.3.pair_out, f32[256,512]{1,0:T(8,128)S(1)} %collective-permute-done.5.pair_in, f32[4,56,128]{2,1,0:T(8,128)S(1)} %all_to_all.5.turns), custom_call_target="tpu_custom_call" | custom-call | flops 6291456 | bytes 1953792 | tf_op jit(solution)/shard_map/pallas_call | solution.py:419
  35.2 0.0 collective-permute-done.7.ahead
  35.2 1.8 %shard_map.45 = f32[128,1024]{1,0:T(8,128)} custom-call(f32[256,512]{1,0:T(8,128)S(1)} %collective-permute-done.5.pair_in, f32[128,512]{1,0:T(8,128)S(1)} %collective-permute-done.7.ahead, f32[128,512]{1,0:T(8,128)S(1)} %get-tuple-element.28.near, f32[128,512]{1,0:T(8,128)S(1)} %get-tuple-element.29.done, f32[4,56,128]{2,1,0:T(8,128)S(1)} %all_to_all.5.turns), custom_call_target="tpu_custom_call" | custom-call | flops 6291456 | bytes 1949696 | tf_op jit(solution)/shard_map/pallas_call | solution.py:419
Async XLA Ops:
  0.6 1.2 %copy-start = (f32[256,1024]{1,0:T(8,128)S(1)}, f32[256,1024]{1,0:T(8,128)}, u32[]{:S(2)}) copy-start(f32[256,1024]{1,0:T(8,128)} %root_ref.1) | copy-start | bytes 3145732
  1.9 7.2 %copy-start.1 = (bf16[128,1024]{1,0:T(8,128)(2,1)S(1)}, bf16[128,1024]{1,0:T(8,128)(2,1)}, u32[]{:S(2)}) copy-start(bf16[128,1024]{1,0:T(8,128)(2,1)} %grad_ref.1) | copy-start | bytes 786436
  3.1 9.6 %collective-permute-start.4 = (f32[288,128]{1,0:T(8,128)S(1)}, f32[288,128]{1,0:T(8,128)S(1)}, u32[]{:S(2)}, u32[]{:S(2)}) collective-permute-start(f32[288,128]{1,0:T(8,128)S(1)} %get-tuple-element.23), channel_id=1, source_target_pairs={{48,0},{224,16},{80,32},{0,48},{112,64},{32,80},{144,96},{64,112},... | collective-permute-start | bytes 442376 | tf_op jit(solution)/shard_map/ppermute | solution.py:432
  8.7 4.7 %collective-permute-start.2 = (f32[288,128]{1,0:T(8,128)S(1)}, f32[288,128]{1,0:T(8,128)S(1)}, u32[]{:S(2)}, u32[]{:S(2)}) collective-permute-start(f32[288,128]{1,0:T(8,128)S(1)} %get-tuple-element.21), channel_id=1, source_target_pairs={{208,0},{64,16},{240,32},{96,48},{16,64},{128,80},{48,96},{160,112... | collective-permute-start | bytes 442376 | tf_op jit(solution)/shard_map/ppermute | solution.py:432
  8.7 9.2 %collective-permute-start = (f32[576,128]{1,0:T(8,128)S(1)}, f32[576,128]{1,0:T(8,128)S(1)}, u32[]{:S(2)}, u32[]{:S(2)}) collective-permute-start(f32[576,128]{1,0:T(8,128)S(1)} %get-tuple-element.18), channel_id=1, source_target_pairs={{240,0},{32,16},{16,32},{64,48},{48,64},{96,80},{80,96},{128,112},... | collective-permute-start | bytes 884744 | tf_op jit(solution)/shard_map/ppermute | solution.py:432
  13.4 20.2 %collective-permute-start.3 = (f32[256,512]{1,0:T(8,128)S(1)}, f32[256,512]{1,0:T(8,128)S(1)}, u32[]{:S(2)}, u32[]{:S(2)}) collective-permute-start(f32[256,512]{1,0:T(8,128)S(1)} %get-tuple-element.24), channel_id=1, source_target_pairs={{240,0},{32,16},{16,32},{64,48},{48,64},{96,80},{80,96},{128,112},... | collective-permute-start | bytes 1572872 | tf_op jit(solution)/shard_map/ppermute | solution.py:432
  14.7 18.9 %collective-permute-start.5 = (f32[256,512]{1,0:T(8,128)S(1)}, f32[256,512]{1,0:T(8,128)S(1)}, u32[]{:S(2)}, u32[]{:S(2)}) collective-permute-start(f32[256,512]{1,0:T(8,128)S(1)} %get-tuple-element.24), channel_id=1, source_target_pairs={{16,0},{0,16},{48,32},{32,48},{80,64},{64,80},{112,96},{96,112},{1... | collective-permute-start | bytes 1572872 | tf_op jit(solution)/shard_map/ppermute | solution.py:432
  17.8 4.0 %collective-permute-start.6 = (f32[576,128]{1,0:T(8,128)S(1)}, f32[576,128]{1,0:T(8,128)S(1)}, u32[]{:S(2)}, u32[]{:S(2)}) collective-permute-start(f32[576,128]{1,0:T(8,128)S(1)} %get-tuple-element.18), channel_id=1, source_target_pairs={{16,0},{0,16},{48,32},{32,48},{80,64},{64,80},{112,96},{96,112},{1... | collective-permute-start | bytes 884744 | tf_op jit(solution)/shard_map/ppermute | solution.py:432
  17.8 15.8 %collective-permute-start.1 = (f32[128,512]{1,0:T(8,128)S(1)}, f32[128,512]{1,0:T(8,128)S(1)}, u32[]{:S(2)}, u32[]{:S(2)}) collective-permute-start(f32[128,512]{1,0:T(8,128)S(1)} %get-tuple-element.19), channel_id=1, source_target_pairs={{208,0},{64,16},{240,32},{96,48},{16,64},{128,80},{48,96},{160,112... | collective-permute-start | bytes 786440 | tf_op jit(solution)/shard_map/ppermute | solution.py:432
  20.6 14.6 %collective-permute-start.7 = (f32[128,512]{1,0:T(8,128)S(1)}, f32[128,512]{1,0:T(8,128)S(1)}, u32[]{:S(2)}, u32[]{:S(2)}) collective-permute-start(f32[128,512]{1,0:T(8,128)S(1)} %get-tuple-element.27), channel_id=1, source_target_pairs={{48,0},{224,16},{80,32},{0,48},{112,64},{32,80},{144,96},{64,112},... | collective-permute-start | bytes 786440 | tf_op jit(solution)/shard_map/ppermute | solution.py:432
